TPU v7x, 32 devices: a whole 2x2x4 slice. The times are simulated.
32 devices in a mesh: items: 4 (over x, core), heads: 2 (over y), rows: 4 (over z).
Axes of the slice: x: 2, y: 2, z: 4, core: 2. Of those that a mesh axis runs over, the one named last changes fastest.
Arguments:
- inputs: bfloat16 [4, 1024, 1536], P('items', 'rows', 'heads'), may hold values from -6 to 6
- skip_input: bfloat16 [4, 2048, 1280], P('items', 'rows'), may hold values from -6 to 6
- cotangent: bfloat16 [4, 2048, 1536], P('items', 'rows', 'heads'), may hold values from -6 to 6
- track_mask: int32 [4, 1536], P('items', 'heads'), may hold values 0 or 1
- norm1_gain: float32 [1536], P(('items', 'rows')), may hold values from 0.1 to 1.9
- norm1_bias: float32 [1536], P(('items', 'rows')), may hold values from -1.8 to 1.8
- query_weight: float32 [1536, 512], P(('items', 'rows'), 'heads'), may hold values from -0.15625 to 0.15625
- key_weight: float32 [1536, 512], P(('items', 'rows'), 'heads'), may hold values from -0.15625 to 0.15625
- value_weight: float32 [1536, 1536], P(('items', 'rows'), 'heads'), may hold values from -0.15625 to 0.15625
- rel_weight: float32 [8, 2048], P('heads', ('items', 'rows')), may hold values from -1 to 1
- out_weight: float32 [1536, 1536], P('heads', ('items', 'rows')), may hold values from -0.625 to 0.625
- norm2_gain: float32 [1536], P(('items', 'rows')), may hold values from 0.1 to 1.9
- norm2_bias: float32 [1536], P(('items', 'rows')), may hold values from -1.8 to 1.8
- up_weight: float32 [1536, 3072], P(('items', 'rows'), 'heads'), may hold values from -0.15625 to 0.15625
- up_bias: float32 [2, 1536], P('heads', ('items', 'rows')), may hold values from -1.8 to 1.8
- down_weight: float32 [3072, 1536], P('heads', ('items', 'rows')), may hold values from -0.109375 to 0.109375
- down_bias: float32 [1536], P(('items', 'rows')), may hold values from -1.8 to 1.8
- skip_weight: float32 [1280, 1536], P(('items', 'rows'), 'heads'), may hold values from -0.15625 to 0.15625
- skip_bias: float32 [2, 768], P('heads', ('items', 'rows')), may hold values from -1.8 to 1.8
- depth_weight: float32 [3, 2, 768], P(None, 'heads', ('items', 'rows')), may hold values from -3 to 3
- point_weight: float32 [1536, 1536], P(('items', 'rows'), 'heads'), may hold values from -0.15625 to 0.15625
- point_bias: float32 [2, 768], P('heads', ('items', 'rows')), may hold values from -1.8 to 1.8
Outputs:
- block_output: bfloat16 [4, 2048, 1536], P('items', 'rows', 'heads')
- input_grad: float32 [4, 1024, 1536], P('items', 'rows', 'heads')
- grad_norm1_gain: float32 [1536], P(('items', 'rows'))
- grad_norm1_bias: float32 [1536], P(('items', 'rows'))
- grad_query_weight: float32 [1536, 512], P(('items', 'rows'), 'heads')
- grad_key_weight: float32 [1536, 512], P(('items', 'rows'), 'heads')
- grad_value_weight: float32 [1536, 1536], P(('items', 'rows'), 'heads')
- grad_rel_weight: float32 [8, 2048], P('heads', ('items', 'rows'))
- grad_out_weight: float32 [1536, 1536], P('heads', ('items', 'rows'))
- grad_norm2_gain: float32 [1536], P(('items', 'rows'))
- grad_norm2_bias: float32 [1536], P(('items', 'rows'))
- grad_up_weight: float32 [1536, 3072], P(('items', 'rows'), 'heads')
- grad_up_bias: float32 [2, 1536], P('heads', ('items', 'rows'))
- grad_down_weight: float32 [3072, 1536], P('heads', ('items', 'rows'))
- grad_down_bias: float32 [1536], P(('items', 'rows'))
- grad_skip_weight: float32 [1280, 1536], P(('items', 'rows'), 'heads')
- grad_skip_bias: float32 [2, 768], P('heads', ('items', 'rows'))
- grad_depth_weight: float32 [3, 2, 768], P(None, 'heads', ('items', 'rows'))
- grad_point_weight: float32 [1536, 1536], P(('items', 'rows'), 'heads')
- grad_point_bias: float32 [2, 768], P('heads', ('items', 'rows'))
Inputs may be any that keep to these rules, and one draw needn't show every extreme that they name: `track_mask`: 1 where the item's track in that channel is observed.
All inputs are finite; a program needn't handle non-finite values. No bound on the sum of `track_mask` on one device may be relied on, other than what follows from the above.
Results may differ from a plain program's by a relative error of at most 0.02.
Values may be sent and summed in bfloat16 or wider, within the bound.
No kernel may reach another device: no remote copies, remote signals or barrier semaphores. Data moves between devices by JAX's collectives and lax.ppermute only.
A program may use at most 256 MiB of HBM per device.

v0:
```python
import functools

import jax
import jax.numpy as jnp
import numpy as np
from jax import lax
from jax.experimental import pallas as pl
from jax.experimental.pallas import tpu as pltpu
from jax.sharding import PartitionSpec as P

KEY = 64
VAL = 192
NB = 32
EPS = 1e-05
IT, HD, RW = "items", "heads", "rows"
LOW = jnp.bfloat16
F32 = jnp.float32
VMEM = pltpu.CompilerParams(vmem_limit_bytes=56 * 2**20)
SHORT = pl.CostEstimate(flops=1, bytes_accessed=1, transcendentals=0)


def nn(a, b):
    return lax.dot_general(a, b, (((1,), (0,)), ((), ())), preferred_element_type=F32)


def nt(a, b):
    return lax.dot_general(a, b, (((1,), (1,)), ((), ())), preferred_element_type=F32)


def tn(a, b):
    return lax.dot_general(a, b, (((0,), (0,)), ((), ())), preferred_element_type=F32)


def wide(a):
    return a.astype(F32)


def low(a):
    return lax.reduce_precision(a, 8, 7).astype(LOW)


def bit_order(n):
    out, bit = [0], n // 2
    while bit:
        out += [i + bit for i in out]
        bit //= 2
    return out


def to_core(a):
    n = lax.axis_size(IT)
    return lax.ppermute(a, IT, [(i, i ^ 1) for i in range(n)])


def to_pair(a, k):
    n = lax.axis_size(IT)
    return lax.ppermute(a, IT, [(i, (i + 2 * k) % n) for i in range(n)])


def to_head(a):
    return lax.ppermute(a, HD, [(0, 1), (1, 0)])


def place():
    item = lax.axis_index(IT)
    return item // 2, item % 2, lax.axis_index(RW)


def to_bit(a, bit):
    n = lax.axis_size(RW)
    return lax.ppermute(a, RW, [(i, i ^ bit) for i in range(n)])


def halve(keep, got, pick_bit, pieces, after=()):
    w, n = keep.shape[0] // pieces, keep.shape[1]
    shape = (pieces // 2, 2, w, n)
    if w % 16:
        total = (keep + wide(jnp.concatenate(got, axis=1))).reshape(shape)
        mine = lax.dynamic_index_in_dim(total, pick_bit, 1, keepdims=False)
        send = lax.dynamic_index_in_dim(total, 1 - pick_bit, 1, keepdims=False)
        return mine.reshape(-1, n), low(send).reshape(-1, n)
    widths = [g.shape[1] for g in got]

    def body(bit_ref, keep_ref, *refs):
        got_refs, (mine_ref, send_ref) = refs[:-2], refs[-2:]

        def write(bit):
            at = 0
            for ref, count in zip(got_refs, widths):
                there = slice(at, at + count)
                at += count
                mine_ref[0, :, there] = keep_ref[0, bit, :, there] + ref[0, bit].astype(F32)
                total = keep_ref[0, 1 - bit, :, there] + ref[0, 1 - bit].astype(F32)
                send_ref[0, :, there] = total.astype(LOW)

        for bit in range(2):
            pl.when(bit_ref[0] == bit)(functools.partial(write, bit))

    def block(count):
        return (1, 2, w, count), lambda i: (i, 0, 0, 0)

    out = (1, w, n), lambda i: (i, 0, 0)
    half_shape = (pieces // 2, w, n)
    mine, send = run(
        body,
        pieces // 2,
        [(pick_bit.reshape(1), None, None), (keep.reshape(shape), *block(n))]
        + [(g.reshape(pieces // 2, 2, w, count), *block(count)) for g, count in zip(got, widths)],
        [(new(half_shape, F32), *out), (new(half_shape, LOW), *out)],
        after=after,
    )
    return mine.reshape(-1, n), send.reshape(-1, n)


def find(bounds, start, end):
    at = next(i for i, (a, b) in enumerate(bounds) if a <= start and end <= b)
    return at, slice(start - bounds[at][0], end - bounds[at][0])


def bounds_of(arrays):
    ends = [int(e) for e in np.cumsum([0] + [a.shape[1] for a in arrays])]
    return list(zip(ends, ends[1:]))


def spots_of(side, w):
    pairs = lax.axis_size(IT) // 2
    x, _, _ = place()
    return [(((x + k) % pairs) * 2 + side) for k in range(pairs)]


def fits(w):
    rows = lax.axis_size(RW)
    return lax.axis_size(IT) == 4 and w % 128 == 0 and (w // rows) % 16 == 0


def columns_product(spots_ref, left_ref, right, out_ref, there):
    count = spots_ref.shape[0]
    w = out_ref.shape[0] // count
    for k in range(count):
        start = pl.multiple_of(spots_ref[k] * w, 128)
        left = left_ref[pl.ds(0, right.shape[0]), pl.ds(start, w)]
        out_ref[k * w : (k + 1) * w, there] = tn(left, right).astype(LOW)


def side_product(pairs_of, side, got=None, after=(), groups=None, others=False):
    pairs = lax.axis_size(IT) // 2
    w = pairs_of[0][0].shape[1] // (2 * pairs)
    spots = spots_of(side, w)
    cols = [right.shape[1] for _, right in pairs_of]
    ends = [int(e) for e in np.cumsum([0] + cols)]
    groups = groups or [[k] for k in range(len(cols))]
    bounds = [(ends[g[0]], ends[g[-1] + 1]) for g in groups]
    if w % 128:
        out = []
        for left, right in pairs_of:
            part = [lax.dynamic_slice_in_dim(left, spot * w, w, 1) for spot in spots]
            out.append(tn(jnp.concatenate(part, axis=1)[: right.shape[0]], right))
        out = jnp.concatenate(out, axis=1)
        if got is None:
            return low(out)
        out = out + wide(jnp.concatenate(got, axis=1))
        return out[:w], [low(out[w:, i:j]) for i, j in bounds]
    n, count, m = sum(cols), len(pairs_of), len(after)
    first = int(others)
    got = got or []
    got_bounds = bounds_of(got)

    def body(spot_ref, *refs):
        lefts, rights = refs[:count], refs[count : 2 * count]
        gots = refs[2 * count : 2 * count + len(got)]
        outs = refs[2 * count + len(got) + m :]
        if others:
            outs = (None,) + tuple(outs)
        step = pl.program_id(0)
        for k in range(count):
            there = slice(ends[k], ends[k + 1])
            to = next(i for i, g in enumerate(groups) if k in g)
            inside = slice(ends[k] - bounds[to][0], ends[k + 1] - bounds[to][0])
            part = tn(lefts[k][...], rights[k][...])
            if not got:
                outs[0][:, there] = part.astype(LOW)
                continue
            which, where = find(got_bounds, ends[k], ends[k + 1])
            part = part + gots[which][:, where].astype(F32)

            if others:
                outs[1 + to][:, inside] = part.astype(LOW)
                continue

            @pl.when(step == 0)
            def _(part=part, there=there):
                outs[0][:, there] = part

            @pl.when(step > 0)
            def _(part=part, to=to, inside=inside):
                outs[1 + to][:, inside] = part.astype(LOW)

    specs = [
        pl.BlockSpec((right.shape[0], w), lambda i, spot: (0, spot[i])) for left, right in pairs_of
    ] + [pl.BlockSpec(right.shape, lambda i, spot: (0, 0)) for _, right in pairs_of]
    operands = [left for left, _ in pairs_of] + [right for _, right in pairs_of]
    specs += [pl.BlockSpec((w, g.shape[1]), lambda i, spot: (i + first, 0)) for g in got]
    operands += got
    if not got:
        out_specs = [pl.BlockSpec((w, n), lambda i, spot: (i, 0))]
        out_shape = [new((pairs * w, n), LOW)]
    else:
        out_specs, out_shape = [pl.BlockSpec((w, n), lambda i, spot: (0, 0))], [new((w, n), F32)]
        for c in [j - i for i, j in bounds]:
            out_specs.append(
                pl.BlockSpec((w, c), lambda i, spot: (jnp.maximum(i - 1 + first, 0), 0))
            )
            out_shape.append(new(((pairs - 1) * w, c), LOW))
        out_specs, out_shape = out_specs[first:], out_shape[first:]
    out = pl.pallas_call(
        body,
        grid_spec=pltpu.PrefetchScalarGridSpec(
            num_scalar_prefetch=1,
            grid=(pairs - first,),
            in_specs=specs + [pl.BlockSpec(memory_space=pl.ANY)] * m,
            out_specs=out_specs,
        ),
        out_shape=out_shape,
        compiler_params=VMEM,
        cost_estimate=SHORT,
    )(jnp.stack(spots[first:]).astype(jnp.int32), *operands, *after)
    if others:
        return list(out)
    return (out[0], list(out[1:])) if got else out[0]


def product_halve(pairs_of, spot, core, terms, pick_bit, pieces, after=()):
    w = pairs_of[0][0].shape[1] // (2 * (lax.axis_size(IT) // 2))
    cols = [right.shape[1] for _, right in pairs_of]
    ends = [int(e) for e in np.cumsum([0] + cols)]
    n, count, m = ends[-1], len(pairs_of), len(after)
    widths = [g.shape[1] for g in terms]
    piece = w // pieces
    core_bounds = bounds_of(core)

    def body(at_ref, *refs):
        lefts, rights = refs[:count], refs[count : 2 * count]
        at = 2 * count + len(core)
        core_refs, term_refs = refs[2 * count : at], refs[at : at + len(terms)]
        mine_ref, send_ref, total = refs[at + len(terms) + m :]
        for k in range(count):
            there = slice(ends[k], ends[k + 1])
            which, where = find(core_bounds, ends[k], ends[k + 1])
            part = core_refs[which][:, where].astype(F32)
            total[:, there] = tn(lefts[k][...], rights[k][...]) + part
        at = 0
        for ref, wide_n in zip(term_refs, widths):
            there = slice(at, at + wide_n)
            at += wide_n
            total[:, there] += ref[...].astype(F32)
        for i in range(pieces // 2):
            out = slice(i * piece, (i + 1) * piece)
            for bit in range(2):

                @pl.when(at_ref[1] == bit)
                def _(i=i, bit=bit, out=out):
                    mine = (2 * i + bit) * piece
                    send = (2 * i + 1 - bit) * piece
                    mine_ref[out] = total[mine : mine + piece]
                    send_ref[out] = total[send : send + piece].astype(LOW)

    in_specs = [
        pl.BlockSpec((right.shape[0], w), lambda i, at: (0, at[0])) for _, right in pairs_of
    ] + [pl.BlockSpec(right.shape, lambda i, at: (0, 0)) for _, right in pairs_of]
    in_specs += [pl.BlockSpec((w, g.shape[1]), lambda i, at: (0, 0)) for g in core]
    in_specs += [pl.BlockSpec(t.shape, lambda i, at: (0, 0)) for t in terms]
    out_spec = pl.BlockSpec((w // 2, n), lambda i, at: (0, 0))
    return pl.pallas_call(
        body,
        grid_spec=pltpu.PrefetchScalarGridSpec(
            num_scalar_prefetch=1,
            grid=(1,),
            in_specs=in_specs + [pl.BlockSpec(memory_space=pl.ANY)] * m,
            out_specs=[out_spec, out_spec],
            scratch_shapes=[pltpu.VMEM((w, n), F32)],
        ),
        out_shape=[new((w // 2, n), F32), new((w // 2, n), LOW)],
        compiler_params=VMEM,
        cost_estimate=SHORT,
    )(
        jnp.stack([spot, pick_bit]).astype(jnp.int32),
        *[left for left, _ in pairs_of],
        *[right for _, right in pairs_of],
        *core,
        *terms,
        *after,
    )


class Scatter:
    def __init__(self, pairs_of, theirs=None, after=(), after_more=(), groups=None):
        pairs = lax.axis_size(IT) // 2
        self.x, self.c, self.z = place()
        self.pairs_of, self.groups = pairs_of, groups
        self.plain = not fits(pairs_of[0][0].shape[1] // (2 * pairs))
        if theirs is None:
            theirs = [side_product(pairs_of, 1 - self.c, None, after)]
        self.theirs = theirs
        self.core = [to_core(t) for t in theirs]
        if self.plain:
            self.keep, self.send = side_product(pairs_of, self.c, self.core, after_more, groups)
        else:
            self.send = side_product(
                pairs_of, self.c, self.core, after_more, groups, others=True
            )
        self.bit = 1

    def across(self, i):
        pairs = lax.axis_size(IT) // 2
        w = self.send[i].shape[0] // (pairs - 1)
        return [to_pair(self.send[i][(k - 1) * w : k * w], k) for k in range(1, pairs)]

    def take(self, got):
        if self.plain:
            for terms in zip(*[g[:-1] for g in got]):
                self.keep = self.keep + wide(jnp.concatenate(terms, axis=1))
        self.got = [g[-1] for g in got]

    def step(self, after=()):
        pieces = lax.axis_size(RW) // self.bit
        pick_bit = (self.z // self.bit) % 2
        if self.bit == 1 and not self.plain:
            self.keep, self.sent = product_halve(
                self.pairs_of, self.x * 2 + self.c, self.core, self.got, pick_bit, pieces, after
            )
        else:
            self.keep, self.sent = halve(self.keep, self.got, pick_bit, pieces, after)
        self.got = [to_bit(self.sent, self.bit)]
        self.bit *= 2
        return self.got

    def finish(self, after=()):
        while self.bit < lax.axis_size(RW):
            self.step(after)
        return self.keep + wide(self.got[0])


def scatter_small(parts):
    pairs, rows = lax.axis_size(IT) // 2, lax.axis_size(RW)
    x, c, z = place()
    n = parts.shape[1]
    cube = parts.reshape(pairs, 2, rows, n)
    cube = lax.dynamic_index_in_dim(cube, c, 1, keepdims=False) + to_core(
        lax.dynamic_index_in_dim(cube, 1 - c, 1, keepdims=False)
    )
    plane = lax.dynamic_index_in_dim(cube, x, 0, keepdims=False)
    for k in range(1, pairs):
        plane = plane + to_pair(
            lax.dynamic_index_in_dim(cube, (x + k) % pairs, 0, keepdims=False), k
        )
    total = lax.dynamic_index_in_dim(plane, z, 0, keepdims=True)
    for k in range(1, rows):
        spot = jnp.bitwise_xor(z, k)
        total = total + to_bit(lax.dynamic_index_in_dim(plane, spot, 0, keepdims=True), k)
    return total


def attend_kernel(q_ref, kv_ref, wr_ref, basis_ref, out_ref, p_ref):
    rows, seq, heads = q_ref.shape[0], kv_ref.shape[0], p_ref.shape[0]
    width = heads * KEY
    basis = basis_ref[...]
    outs = []
    for h in range(heads):
        qh = q_ref[:, h * KEY : (h + 1) * KEY]
        kh = kv_ref[:, h * KEY : (h + 1) * KEY]
        vh = kv_ref[:, width + h * VAL : width + (h + 1) * VAL]
        features = nt(qh, wr_ref[h * NB : (h + 1) * NB, :].astype(LOW)).astype(LOW)
        table = nt(features, basis)
        rel = [
            pltpu.roll(
                table[:, k * 2 * rows : (k + 1) * 2 * rows], rows + 1, 1, stride=1, stride_axis=0
            )[:, :rows]
            for k in range(seq // rows)
        ]
        logits = nt(qh, kh) + jnp.concatenate(rel, axis=1)
        e = jnp.exp(logits - jnp.max(logits, axis=1, keepdims=True))
        p = (e * (1.0 / jnp.sum(e, axis=1, keepdims=True))).astype(LOW)
        p_ref[h] = p
        outs.append(nn(p, vh))
    out_ref[...] = jnp.concatenate(outs, axis=1).astype(LOW)


def attend_back_kernel(q_ref, kv_ref, wr_ref, basis_ref, p_ref, g_ref, dq_ref, dkv_ref, dwr_ref):
    rows, seq, heads = q_ref.shape[0], kv_ref.shape[0], p_ref.shape[0]
    width = heads * KEY
    basis = basis_ref[...]
    ii = lax.broadcasted_iota(jnp.int32, (rows, rows), 0)
    jj = lax.broadcasted_iota(jnp.int32, (rows, rows), 1)
    flip = (ii + jj == rows - 1).astype(F32).astype(LOW)
    dqs, dks, dvs = [], [], []
    for h in range(heads):
        qh = q_ref[:, h * KEY : (h + 1) * KEY]
        kh = kv_ref[:, h * KEY : (h + 1) * KEY]
        vh = kv_ref[:, width + h * VAL : width + (h + 1) * VAL]
        gh = g_ref[:, h * VAL : (h + 1) * VAL]
        wr = wr_ref[h * NB : (h + 1) * NB, :].astype(LOW)
        p = p_ref[h]
        probs = p.astype(F32)
        dp = nt(gh, vh)
        inner = jnp.sum(probs * dp, axis=1, keepdims=True)
        ds = (probs * (dp - inner)).astype(LOW)
        dvs.append(tn(p, gh))
        dks.append(tn(ds, qh))
        rev = nn(flip, ds)
        zeros = jnp.zeros((rows, rows), F32)
        tabs = [
            pltpu.roll(
                jnp.concatenate([rev[:, k * rows : (k + 1) * rows], zeros], axis=1),
                0,
                1,
                stride=1,
                stride_axis=0,
            ).astype(LOW)
            for k in range(seq // rows)
        ]
        features = nn(jnp.concatenate(tabs, axis=1), basis).astype(LOW)
        features = nn(flip, features).astype(LOW)
        dqs.append(nn(ds, kh) + nn(features, wr))
        dwr_ref[h * NB : (h + 1) * NB, :] = tn(features, qh)
    dq = jnp.concatenate(dqs, axis=1).astype(LOW).astype(F32) * (KEY**-0.5)
    dq_ref[...] = dq.astype(LOW)
    dkv_ref[...] = jnp.concatenate(dks + dvs, axis=1).astype(LOW)


def run(body, grid, ins, outs, scratch=(), after=()):
    n, m = len(ins), len(after)

    def kernel(*refs):
        body(*refs[:n], *refs[n + m :])

    def spec(shape, index):
        if index is None:
            return pl.BlockSpec(memory_space=pltpu.SMEM)
        return pl.BlockSpec(shape, index)

    def whole(a):
        return (a, a.shape, lambda i: (0,) * a.ndim)

    full = [entry if isinstance(entry, tuple) else whole(entry) for entry in ins]
    out_full = [entry if isinstance(entry, tuple) else whole(entry) for entry in outs]
    return pl.pallas_call(
        kernel,
        grid=(grid,),
        in_specs=[spec(shape, index) for _, shape, index in full]
        + [pl.BlockSpec(memory_space=pl.ANY)] * m,
        out_specs=tuple(spec(shape, index) for _, shape, index in out_full),
        out_shape=tuple(a for a, _, _ in out_full),
        scratch_shapes=scratch,
        compiler_params=VMEM,
        cost_estimate=SHORT,
    )(*[a for a, _, _ in full], *after)


def new(shape, dtype):
    return jax.ShapeDtypeStruct(shape, dtype)


def ordered(head_ref, own, other):
    first = head_ref[0] == 0
    return jnp.concatenate([jnp.where(first, own, other), jnp.where(first, other, own)], axis=1)


def my_half(head_ref, a):
    n = a.shape[1] // 2
    first = head_ref[0] == 0
    return jnp.where(first, a[:, :n], a[:, n:]), jnp.where(first, a[:, n:], a[:, :n])


def pack_kernel(count, *refs):
    out_ref, rows_ref = refs[-2:]
    rows, height = rows_ref.shape[0], out_ref.shape[0]
    at = 0
    for ref in refs[:count]:
        there = slice(at, at + ref.shape[1])
        at += ref.shape[1]
        out_ref[: ref.shape[0], there] = ref[...].astype(LOW)
        if ref.shape[0] < height:
            below = there
    rows_ref[...] = jnp.zeros_like(rows_ref)
    spot, width = 0, rows_ref.shape[1]
    for ref in refs[count:-2]:
        for i in range(ref.shape[0]):
            done, n = 0, ref.shape[1]
            while done < n:
                row, col = divmod(spot, width)
                part = min(n - done, width - col)
                rows_ref[row : row + 1, col : col + part] = ref[i : i + 1, done : done + part]
                done, spot = done + part, spot + part
    out_ref[height - rows :, below] = rows_ref[...].astype(LOW)


def unpack_kernel(shard, skip_rows, lengths, last_ref, skip_ref, rel_ref, *outs):
    group = last_ref.shape[0] // shard
    heads = rel_ref.shape[0] // NB
    width = last_ref.shape[1]
    for g in range(group):
        start = g * shard
        skip_ref[g * skip_rows : (g + 1) * skip_rows] = last_ref[start : start + skip_rows]
        rows = last_ref[start + skip_rows : start + shard].astype(F32)

        def piece(spot, n):
            parts, done = [], 0
            while done < n:
                row, col = divmod(spot + done, width)
                part = min(n - done, width - col)
                parts.append(rows[row : row + 1, col : col + part])
                done += part
            return parts[0] if len(parts) == 1 else jnp.concatenate(parts, axis=1)

        spot = 0
        for n, out in zip(lengths, outs):
            out[:, g * n : (g + 1) * n] = piece(spot, n)
            spot += n
        each = NB // group
        for h in range(heads):
            for j in range(each):
                row = h * NB + g * each + j
                rel_ref[row : row + 1] = piece(spot, KEY)
                spot += KEY


def project_kernel(rows, head_ref, *refs):
    own, other = refs[:rows], refs[rows : 2 * rows]
    gain_ref, bias_ref, qk_ref, v_ref, q_ref, kv_ref, normed_ref = refs[2 * rows :]
    width, kw = q_ref.shape
    for k in range(rows):
        x = ordered(head_ref, own[k][...].astype(F32), other[k][...].astype(F32))
        normed = (normalize(x)[0] * gain_ref[...] + bias_ref[...]).astype(LOW)
        at = slice(k * width, (k + 1) * width)
        normed_ref[at, :] = normed
        kv_ref[at, :kw] = nn(normed, qk_ref[:, kw:]).astype(LOW)
        kv_ref[at, kw:] = nn(normed, v_ref[...]).astype(LOW)
        if k == 0:
            q_ref[...] = (nn(normed, qk_ref[:, :kw]) * (KEY**-0.5)).astype(LOW)


def attend_out_kernel(q_ref, kv_ref, wr_ref, basis_ref, out_w_ref, out_ref, p_ref, part_ref):
    attend_kernel(q_ref, kv_ref, wr_ref, basis_ref, out_ref, p_ref)
    part_ref[...] = nt(out_ref[...], out_w_ref[...]).astype(LOW)


def ff_kernel(
    head_ref, own_ref, other_ref, p_ref, po_ref, gain_ref, bias_ref, b_up_ref, b_down_ref, up_ref, down_ref,
    hidden_ref, normed_ref, act_ref, slope_ref, mine_ref, send_ref, acc,
):
    step = pl.program_id(0)

    @pl.when(step == 0)
    def _():
        x = ordered(head_ref, own_ref[...].astype(F32), other_ref[...].astype(F32))
        hidden = x + (p_ref[...].astype(F32) + po_ref[...].astype(F32))
        hidden_ref[...] = hidden
        normed_ref[...] = (normalize(hidden)[0] * gain_ref[...] + bias_ref[...]).astype(LOW)
        acc[...] = hidden + b_down_ref[...]

    u = nn(normed_ref[...], up_ref[...]) + b_up_ref[...]
    t = jnp.tanh(G0 * (u + G1 * u * u * u))
    act = (0.5 * u * (1.0 + t)).astype(LOW)
    slope = 0.5 * (1.0 + t) + 0.5 * u * (1.0 - t * t) * (G0 * (1.0 + 3.0 * G1 * u * u))
    act_ref[...] = act
    slope_ref[...] = slope.astype(LOW)
    n = acc.shape[1] // 2
    part = nt(act, down_ref[...])
    mine, theirs = my_half(head_ref, part)

    @pl.when(step == 0)
    def _():
        mine_ref[...] = my_half(head_ref, acc[...])[0] + mine
        acc[:, :n] = theirs

    @pl.when(step > 0)
    def _():
        mine_ref[...] += mine
        acc[:, :n] += theirs

    @pl.when(step == pl.num_programs(0) - 1)
    def _():
        send_ref[...] = acc[:, :n].astype(LOW)


def ff_back_kernel(
    head_ref, own_ref, other_ref, slope_ref, up_ref, down_ref, *refs
):
    normed_ref, act_ref = refs[:2]
    grad_ref, pre_ref, part_ref, b_up_ref, b_down_ref = refs[2:7]
    step, acc = pl.program_id(0), refs[-1]

    @pl.when(step == 0)
    def _():
        grad = ordered(head_ref, own_ref[...], other_ref[...])
        grad_ref[...] = grad
        b_down_ref[...] = jnp.sum(grad.astype(F32), axis=0, keepdims=True)
        acc[...] = jnp.zeros_like(acc)

    pre = (slope_ref[...].astype(F32) * nn(grad_ref[...], down_ref[...])).astype(LOW)
    pre_ref[...] = pre
    b_up_ref[...] = jnp.sum(pre.astype(F32), axis=0, keepdims=True)
    acc[...] += nt(pre, up_ref[...])
    refs[7][...] = tn(grad_ref[...], act_ref[...]).astype(LOW)
    refs[8][...] = tn(normed_ref[...], pre).astype(LOW)

    @pl.when(step == pl.num_programs(0) - 1)
    def _():
        part_ref[...] = acc[...].astype(LOW)


def inner_back_kernel(
    fused, head_ref, p_ref, po_ref, hidden_ref, grad_ref, trans_ref, gain_ref, out_w_ref,
    q_ref, kv_ref, wr_ref, basis_ref, probs_ref, *refs
):
    spots_ref, normed_ref, out_ref = refs[:3] if fused else (None, None, None)
    outs = refs[3 * fused :]
    proj_ref, resid_ref, gain_sum_ref, bias_sum_ref, dq_ref, dkv_ref, dwr_ref = outs[:7]
    attended = outs[-1]
    grad_normed = p_ref[...].astype(F32) + po_ref[...].astype(F32)
    hat, scale = normalize(hidden_ref[...])
    gain_sum_ref[...] = jnp.sum(grad_normed * hat, axis=0, keepdims=True)
    bias_sum_ref[...] = jnp.sum(grad_normed, axis=0, keepdims=True)
    through = norm_back(grad_normed, hat, scale, gain_ref[...])
    resid_ref[...] = trans_ref[...] + my_half(head_ref, through)[0]
    proj = (grad_ref[...].astype(F32) + through).astype(LOW)
    proj_ref[...] = proj
    attended[...] = nn(proj, out_w_ref[...]).astype(LOW)
    attend_back_kernel(
        q_ref, kv_ref, wr_ref, basis_ref, probs_ref, attended, dq_ref, dkv_ref, dwr_ref
    )
    if fused:
        kw = dq_ref.shape[1]
        columns_product(spots_ref, proj_ref, out_ref[...], outs[7], slice(None))
        columns_product(spots_ref, normed_ref, dq_ref[...], outs[8], slice(0, kw))
        columns_product(spots_ref, normed_ref, dkv_ref[...], outs[8], slice(kw, None))


def point_back_kernel(head_ref, grad_ref, point_ref, mine_ref, send_ref, bias_ref):
    grad = grad_ref[...]
    bias_ref[...] = jnp.sum(grad[: grad.shape[0] - 16].astype(F32), axis=0, keepdims=True)
    mine, theirs = my_half(head_ref, nt(grad, point_ref[...]))
    mine_ref[...] = mine
    send_ref[...] = theirs.astype(LOW)


def before(a, edge):
    row = lax.broadcasted_iota(jnp.int32, a.shape, 0)
    return jnp.where(row == 0, edge, pltpu.roll(a, 1, 0))


def behind(a, edge):
    row = lax.broadcasted_iota(jnp.int32, a.shape, 0)
    return jnp.where(row == a.shape[0] - 1, edge, pltpu.roll(a, a.shape[0] - 1, 0))


def section_back_kernel(mine_ref, got_ref, tap0, tap1, tap2, gm_ref, low_ref, coarse_ref, bias_ref):
    n = coarse_ref.shape[0]
    gm = mine_ref[...] + got_ref[...].astype(F32)
    gm_ref[...] = gm[: 2 * n]
    even, odd = gm[:n], gm[n : 2 * n]
    prev, later = gm[2 * n : 2 * n + 1], gm[2 * n + 1 : 2 * n + 2]
    gs_even = tap0[...] * odd + tap1[...] * even + tap2[...] * before(odd, prev)
    gs_odd = tap0[...] * behind(even, later) + tap1[...] * odd + tap2[...] * even
    coarse_ref[...] = gs_even + gs_odd
    gs = jnp.concatenate([gs_even, gs_odd], axis=0).astype(LOW)
    low_ref[...] = gs
    bias_ref[...] = jnp.sum(gs.astype(F32), axis=0, keepdims=True)


def section_kernel(trans_ref, skip_ref, prev_ref, later_ref, gm_ref, tap0, tap1, tap2, mixed_ref, depth_ref):
    n = trans_ref.shape[0]
    coarse = gelu(trans_ref[...])
    s_even, s_odd = coarse + skip_ref[:n], coarse + skip_ref[n:]
    s_before, s_after = before(s_odd, prev_ref[...]), behind(s_even, later_ref[...])
    mixed_ref[:n] = (tap0[...] * s_before + tap1[...] * s_even + tap2[...] * s_odd).astype(LOW)
    mixed_ref[n:] = (tap0[...] * s_even + tap1[...] * s_odd + tap2[...] * s_after).astype(LOW)
    even, odd = gm_ref[:n], gm_ref[n:]
    for k, a, b in ((0, s_before, s_even), (1, s_even, s_odd), (2, s_odd, s_after)):
        depth_ref[k : k + 1] = jnp.sum(even * a + odd * b, axis=0, keepdims=True)


def project_back_kernel(rows, dq_ref, *refs):
    parts, (qk_ref, v_ref, out_ref) = refs[:rows], refs[rows:]
    kw = dq_ref.shape[1]
    dkv = parts[0][...].astype(F32)
    for k in range(1, rows):
        dkv = dkv + parts[k][...].astype(F32)
    dkv = dkv.astype(LOW)
    dqk = jnp.concatenate([dq_ref[...], dkv[:, :kw]], axis=1)
    out_ref[...] = (nt(dqk, qk_ref[...]) + nt(dkv[:, kw:], v_ref[...])).astype(LOW)


def outer_back_kernel(
    head_ref, own_ref, other_ref, p_ref, po_ref, gain_ref, resid_ref, grad_ref, gain_sum_ref, bias_sum_ref
):
    hat, scale = normalize(
        ordered(head_ref, own_ref[...].astype(F32), other_ref[...].astype(F32))
    )
    grad_normed = p_ref[...].astype(F32) + po_ref[...].astype(F32)
    gain_sum_ref[...] = jnp.sum(grad_normed * hat, axis=0, keepdims=True)
    bias_sum_ref[...] = jnp.sum(grad_normed, axis=0, keepdims=True)
    through = norm_back(grad_normed, hat, scale, gain_ref[...])
    grad_ref[...] = resid_ref[...] + my_half(head_ref, through)[0]


def position_windows(z, width, rows):
    seq = width * rows
    block = jnp.bitwise_xor(z, np.array(bit_order(rows), np.int32)) - z
    t = block[:, None] * width + (np.arange(2 * width) - (width - 1))[None, :]
    distance = t.reshape(-1).astype(F32)
    magnitude = jnp.abs(distance)[:, None]
    number = NB // 4
    steps_up = np.arange(number, dtype=np.float32)
    half_life = (3.0 * (seq / 3.0) ** (steps_up / max(number - 1, 1))).astype(np.float32)
    decays = jnp.exp(-0.6931471805599453 * magnitude / half_life)
    central = (2.0 ** (steps_up + 1.0) - 1.0 > magnitude).astype(F32)
    even = jnp.concatenate([decays, central], axis=1)
    return jnp.concatenate([even, jnp.sign(distance)[:, None] * even], axis=1).astype(LOW)


G0, G1 = 0.7978845608028654, 0.044715


def gelu(u):
    return 0.5 * u * (1.0 + jnp.tanh(G0 * (u + G1 * u * u * u)))


def gelu_slope(u):
    t = jnp.tanh(G0 * (u + G1 * u * u * u))
    return 0.5 * (1.0 + t) + 0.5 * u * (1.0 - t * t) * (G0 * (1.0 + 3.0 * G1 * u * u))


def normalize(values):
    centered = values - jnp.mean(values, axis=-1, keepdims=True)
    scale = lax.rsqrt(jnp.mean(centered * centered, axis=-1, keepdims=True) + EPS)
    return centered * scale, scale


def norm_back(grad, hat, scale, gain):
    gg = grad * gain
    return scale * (
        gg
        - jnp.mean(gg, axis=-1, keepdims=True)
        - hat * jnp.mean(gg * hat, axis=-1, keepdims=True)
    )


def pick(head, own, other):
    return jnp.where(head == 0, own, other), jnp.where(head == 0, other, own)


def both_halves(head, own, other):
    return jnp.concatenate(pick(head, own, other), axis=1)


def half(a, head):
    n = a.shape[1] // 2
    return lax.dynamic_slice_in_dim(a, head * n, n, 1)


def one_hot(select, height, width):
    ii = lax.broadcasted_iota(jnp.int32, (height, width), 0)
    jj = lax.broadcasted_iota(jnp.int32, (height, width), 1)
    return select(ii, jj).astype(LOW)


def from_before(row):
    n = lax.axis_size(RW)
    return lax.ppermute(row, RW, [(i, i + 1) for i in range(n - 1)])


def from_behind(row):
    n = lax.axis_size(RW)
    return lax.ppermute(row, RW, [(i + 1, i) for i in range(n - 1)])


def shards(
    inputs,
    skip_input,
    cotangent,
    track_mask,
    norm1_gain,
    norm1_bias,
    query_weight,
    key_weight,
    value_weight,
    rel_weight,
    out_weight,
    norm2_gain,
    norm2_bias,
    up_weight,
    up_bias,
    down_weight,
    down_bias,
    skip_weight,
    skip_bias,
    depth_weight,
    point_weight,
    point_bias,
):
    head = lax.axis_index(HD)
    _, _, z = place()
    rows = lax.axis_size(RW)
    group = lax.axis_size(IT) * rows
    width, chan = inputs.shape[1], inputs.shape[2]
    model = 2 * chan
    heads = rel_weight.shape[0]
    kw = heads * KEY
    shard = norm1_gain.shape[0]
    small = skip_bias.shape[1]
    rel_cols = rel_weight.shape[1]

    skip_rows = skip_weight.shape[0]
    flat = jnp.concatenate(
        [norm1_gain, norm1_bias, norm2_gain, norm2_bias, down_bias, up_bias[0]]
        + [skip_bias[0], depth_weight.reshape(-1), point_bias[0], rel_weight.reshape(-1)]
    ).astype(LOW)
    spare = shard - skip_rows
    singles = [norm1_gain, norm1_bias, norm2_gain, norm2_bias, down_bias, up_bias]
    singles += [skip_bias, depth_weight, point_bias, rel_weight]
    flat = jnp.pad(flat, (0, spare * chan - flat.size)).reshape(spare, chan)
    ff = up_weight.shape[1]
    order = [up_weight, down_weight.T, out_weight.T, point_weight]
    order += [jnp.concatenate([skip_weight.astype(LOW), flat], axis=0)]
    order += [value_weight, query_weight, key_weight]
    if shard % 16 == 0 and skip_rows % 16 == 0 and spare == 16:
        order[4] = skip_weight
        singles = [v.reshape(-1, v.shape[-1]) for v in singles]
        (piece,) = run(
            functools.partial(pack_kernel, len(order)),
            1,
            order + singles,
            [new((shard, sum(w.shape[1] for w in order)), LOW)],
            [pltpu.VMEM((spare, chan), F32)],
        )
    else:
        piece = jnp.concatenate([w.astype(LOW) for w in order], axis=1)
    big = lax.all_gather(piece, (IT, RW), axis=0, tiled=True)
    at = 2 * ff

    def columns(start, count):
        return (big, (model, count), lambda i: (0, start // count))

    w_out, w_value = columns(at, chan), columns(at + 3 * chan, heads * VAL)
    w_qk = columns(at + 3 * chan + heads * VAL, 2 * kw)
    w_point = columns(at + chan, chan)
    steps = 3
    cut = ff // steps
    w_up = (big, (model, cut), lambda i: (0, i))
    w_down = (big, (model, cut), lambda i: (0, steps + i))
    if shard % 16 == 0 and skip_rows % 16 == 0 and spare == 16 and NB % group == 0:
        lengths = [shard] * 6 + [small] * 5
        w_skip, w_rel, *singles = run(
            functools.partial(unpack_kernel, shard, skip_rows, lengths),
            1,
            [columns(at + 2 * chan, chan)],
            [new((group * skip_rows, chan), LOW), new((heads * NB, KEY), F32)]
            + [new((1, group * n), F32) for n in lengths],
        )
        gain_one, bias_one, gain_two, bias_two, b_down, b_up = singles[:6]
        b_skip, tap0, tap1, tap2, b_point = singles[6:]
    else:
        last = big[:, at + 2 * chan : at + 3 * chan].reshape(group, shard, chan)
        w_skip = last[:, :skip_rows].reshape(group * skip_rows, chan)
        tails = last[:, skip_rows:].reshape(group, -1)

        def vector(start, count):
            return wide(tails[:, start : start + count]).reshape(1, -1)

        gain_one, bias_one, gain_two, bias_two, b_down, b_up = (
            vector(i * shard, shard) for i in range(6)
        )
        at = 6 * shard
        b_skip, tap0, tap1, tap2, b_point = (vector(at + i * small, small) for i in range(5))
        at += 5 * small
        w_rel = tails[:, at : at + heads * rel_cols].reshape(group, heads, rel_cols)
        w_rel = w_rel.transpose(1, 0, 2).reshape(heads * NB, KEY)

    at_head = (head.reshape(1).astype(jnp.int32), None, None)
    even = one_hot(lambda i, j: j == 2 * i, width, 2 * width)
    odd = one_hot(lambda i, j: j == 2 * i + 1, width, 2 * width)
    apart = jnp.concatenate([even, odd], axis=0)
    masked = (wide(cotangent[0]) * wide(track_mask)).astype(LOW)
    edges = [from_before(masked[-1:]), from_behind(masked[:1]), jnp.zeros((14, chan), LOW)]
    grad_out = nn(apart, masked).astype(LOW)
    grad_rows = jnp.concatenate([grad_out] + edges, axis=0)
    skip_low = nn(apart, gelu(wide(skip_input[0])).astype(LOW)).astype(LOW)

    own_blocks = [to_bit(inputs[0], k) if k else inputs[0] for k in bit_order(rows)]
    other_blocks = [to_head(b) for b in own_blocks]
    basis = position_windows(z, width, rows)
    queries, kv, normed_all = run(
        functools.partial(project_kernel, rows),
        1,
        [at_head] + own_blocks + other_blocks + [gain_one, bias_one, w_qk, w_value],
        [new((width, kw), LOW), new((rows * width, kw + heads * VAL), LOW)]
        + [new((rows * width, model), LOW)],
        after=[skip_low, grad_rows, basis],
    )
    attended, probs, partial_attn = run(
        attend_out_kernel,
        1,
        [queries, kv, w_rel, basis, w_out],
        [new((width, heads * VAL), LOW), new((heads, width, rows * width), LOW)]
        + [new((width, model), LOW)],
    )
    skip_term = nn(skip_low, w_skip) + b_skip
    gm_mine, gm_send, grad_point_bias = run(
        point_back_kernel,
        1,
        [at_head, grad_rows, w_point],
        [new((2 * width + 16, chan), F32), new((2 * width + 16, chan), LOW), new((1, chan), F32)],
        after=[partial_attn],
    )
    grad_mixed, grad_skip_low, grad_coarse, grad_skip_bias = run(
        section_back_kernel,
        1,
        [gm_mine, to_head(gm_send), tap0, tap1, tap2],
        [new((2 * width, chan), F32), new((2 * width, chan), LOW)]
        + [new((width, chan), F32), new((1, chan), F32)],
    )

    by_cut = (width, cut), lambda i: (0, i)
    hidden, normed_two, activated, slope, trans, send = run(
        ff_kernel,
        steps,
        [at_head, own_blocks[0], other_blocks[0], partial_attn, to_head(partial_attn)]
        + [gain_two, bias_two, (b_up, (1, cut), lambda i: (0, i)), b_down, w_up, w_down],
        [new((width, model), F32), new((width, model), LOW), (new((width, ff), LOW), *by_cut)]
        + [(new((width, ff), LOW), *by_cut), new((width, chan), F32), new((width, chan), LOW)],
        [pltpu.VMEM((width, model), F32)],
        after=[skip_term],
    )
    trans = trans + wide(to_head(send))

    for_skip = Scatter([(skip_low, grad_skip_low)])

    s_first = gelu(trans[:1]) + skip_term[:1]
    s_last = gelu(trans[-1:]) + skip_term[-1:]
    prev, later = wide(from_before(low(s_last))), wide(from_behind(low(s_first)))

    grad_trans = gelu_slope(trans) * grad_coarse
    grad_own = low(grad_trans)
    owned = model // lax.axis_size(IT)
    fused = fits(owned)
    core_rows = model // 2
    spots = jnp.stack(spots_of(1 - place()[1], owned)).astype(jnp.int32), None, None
    extra = new((model, ff), LOW), (model, cut), lambda i: (0, i)
    grad_ff_low, grad_pre_low, partial_two, grad_up_bias, grad_down_bias, *theirs = run(
        ff_back_kernel,
        steps,
        [at_head, grad_own, to_head(grad_own), (slope, *by_cut), w_up, w_down]
        + [normed_two, (activated, *by_cut)],
        [new((width, model), LOW), (new((width, ff), LOW), *by_cut), new((width, model), LOW)]
        + [(new((1, ff), F32), (1, cut), lambda i: (0, i)), new((1, model), F32)]
        + [extra, extra],
        [pltpu.VMEM((width, model), F32)],
        after=[prev, later],
    )
    grad_down, grad_up = (
        lax.psum_scatter(t, (IT, RW), scatter_dimension=0, tiled=True) for t in theirs
    )
    mixed, grad_depth = run(
        section_kernel,
        1,
        [trans, skip_term, prev, later, grad_mixed, tap0, tap1, tap2],
        [new((2 * width, chan), LOW), new((3, chan), F32)],
    )
    grad_proj_low, resid, grad_gain_two, grad_bias_two, dq, dkv, grad_rel, *theirs = run(
        functools.partial(inner_back_kernel, fused),
        1,
        [at_head, partial_two, to_head(partial_two), hidden, grad_ff_low, grad_trans, gain_two]
        + [w_out, queries, kv, w_rel, basis, probs]
        + [spots, normed_all, attended][: 3 * fused],
        [new((width, model), LOW), new((width, chan), F32)]
        + [new((1, model), F32), new((1, model), F32)]
        + [new(queries.shape, LOW), new(kv.shape, LOW), new(w_rel.shape, F32)]
        + [new((core_rows, heads * VAL), LOW), new((core_rows, kw + kv.shape[1]), LOW)][: 2 * fused],
        [pltpu.VMEM((width, heads * VAL), LOW)],
        after=for_skip.send + [mixed],
    )
    dkv_parts, rest, bit, arrived = [dkv[:width]], dkv, 1, []
    summed = []
    while bit < rows:
        n = rest.shape[0] // 2
        got = to_bit(rest[n:], bit)
        dkv_parts.append(got[:width])
        arrived.append(got)
        if n > width:
            rest = low(wide(rest[:n]) + wide(got))
            dkv_parts = [rest[:width]]
            summed.append(rest)
        bit *= 2
    skip_across = [for_skip.across(0)]
    mixed_other = to_head(mixed)
    for_attn = Scatter(
        [(grad_proj_low, attended), (normed_all, dq), (normed_all, dkv)],
        theirs or None,
        [],
        [],
        [[0], [1, 2]],
    )
    attn_across = [for_attn.across(i) for i in range(2)]
    mixed_full = both_halves(head, mixed, mixed_other)
    for_point = Scatter([(mixed_full, grad_out)], None, for_attn.send)
    for_skip.take(skip_across)
    (partial_one,) = run(
        functools.partial(project_back_kernel, len(dkv_parts)),
        1,
        [dq] + dkv_parts + [w_qk, w_value],
        [new((width, model), LOW)],
        after=skip_across[0] + attn_across[0] + for_attn.send + for_point.theirs,
    )
    for_skip.step([partial_one])
    point_across = for_point.across(0)
    for_attn.take(attn_across)
    for_attn.step(for_point.send)
    input_grad, grad_gain_one, grad_bias_one = run(
        outer_back_kernel,
        1,
        [at_head, own_blocks[0], other_blocks[0], partial_one, to_head(partial_one)]
        + [gain_one, resid],
        [new((width, chan), F32), new((1, model), F32), new((1, model), F32)],
        after=point_across + for_skip.got + for_attn.got,
    )
    input_grad = input_grad[None]
    for_point.take([point_across])
    for_attn.step()
    for_point.step([for_attn.sent])
    for_skip.step([for_attn.sent])
    for_point.step([for_attn.sent])
    grad_skip = for_skip.finish()
    grad_attn, grad_point = for_attn.finish(), for_point.finish()
    grad_out_w, grad_qkv = grad_attn[:, : heads * VAL], grad_attn[:, heads * VAL :]
    result = (nn(mixed_full, w_point[0][:, 2 * ff + chan : 2 * ff + 2 * chan]) + b_point).astype(LOW)
    block_output = tn(apart, result).astype(LOW)[None]
    grad_depth = [grad_depth[k] for k in range(3)]

    rel_parts = grad_rel.reshape(heads, group, rel_cols).transpose(1, 0, 2)
    parts = [grad_gain_one, grad_bias_one, grad_gain_two, grad_bias_two, grad_down_bias]
    parts += [grad_up_bias, grad_skip_bias] + grad_depth + [grad_point_bias]
    parts = jnp.concatenate([p.reshape(group, -1) for p in parts] + [rel_parts.reshape(group, -1)], axis=1)
    sums = scatter_small(parts)

    def own(start, count):
        return sums[0, start : start + count]

    at = 6 * shard
    return (
        block_output,
        input_grad,
        own(0, shard),
        own(shard, shard),
        grad_qkv[:, :kw],
        grad_qkv[:, kw : 2 * kw],
        grad_qkv[:, 2 * kw :],
        own(at + 5 * small, heads * rel_cols).reshape(heads, rel_cols),
        grad_out_w.T,
        own(2 * shard, shard),
        own(3 * shard, shard),
        wide(grad_up),
        own(5 * shard, shard)[None],
        wide(grad_down).T,
        own(4 * shard, shard),
        grad_skip,
        own(at, small)[None],
        own(at + small, 3 * small).reshape(3, 1, small),
        grad_point,
        own(at + 4 * small, small)[None],
    )


def solution(mesh):
    gr = (IT, RW)
    vec, cols, rws = P(gr), P(gr, HD), P(HD, gr)
    act = P(IT, RW, HD)
    taps = P(None, HD, gr)
    weights = (vec, vec, cols, cols, cols, rws, rws, vec, vec, cols, rws, rws, vec, cols, rws)
    weights += (taps, cols, rws)
    return jax.shard_map(
        shards,
        mesh=mesh,
        in_specs=(act, P(IT, RW, None), act, P(IT, HD)) + weights,
        out_specs=(act, act) + weights,
        check_vma=False,
    )
```

profile of v0, /device:TPU:0, one launch (start us, length us, event | category | flops | bytes accessed | tf_op | source)
XLA Modules:
  0.0 496.7 jit_solution(12344737174783614295)
XLA Ops:
  8.5 2.9 shard_map.401
  11.6 5.1 %collective-permute-start.3 = (bf16[256,768]{1,0:T(8,128)(2,1)S(1)}, bf16[256,768]{1,0:T(8,128)(2,1)S(1)}, u32[]{:S(2)}, u32[]{:S(2)}) collective-permute-start(bf16[256,768]{1,0:T(8,128)(2,1)S(1)} %bitcast.87), channel_id=1, source_target_pairs={{0,3},{1,2},{2,1},{3,0},{4,7},{5,6},{6,5},{7,4},{8,11},{9,10},{10,... | collective-permute-start | bytes 1179656 | tf_op jit(solution)/shard_map/ppermute | solution.py:71
  19.2 3.1 collective-permute-start.7
  22.9 3.8 convolution_convert_fusion.refs_13_
  27.3 25.7 %collective-permute-done.7 = bf16[1,768]{1,0:T(2,128)(2,1)S(1)} collective-permute-done((bf16[1,768]{1,0:T(2,128)(2,1)S(1)}, bf16[1,768]{1,0:T(2,128)(2,1)S(1)}, u32[]{:S(2)}, u32[]{:S(2)}) %collective-permute-start.7) | collective-permute-done | bytes 1568 | tf_op jit(solution)/shard_map/ppermute | solution.py:770
  56.6 2.1 collective-permute-done.1.refs_2_
  62.6 83.8 %all-gather.2.cloned.1.call-done.refs_0_.refs_11_.refs_12_.refs_4_.refs_9_.refs_10_.refs_2_.refs_5_.refs_7_.refs_3_ = bf16[1536,6656]{1,0:T(8,128)(2,1)} async-done(((bf16[96,6656]{1,0:T(8,128)(2,1)}), bf16[1536,6656]{1,0:T(8,128)(2,1)}) %all-gather.2.cloned.1.call-update) | async-done | bytes 20447248 | tf_op jit(solution)/shard_map/all_gather | solution.py:839
  146.4 3.3 shard_map.402
  150.7 9.9 %shard_map.403 = (bf16[256,256]{1,0:T(8,128)(2,1)}, bf16[1024,1024]{1,0:T(8,128)(2,1)}, bf16[1024,1536]{1,0:T(8,128)(2,1)}) custom-call(s32[1]{0:T(128)} %bitcast.refs_0_, bf16[256,768]{1,0:T(8,128)(2,1)} %bitcast.84, bf16[256,768]{1,0:T(8,128)(2,1)} %collective-permute-done.1.refs_2_, bf16[256,768]{1,0:T(8,128)(2,1)} %copy-done.30, ...), custom_call_target="tpu_custom_call" | custom-call | flops 1 | bytes 1 | tf_op jit(solution)/shard_map/pallas_call | solution.py:446
  160.6 9.5 %shard_map.404 = (bf16[256,768]{1,0:T(8,128)(2,1)}, bf16[4,256,1024]{2,1,0:T(8,128)(2,1)}, bf16[256,1536]{1,0:T(8,128)(2,1)}) custom-call(bf16[256,256]{1,0:T(8,128)(2,1)} %get-tuple-element.88.refs_0_.refs_8_, bf16[1024,1024]{1,0:T(8,128)(2,1)} %get-tuple-element.89.refs_1_.refs_9_, f32[128,64]{1,0:T(8,128)} %get-tuple-element.90.refs_2_.refs_10_, ...), custom_call_target="tpu_custom_call" | custom-call | flops 1 | bytes 1 | tf_op jit(solution)/shard_map/pallas_call | solution.py:446
  171.6 4.8 shard_map.406
  176.9 4.4 convolution_add_fusion.refs_11_.refs_1_
  181.3 9.5 %collective-permute-done.9.refs_4_ = bf16[256,1536]{1,0:T(8,128)(2,1)S(1)} collective-permute-done((bf16[256,1536]{1,0:T(8,128)(2,1)}, bf16[256,1536]{1,0:T(8,128)(2,1)S(1)}, u32[]{:S(2)}, u32[]{:S(2)}) %collective-permute-start.9) | collective-permute-done | bytes 786464 | tf_op jit(solution)/shard_map/ppermute | solution.py:61
  191.7 10.9 %shard_map.405 = (f32[256,1536]{1,0:T(8,128)}, bf16[256,1536]{1,0:T(8,128)(2,1)}, bf16[256,1536]{1,0:T(8,128)(2,1)}, bf16[256,1536]{1,0:T(8,128)(2,1)}, f32[256,768]{1,0:T(8,128)}, /*index=5*/bf16[256,768]{1,0:T(8,128)(2,1)}) custom-call(s32[1]{0:T(128)} %bitcast.refs_0_, bf16[256,768]{1,0:T(8,128)(2,1)} %bitcast.85, bf16[256,768]{1,0:T(8,128)(2,1)} %copy-done.8, ...), custom_call_target="tpu_custom_call" | custom-call | flops 1 | bytes 1 | tf_op jit(solution)/shard_map/pallas_call | solution.py:446
  204.2 2.0 collective-permute-done.13.refs_1_
  207.1 3.7 shard_map.407
  211.7 2.6 reduce-precision_convert_fusion.2
  217.9 10.5 %collective-permute-start.11 = (bf16[1,768]{1,0:T(2,128)(2,1)S(1)}, bf16[1,768]{1,0:T(2,128)(2,1)S(1)}, u32[]{:S(2)}, u32[]{:S(2)}) collective-permute-start(bf16[1,768]{1,0:T(2,128)(2,1)S(1)} %get-tuple-element.159), channel_id=1, source_target_pairs={{0,1},{1,2},{2,3},{4,5},{5,6},{6,7},{8,9},{9,10},{10,11},{12,13},{... | collective-permute-start | bytes 4616 | tf_op jit(solution)/shard_map/ppermute | solution.py:770
  231.1 13.7 %shard_map.409 = (bf16[256,1536]{1,0:T(8,128)(2,1)}, bf16[256,1536]{1,0:T(8,128)(2,1)}, bf16[256,1536]{1,0:T(8,128)(2,1)}, f32[1,1536]{1,0:T(1,128)}, f32[1,1536...) custom-call(s32[1]{0:T(128)} %bitcast.refs_0_, bf16[256,768]{1,0:T(8,128)(2,1)} %copy-done.19, ...), custom_call_target="tpu_custom_call" | custom-call | flops 1 | bytes 1 | tf_op jit(solution)/shard_map/pallas_call | solution.py:446
  248.2 4.1 shard_map.408
  254.5 12.5 %collective-permute-done.16.refs_2_ = bf16[256,1536]{1,0:T(8,128)(2,1)S(1)} collective-permute-done((bf16[256,1536]{1,0:T(8,128)(2,1)S(1)}, bf16[256,1536]{1,0:T(8,128)(2,1)S(1)}, u32[]{:S(2)}, u32[]{:S(2)}) %collective-permute-start.16) | collective-permute-done | bytes 786464 | tf_op jit(solution)/shard_map/ppermute | solution.py:61
  267.8 17.5 %shard_map.410 = (bf16[256,1536]{1,0:T(8,128)(2,1)}, f32[256,768]{1,0:T(8,128)}, f32[1,1536]{1,0:T(1,128)}, f32[1,1536]{1,0:T(1,128)}, bf16[256,256]{1,0:T(8,128...) custom-call(s32[1]{0:T(128)} %bitcast.refs_0_, ...), custom_call_target="tpu_custom_call" | custom-call | flops 1 | bytes 1 | tf_op jit(solution)/shard_map/pallas_call | solution.py:446
  286.1 2.3 slice.103
  288.4 2.2 collective-permute-start.18
  290.7 14.9 %collective-permute-done.14 = bf16[512,768]{1,0:T(8,128)(2,1)} collective-permute-done((bf16[512,768]{1,0:T(8,128)(2,1)}, bf16[512,768]{1,0:T(8,128)(2,1)}, u32[]{:S(2)}, u32[]{:S(2)}) %collective-permute-start.14) | collective-permute-done | bytes 786464 | tf_op jit(solution)/shard_map/ppermute | solution.py:61
  310.2 4.7 shard_map.411
  315.0 4.1 shard_map.412.refs_9_
  319.2 11.1 %collective-permute-done.18 = bf16[512,1024]{1,0:T(8,128)(2,1)} collective-permute-done((bf16[512,1024]{1,0:T(8,128)(2,1)}, bf16[512,1024]{1,0:T(8,128)(2,1)}, u32[]{:S(2)}, u32[]{:S(2)}) %collective-permute-start.18) | collective-permute-done | bytes 1048608 | tf_op jit(solution)/shard_map/ppermute | solution.py:71
  333.0 2.2 collective-permute-start.19
  337.4 29.1 %collective-permute-done.20.refs_5_ = bf16[320,768]{1,0:T(8,128)(2,1)} collective-permute-done((bf16[320,768]{1,0:T(8,128)(2,1)}, bf16[320,768]{1,0:T(8,128)(2,1)}, u32[]{:S(2)}, u32[]{:S(2)}) %collective-permute-start.20) | collective-permute-done | bytes 491552 | tf_op jit(solution)/shard_map/ppermute | solution.py:57
  367.3 5.2 %shard_map.413.refs_3_ = bf16[256,1536]{1,0:T(8,128)(2,1)} custom-call(bf16[256,256]{1,0:T(8,128)(2,1)} %get-tuple-element.119.refs_4_.refs_0_, bf16[256,1024]{1,0:T(8,128)(2,1)} %get-tuple-element.169.refs_1_, bf16[256,1024]{1,0:T(8,128)(2,1)} %collective-permute-done.19.refs_2_, ...), custom_call_target="tpu_custom_call" | custom-call | flops 1 | bytes 1 | tf_op jit(solution)/shard_map/pallas_call | solution.py:446
  374.2 2.8 shard_map.414.refs_10_
  376.9 6.9 %shard_map.416 = (f32[192,2048]{1,0:T(8,128)}, bf16[192,2048]{1,0:T(8,128)(2,1)}) custom-call(s32[2]{0:T(128)} %pad_add_fusion.2.at_ref, bf16[256,1536]{1,0:T(8,128)(2,1)} %get-tuple-element.121.refs_0_, bf16[1024,1536]{1,0:T(8,128)(2,1)} %get-tuple-element.116.refs_14_.refs_1_.refs_2_, bf16[1024,1536]{1,0:T(8,128)(2,1)} %get-tuple-element.116.refs_14_.refs_1_.refs_2_, ...), custom_call_target="tpu_custom_call" | custom-call | flops 1 | bytes 1 | tf_op jit(solution)/shard_map/pallas_call | solution.py:273
  383.9 2.5 collective-permute-start.29
  387.1 2.1 shard_map.415
  390.4 34.8 %collective-permute-done.27.refs_8_ = bf16[160,768]{1,0:T(8,128)(2,1)S(1)} collective-permute-done((bf16[160,768]{1,0:T(8,128)(2,1)}, bf16[160,768]{1,0:T(8,128)(2,1)S(1)}, u32[]{:S(2)}, u32[]{:S(2)}) %collective-permute-start.27) | collective-permute-done | bytes 245792 | tf_op jit(solution)/shard_map/ppermute | solution.py:71
  426.8 4.1 shard_map.417
  434.2 3.7 collective-permute-done.31
  438.0 2.5 collective-permute-start.34
  441.5 4.9 fusion.16
  446.4 2.8 shard_map.418
  449.2 1.9 collective-permute-start.35
  451.2 1.9 shard_map.419
  454.0 3.8 shard_map.420
  461.4 11.9 %collective-permute-done.36 = bf16[80,768]{1,0:T(8,128)(2,1)S(1)} collective-permute-done((bf16[80,768]{1,0:T(8,128)(2,1)}, bf16[80,768]{1,0:T(8,128)(2,1)S(1)}, u32[]{:S(2)}, u32[]{:S(2)}) %collective-permute-start.36) | collective-permute-done | bytes 122912 | tf_op jit(solution)/shard_map/ppermute | solution.py:71
  475.5 2.0 shard_map.421
  479.6 6.0 %collective-permute-done.38 = bf16[96,768]{1,0:T(8,128)(2,1)S(1)} collective-permute-done((bf16[96,768]{1,0:T(8,128)(2,1)}, bf16[96,768]{1,0:T(8,128)(2,1)S(1)}, u32[]{:S(2)}, u32[]{:S(2)}) %collective-permute-start.38) | collective-permute-done | bytes 147488 | tf_op jit(solution)/shard_map/ppermute | solution.py:71
  486.3 1.8 convert_bitcast_fusion
  (251 shorter events, 64.1 us)
Async XLA Ops:
  7.2 139.2 %all-gather.2.cloned.1.call-start = ((), (), s32[]{:S(2)}) async-start(), calls=%async_computation.2 | async-start | bytes 21725184 | tf_op jit(solution)/shard_map/all_gather | solution.py:839
  11.5 474.8 %reduce-scatter.5.cloned.1.call-start = ((), (), s32[]{:S(2)}) async-start(), calls=%async_computation.4 | async-start | bytes 5013504 | tf_op jit(solution)/shard_map/reduce_scatter | solution.py:962
  11.6 43.0 %collective-permute-start.3 = (bf16[256,768]{1,0:T(8,128)(2,1)S(1)}, bf16[256,768]{1,0:T(8,128)(2,1)S(1)}, u32[]{:S(2)}, u32[]{:S(2)}) collective-permute-start(bf16[256,768]{1,0:T(8,128)(2,1)S(1)} %bitcast.87), channel_id=1, source_target_pairs={{0,3},{1,2},{2,1},{3,0},{4,7},{5,6},{6,5},{7,4},{8,11},{9,10},{10,... | collective-permute-start | bytes 1179656 | tf_op jit(solution)/shard_map/ppermute | solution.py:71
  16.7 39.3 %collective-permute-start.2 = (bf16[256,768]{1,0:T(8,128)(2,1)S(1)}, bf16[256,768]{1,0:T(8,128)(2,1)S(1)}, u32[]{:S(2)}, u32[]{:S(2)}) collective-permute-start(bf16[256,768]{1,0:T(8,128)(2,1)S(1)} %bitcast.88), channel_id=1, source_target_pairs={{0,1},{1,0},{2,3},{3,2},{4,5},{5,4},{6,7},{7,6},{8,9},{9,8},{10,11... | collective-permute-start | bytes 1179656 | tf_op jit(solution)/shard_map/ppermute | solution.py:71
  16.7 42.1 %collective-permute-start.1 = (bf16[256,768]{1,0:T(8,128)(2,1)S(1)}, bf16[256,768]{1,0:T(8,128)(2,1)}, u32[]{:S(2)}, u32[]{:S(2)}) collective-permute-start(bf16[256,768]{1,0:T(8,128)(2,1)S(1)} %bitcast.89), channel_id=1, source_target_pairs={{0,2},{1,3},{2,0},{3,1},{4,6},{5,7},{6,4},{7,5},{8,10},{9,11},{10,... | collective-permute-start | bytes 1179656 | tf_op jit(solution)/shard_map/ppermute | solution.py:71
  17.3 132.4 %collective-permute-start = (bf16[256,768]{1,0:T(8,128)(2,1)S(1)}, bf16[256,768]{1,0:T(8,128)(2,1)S(1)}, u32[]{:S(2)}, u32[]{:S(2)}) collective-permute-start(bf16[256,768]{1,0:T(8,128)(2,1)S(1)} %bitcast.90), channel_id=1, source_target_pairs={{0,4},{4,0},{1,5},{5,1},{2,6},{6,2},{3,7},{7,3},{8,12},{12,8},{9,1... | collective-permute-start | bytes 1179656 | tf_op jit(solution)/shard_map/ppermute | solution.py:61
  19.2 33.8 %collective-permute-start.7 = (bf16[1,768]{1,0:T(2,128)(2,1)S(1)}, bf16[1,768]{1,0:T(2,128)(2,1)S(1)}, u32[]{:S(2)}, u32[]{:S(2)}) collective-permute-start(bf16[1,768]{1,0:T(2,128)(2,1)S(1)} %get-tuple-element.174), channel_id=1, source_target_pairs={{0,1},{1,2},{2,3},{4,5},{5,6},{6,7},{8,9},{9,10},{10,11},{12,13},{... | collective-permute-start | bytes 4616 | tf_op jit(solution)/shard_map/ppermute | solution.py:770
  27.3 122.4 %copy-start.1 = (bf16[512,768]{1,0:T(8,128)(2,1)}, bf16[512,768]{1,0:T(8,128)(2,1)S(1)}, u32[]{:S(2)}) copy-start(bf16[512,768]{1,0:T(8,128)(2,1)S(1)} %convolution_convert_fusion.2.refs_1_) | copy-start | bytes 2359300
  53.0 8.4 %collective-permute-start.8 = (bf16[1,768]{1,0:T(2,128)(2,1)S(1)}, bf16[1,768]{1,0:T(2,128)(2,1)S(1)}, u32[]{:S(2)}, u32[]{:S(2)}) collective-permute-start(bf16[1,768]{1,0:T(2,128)(2,1)S(1)} %get-tuple-element.175), channel_id=1, source_target_pairs={{1,0},{2,1},{3,2},{5,4},{6,5},{7,6},{9,8},{10,9},{11,10},{13,12},{... | collective-permute-start | bytes 4616 | tf_op jit(solution)/shard_map/ppermute | solution.py:775
  54.5 95.2 %copy-start.29 = (bf16[256,768]{1,0:T(8,128)(2,1)}, bf16[256,768]{1,0:T(8,128)(2,1)S(1)}, u32[]{:S(2)}) copy-start(bf16[256,768]{1,0:T(8,128)(2,1)S(1)} %collective-permute-done.3.refs_4_) | copy-start | bytes 1179652
  54.5 95.2 %collective-permute-start.6 = (bf16[256,768]{1,0:T(8,128)(2,1)S(1)}, bf16[256,768]{1,0:T(8,128)(2,1)S(1)}, u32[]{:S(2)}, u32[]{:S(2)}) collective-permute-start(bf16[256,768]{1,0:T(8,128)(2,1)S(1)} %collective-permute-done.3.refs_4_), channel_id=1, source_target_pairs={{0,4},{4,0},{1,5},{5,1},{2,6},{6,2},{3,7},{7,3},{8,12},{12,8},{9,1... | collective-permute-start | bytes 1179656 | tf_op jit(solution)/shard_map/ppermute | solution.py:61
  56.0 93.7 %copy-start.30 = (bf16[256,768]{1,0:T(8,128)(2,1)}, bf16[256,768]{1,0:T(8,128)(2,1)S(1)}, u32[]{:S(2)}) copy-start(bf16[256,768]{1,0:T(8,128)(2,1)S(1)} %collective-permute-done.2.refs_3_) | copy-start | bytes 1179652
  56.0 93.8 %collective-permute-start.5 = (bf16[256,768]{1,0:T(8,128)(2,1)S(1)}, bf16[256,768]{1,0:T(8,128)(2,1)S(1)}, u32[]{:S(2)}, u32[]{:S(2)}) collective-permute-start(bf16[256,768]{1,0:T(8,128)(2,1)S(1)} %collective-permute-done.2.refs_3_), channel_id=1, source_target_pairs={{0,4},{4,0},{1,5},{5,1},{2,6},{6,2},{3,7},{7,3},{8,12},{12,8},{9,1... | collective-permute-start | bytes 1179656 | tf_op jit(solution)/shard_map/ppermute | solution.py:61
  58.7 91.0 %collective-permute-start.4 = (bf16[256,768]{1,0:T(8,128)(2,1)}, bf16[256,768]{1,0:T(8,128)(2,1)}, u32[]{:S(2)}, u32[]{:S(2)}) collective-permute-start(bf16[256,768]{1,0:T(8,128)(2,1)} %collective-permute-done.1.refs_2_), channel_id=1, source_target_pairs={{0,4},{4,0},{1,5},{5,1},{2,6},{6,2},{3,7},{7,3},{8,12},{12,8},{9,1... | collective-permute-start | bytes 1179656 | tf_op jit(solution)/shard_map/ppermute | solution.py:61
  170.1 20.7 %collective-permute-start.9 = (bf16[256,1536]{1,0:T(8,128)(2,1)}, bf16[256,1536]{1,0:T(8,128)(2,1)S(1)}, u32[]{:S(2)}, u32[]{:S(2)}) collective-permute-start(bf16[256,1536]{1,0:T(8,128)(2,1)} %get-tuple-element.91.refs_3_), channel_id=1, source_target_pairs={{0,4},{4,0},{1,5},{5,1},{2,6},{6,2},{3,7},{7,3},{8,12},{12,8},{9,1... | collective-permute-start | bytes 2359304 | tf_op jit(solution)/shard_map/ppermute | solution.py:61
  176.4 29.8 %collective-permute-start.13 = (bf16[528,768]{1,0:T(8,128)(2,1)}, bf16[528,768]{1,0:T(8,128)(2,1)S(1)}, u32[]{:S(2)}, u32[]{:S(2)}) collective-permute-start(bf16[528,768]{1,0:T(8,128)(2,1)} %get-tuple-element.101), channel_id=1, source_target_pairs={{0,4},{4,0},{1,5},{5,1},{2,6},{6,2},{3,7},{7,3},{8,12},{12,8},{9,1... | collective-permute-start | bytes 2433032 | tf_op jit(solution)/shard_map/ppermute | solution.py:61
  202.6 9.1 %collective-permute-start.10 = (bf16[256,768]{1,0:T(8,128)(2,1)}, bf16[256,768]{1,0:T(8,128)(2,1)S(1)}, u32[]{:S(2)}, u32[]{:S(2)}) collective-permute-start(bf16[256,768]{1,0:T(8,128)(2,1)} %get-tuple-element.99), channel_id=1, source_target_pairs={{0,4},{4,0},{1,5},{5,1},{2,6},{6,2},{3,7},{7,3},{8,12},{12,8},{9,1... | collective-permute-start | bytes 1179656 | tf_op jit(solution)/shard_map/ppermute | solution.py:61
  214.3 30.5 %copy-start.9 = (f32[256,768]{1,0:T(8,128)}, f32[256,768]{1,0:T(8,128)S(1)}, u32[]{:S(2)}) copy-start(f32[256,768]{1,0:T(8,128)S(1)} %get-tuple-element.157.refs_0_) | copy-start | bytes 2359300
  214.3 16.0 %collective-permute-start.15 = (bf16[256,768]{1,0:T(8,128)(2,1)S(1)}, bf16[256,768]{1,0:T(8,128)(2,1)S(1)}, u32[]{:S(2)}, u32[]{:S(2)}) collective-permute-start(bf16[256,768]{1,0:T(8,128)(2,1)S(1)} %get-tuple-element.155.refs_1_), channel_id=1, source_target_pairs={{0,4},{4,0},{1,5},{5,1},{2,6},{6,2},{3,7},{7,3},{8,12},{12,8},{9,1... | collective-permute-start | bytes 1179656 | tf_op jit(solution)/shard_map/ppermute | solution.py:61
  216.6 11.9 %collective-permute-start.12 = (bf16[1,768]{1,0:T(2,128)(2,1)S(1)}, bf16[1,768]{1,0:T(2,128)(2,1)S(1)}, u32[]{:S(2)}, u32[]{:S(2)}) collective-permute-start(bf16[1,768]{1,0:T(2,128)(2,1)S(1)} %get-tuple-element.158), channel_id=1, source_target_pairs={{1,0},{2,1},{3,2},{5,4},{6,5},{7,6},{9,8},{10,9},{11,10},{13,12},{... | collective-permute-start | bytes 4616 | tf_op jit(solution)/shard_map/ppermute | solution.py:775
  217.9 11.9 %collective-permute-start.11 = (bf16[1,768]{1,0:T(2,128)(2,1)S(1)}, bf16[1,768]{1,0:T(2,128)(2,1)S(1)}, u32[]{:S(2)}, u32[]{:S(2)}) collective-permute-start(bf16[1,768]{1,0:T(2,128)(2,1)S(1)} %get-tuple-element.159), channel_id=1, source_target_pairs={{0,1},{1,2},{2,3},{4,5},{5,6},{6,7},{8,9},{9,10},{10,11},{12,13},{... | collective-permute-start | bytes 4616 | tf_op jit(solution)/shard_map/ppermute | solution.py:770
  244.8 243.4 %reduce-scatter.3.cloned.1.call-start = ((), (), s32[]{:S(2)}) async-start(), calls=%async_computation.3 | async-start | bytes 5013504 | tf_op jit(solution)/shard_map/reduce_scatter | solution.py:962
  246.9 5.4 %collective-permute-start.17 = (bf16[640,768]{1,0:T(8,128)(2,1)S(1)}, bf16[640,768]{1,0:T(8,128)(2,1)S(1)}, u32[]{:S(2)}, u32[]{:S(2)}) collective-permute-start(bf16[640,768]{1,0:T(8,128)(2,1)S(1)} %reduce-precision_convert_fusion.1), channel_id=1, source_target_pairs={{0,8},{8,0},{16,24},{24,16},{1,9},{9,1},{17,25},{25,17},{2,10},{10... | collective-permute-start | bytes 2949128 | tf_op jit(solution)/shard_map/ppermute | solution.py:52
  247.1 19.8 %collective-permute-start.16 = (bf16[256,1536]{1,0:T(8,128)(2,1)S(1)}, bf16[256,1536]{1,0:T(8,128)(2,1)S(1)}, u32[]{:S(2)}, u32[]{:S(2)}) collective-permute-start(bf16[256,1536]{1,0:T(8,128)(2,1)S(1)} %copy-done.26), channel_id=1, source_target_pairs={{0,4},{4,0},{1,5},{5,1},{2,6},{6,2},{3,7},{7,3},{8,12},{12,8},{9,1... | collective-permute-start | bytes 2359304 | tf_op jit(solution)/shard_map/ppermute | solution.py:61
  285.3 23.2 %collective-permute-start.22 = (bf16[768,1280]{1,0:T(8,128)(2,1)}, bf16[768,1280]{1,0:T(8,128)(2,1)S(1)}, u32[]{:S(2)}, u32[]{:S(2)}) collective-permute-start(bf16[768,1280]{1,0:T(8,128)(2,1)} %get-tuple-element.123), channel_id=1, source_target_pairs={{0,8},{8,0},{16,24},{24,16},{1,9},{9,1},{17,25},{25,17},{2,10},{10... | collective-permute-start | bytes 5898248 | tf_op jit(solution)/shard_map/ppermute | solution.py:52
  285.4 20.3 %collective-permute-start.14 = (bf16[512,768]{1,0:T(8,128)(2,1)}, bf16[512,768]{1,0:T(8,128)(2,1)}, u32[]{:S(2)}, u32[]{:S(2)}) collective-permute-start(bf16[512,768]{1,0:T(8,128)(2,1)} %get-tuple-element.106.refs_17_), channel_id=1, source_target_pairs={{0,4},{4,0},{1,5},{5,1},{2,6},{6,2},{3,7},{7,3},{8,12},{12,8},{9,1... | collective-permute-start | bytes 2359304 | tf_op jit(solution)/shard_map/ppermute | solution.py:61
  286.0 22.6 %collective-permute-start.21 = (bf16[768,768]{1,0:T(8,128)(2,1)}, bf16[768,768]{1,0:T(8,128)(2,1)S(1)}, u32[]{:S(2)}, u32[]{:S(2)}) collective-permute-start(bf16[768,768]{1,0:T(8,128)(2,1)} %get-tuple-element.122), channel_id=1, source_target_pairs={{0,8},{8,0},{16,24},{24,16},{1,9},{9,1},{17,25},{25,17},{2,10},{10... | collective-permute-start | bytes 3538952 | tf_op jit(solution)/shard_map/ppermute | solution.py:52
  288.4 41.8 %collective-permute-start.18 = (bf16[512,1024]{1,0:T(8,128)(2,1)}, bf16[512,1024]{1,0:T(8,128)(2,1)}, u32[]{:S(2)}, u32[]{:S(2)}) collective-permute-start(bf16[512,1024]{1,0:T(8,128)(2,1)} %slice.103), channel_id=1, source_target_pairs={{0,1},{1,0},{2,3},{3,2},{4,5},{5,4},{6,7},{7,6},{8,9},{9,8},{10,11... | collective-permute-start | bytes 3145736 | tf_op jit(solution)/shard_map/ppermute | solution.py:71
  319.1 54.1 %collective-permute-start.25 = (bf16[768,768]{1,0:T(8,128)(2,1)}, bf16[768,768]{1,0:T(8,128)(2,1)S(1)}, u32[]{:S(2)}, u32[]{:S(2)}) collective-permute-start(bf16[768,768]{1,0:T(8,128)(2,1)} %shard_map.412.refs_9_), channel_id=1, source_target_pairs={{0,8},{8,0},{16,24},{24,16},{1,9},{9,1},{17,25},{25,17},{2,10},{10... | collective-permute-start | bytes 3538952 | tf_op jit(solution)/shard_map/ppermute | solution.py:52
  319.1 57.9 %collective-permute-start.28 = (bf16[384,1280]{1,0:T(8,128)(2,1)S(1)}, bf16[384,1280]{1,0:T(8,128)(2,1)}, u32[]{:S(2)}, u32[]{:S(2)}) collective-permute-start(bf16[384,1280]{1,0:T(8,128)(2,1)S(1)} %copy-done.6), channel_id=1, source_target_pairs={{0,16},{8,24},{16,0},{24,8},{1,17},{9,25},{17,1},{25,9},{2,18},{10... | collective-permute-start | bytes 2949128 | tf_op jit(solution)/shard_map/ppermute | solution.py:57
  331.9 34.6 %collective-permute-start.23 = (bf16[384,768]{1,0:T(8,128)(2,1)S(1)}, bf16[384,768]{1,0:T(8,128)(2,1)S(1)}, u32[]{:S(2)}, u32[]{:S(2)}) collective-permute-start(bf16[384,768]{1,0:T(8,128)(2,1)S(1)} %copy-done.18), channel_id=1, source_target_pairs={{0,16},{8,24},{16,0},{24,8},{1,17},{9,25},{17,1},{25,9},{2,18},{10... | collective-permute-start | bytes 1769480 | tf_op jit(solution)/shard_map/ppermute | solution.py:57
  333.0 33.5 %collective-permute-start.19 = (bf16[256,1024]{1,0:T(8,128)(2,1)}, bf16[256,1024]{1,0:T(8,128)(2,1)}, u32[]{:S(2)}, u32[]{:S(2)}) collective-permute-start(bf16[256,1024]{1,0:T(8,128)(2,1)} %get-tuple-element.168), channel_id=1, source_target_pairs={{0,2},{1,3},{2,0},{3,1},{4,6},{5,7},{6,4},{7,5},{8,10},{9,11},{10,... | collective-permute-start | bytes 1572872 | tf_op jit(solution)/shard_map/ppermute | solution.py:71
  335.2 31.3 %collective-permute-start.20 = (bf16[320,768]{1,0:T(8,128)(2,1)}, bf16[320,768]{1,0:T(8,128)(2,1)}, u32[]{:S(2)}, u32[]{:S(2)}) collective-permute-start(bf16[320,768]{1,0:T(8,128)(2,1)} %get-tuple-element.161.refs_16_), channel_id=1, source_target_pairs={{0,16},{8,24},{16,0},{24,8},{1,17},{9,25},{17,1},{25,9},{2,18},{10... | collective-permute-start | bytes 1474568 | tf_op jit(solution)/shard_map/ppermute | solution.py:57
  372.5 52.6 %collective-permute-start.24 = (bf16[256,1536]{1,0:T(8,128)(2,1)}, bf16[256,1536]{1,0:T(8,128)(2,1)}, u32[]{:S(2)}, u32[]{:S(2)}) collective-permute-start(bf16[256,1536]{1,0:T(8,128)(2,1)} %shard_map.413.refs_3_), channel_id=1, source_target_pairs={{0,4},{4,0},{1,5},{5,1},{2,6},{6,2},{3,7},{7,3},{8,12},{12,8},{9,1... | collective-permute-start | bytes 2359304 | tf_op jit(solution)/shard_map/ppermute | solution.py:61
  383.9 41.2 %collective-permute-start.29 = (bf16[192,2048]{1,0:T(8,128)(2,1)}, bf16[192,2048]{1,0:T(8,128)(2,1)S(1)}, u32[]{:S(2)}, u32[]{:S(2)}) collective-permute-start(bf16[192,2048]{1,0:T(8,128)(2,1)} %get-tuple-element.128), channel_id=1, source_target_pairs={{0,1},{1,0},{2,3},{3,2},{4,5},{5,4},{6,7},{7,6},{8,9},{9,8},{10,11... | collective-permute-start | bytes 2359304 | tf_op jit(solution)/shard_map/ppermute | solution.py:71
  386.4 38.8 %collective-permute-start.26 = (bf16[384,768]{1,0:T(8,128)(2,1)S(1)}, bf16[384,768]{1,0:T(8,128)(2,1)S(1)}, u32[]{:S(2)}, u32[]{:S(2)}) collective-permute-start(bf16[384,768]{1,0:T(8,128)(2,1)S(1)} %copy-done.15), channel_id=1, source_target_pairs={{0,16},{8,24},{16,0},{24,8},{1,17},{9,25},{17,1},{25,9},{2,18},{10... | collective-permute-start | bytes 1769480 | tf_op jit(solution)/shard_map/ppermute | solution.py:57
  389.2 35.9 %collective-permute-start.27 = (bf16[160,768]{1,0:T(8,128)(2,1)}, bf16[160,768]{1,0:T(8,128)(2,1)S(1)}, u32[]{:S(2)}, u32[]{:S(2)}) collective-permute-start(bf16[160,768]{1,0:T(8,128)(2,1)} %bitcast.115), channel_id=1, source_target_pairs={{0,1},{1,0},{2,3},{3,2},{4,5},{5,4},{6,7},{7,6},{8,9},{9,8},{10,11... | collective-permute-start | bytes 737288 | tf_op jit(solution)/shard_map/ppermute | solution.py:71
  432.7 1.3 collective-permute-start.30
  434.1 3.9 collective-permute-start.31
  438.0 19.8 %collective-permute-start.32 = (f32[1,1328]{1,0:T(1,128)S(1)}, f32[1,1328]{1,0:T(1,128)S(1)}, u32[]{:S(2)}, u32[]{:S(2)}) collective-permute-start(f32[1,1328]{1,0:T(1,128)S(1)} %get-tuple-element.176), channel_id=1, source_target_pairs={{0,1},{1,0},{2,3},{3,2},{4,5},{5,4},{6,7},{7,6},{8,9},{9,8},{10,11... | collective-permute-start | bytes 15944 | tf_op jit(solution)/shard_map/ppermute | solution.py:71
  438.0 20.8 %collective-permute-start.34 = (f32[1,1328]{1,0:T(1,128)S(1)}, f32[1,1328]{1,0:T(1,128)S(1)}, u32[]{:S(2)}, u32[]{:S(2)}) collective-permute-start(f32[1,1328]{1,0:T(1,128)S(1)} %get-tuple-element.177), channel_id=1, source_target_pairs={{0,3},{1,2},{2,1},{3,0},{4,7},{5,6},{6,5},{7,4},{8,11},{9,10},{10,... | collective-permute-start | bytes 15944 | tf_op jit(solution)/shard_map/ppermute | solution.py:71
  440.5 18.3 %collective-permute-start.33 = (f32[1,1328]{1,0:T(1,128)S(1)}, f32[1,1328]{1,0:T(1,128)S(1)}, u32[]{:S(2)}, u32[]{:S(2)}) collective-permute-start(f32[1,1328]{1,0:T(1,128)S(1)} %get-tuple-element.178), channel_id=1, source_target_pairs={{0,2},{1,3},{2,0},{3,1},{4,6},{5,7},{6,4},{7,5},{8,10},{9,11},{10,... | collective-permute-start | bytes 15944 | tf_op jit(solution)/shard_map/ppermute | solution.py:71
  449.2 28.8 %collective-permute-start.35 = (bf16[96,2048]{1,0:T(8,128)(2,1)}, bf16[96,2048]{1,0:T(8,128)(2,1)S(1)}, u32[]{:S(2)}, u32[]{:S(2)}) collective-permute-start(bf16[96,2048]{1,0:T(8,128)(2,1)} %bitcast.91), channel_id=1, source_target_pairs={{0,2},{1,3},{2,0},{3,1},{4,6},{5,7},{6,4},{7,5},{8,10},{9,11},{10,... | collective-permute-start | bytes 1179656 | tf_op jit(solution)/shard_map/ppermute | solution.py:71
  453.0 20.3 %copy-start.36 = (f32[1,80,768]{2,1,0:T(8,128)S(1)}, f32[1,80,768]{2,1,0:T(8,128)}, u32[]{:S(2)}) copy-start(f32[1,80,768]{2,1,0:T(8,128)} %get-tuple-element.146) | copy-start | bytes 737284
  453.0 20.3 %collective-permute-start.36 = (bf16[80,768]{1,0:T(8,128)(2,1)}, bf16[80,768]{1,0:T(8,128)(2,1)S(1)}, u32[]{:S(2)}, u32[]{:S(2)}) collective-permute-start(bf16[80,768]{1,0:T(8,128)(2,1)} %bitcast.117), channel_id=1, source_target_pairs={{0,2},{1,3},{2,0},{3,1},{4,6},{5,7},{6,4},{7,5},{8,10},{9,11},{10,... | collective-permute-start | bytes 368648 | tf_op jit(solution)/shard_map/ppermute | solution.py:71
  457.8 20.2 %copy-start.23 = (f32[1,96,2048]{2,1,0:T(8,128)S(1)}, f32[1,96,2048]{2,1,0:T(8,128)}, u32[]{:S(2)}) copy-start(f32[1,96,2048]{2,1,0:T(8,128)} %get-tuple-element.141) | copy-start | bytes 2359300
  457.8 17.0 %collective-permute-start.37 = (bf16[192,768]{1,0:T(8,128)(2,1)}, bf16[192,768]{1,0:T(8,128)(2,1)S(1)}, u32[]{:S(2)}, u32[]{:S(2)}) collective-permute-start(bf16[192,768]{1,0:T(8,128)(2,1)} %get-tuple-element.149), channel_id=1, source_target_pairs={{0,1},{1,0},{2,3},{3,2},{4,5},{5,4},{6,7},{7,6},{8,9},{9,8},{10,11... | collective-permute-start | bytes 884744 | tf_op jit(solution)/shard_map/ppermute | solution.py:71
  477.5 8.1 %collective-permute-start.38 = (bf16[96,768]{1,0:T(8,128)(2,1)}, bf16[96,768]{1,0:T(8,128)(2,1)S(1)}, u32[]{:S(2)}, u32[]{:S(2)}) collective-permute-start(bf16[96,768]{1,0:T(8,128)(2,1)} %bitcast.116), channel_id=1, source_target_pairs={{0,2},{1,3},{2,0},{3,1},{4,6},{5,7},{6,4},{7,5},{8,10},{9,11},{10,... | collective-permute-start | bytes 442376 | tf_op jit(solution)/shard_map/ppermute | solution.py:71
  (48 other events, 278.5 us)
Sparse Core Ops, SparseCore 0:
  11.6 134.7 all-gather.1
  244.9 90.3 reduce-scatter.4
  339.6 86.2 reduce-scatter.2
where the time goes:
time: 503 us; the launch traced here: 497 us
  waiting for transfers between devices  251 us (50%)
  Pallas kernels  121 us (24%)
  starting transfers between devices  52.2 us (10%)
  local copies, waits for them, and re-layouts  22.5 us (4%)
  other arithmetic  20.1 us (4%)
  matrix products  15.4 us (3%)
  between operations  14.9 us (3%)
    pallas_call x16, Pallas kernels, run(): pl.pallas_call(kernel, grid=(grid,), in_specs=[spec(shape, index) for _,...  98.4 us
    all_gather x1, waiting for transfers between devices, shards(): big = lax.all_gather(piece, (IT, RW), axis=0, tiled=True)  83.8 us
    ppermute x14, waiting for transfers between devices, to_bit(): return lax.ppermute(a, RW, [(i, i ^ bit) for i in range(n)])  66.7 us
    ppermute x11, waiting for transfers between devices, to_head(): return lax.ppermute(a, HD, [(0, 1), (1, 0)])  39.8 us
    ppermute x5, waiting for transfers between devices, to_pair(): return lax.ppermute(a, IT, [(i, (i + 2 * k) % n) for i in range(n)])  32.9 us
    ppermute x2, waiting for transfers between devices, from_before(): return lax.ppermute(row, RW, [(i, i + 1) for i in range(n - 1)])  26.4 us
    ppermute x14, starting transfers between devices, to_bit(): return lax.ppermute(a, RW, [(i, i ^ bit) for i in range(n)])  20.7 us
    ppermute x2, starting transfers between devices, from_before(): return lax.ppermute(row, RW, [(i, i + 1) for i in range(n - 1)])  13.7 us
  transfers between devices with their start and end apart: 42, of which 17 were waited for; matrix products, arithmetic and copies ran while one was open for 8% of the time, Pallas kernels for 17%

commit v1 on v0

--- a/solution.py
+++ b/solution.py
@@ -75,7 +75,10 @@
     w, n = keep.shape[0] // pieces, keep.shape[1]
     shape = (pieces // 2, 2, w, n)
     if w % 16:
-        total = (keep + wide(jnp.concatenate(got, axis=1))).reshape(shape)
+        total = wide(keep)
+        if got:
+            total = total + wide(jnp.concatenate(got, axis=1))
+        total = total.reshape(shape)
         mine = lax.dynamic_index_in_dim(total, pick_bit, 1, keepdims=False)
         send = lax.dynamic_index_in_dim(total, 1 - pick_bit, 1, keepdims=False)
         return mine.reshape(-1, n), low(send).reshape(-1, n)
@@ -85,6 +88,9 @@
         got_refs, (mine_ref, send_ref) = refs[:-2], refs[-2:]
 
         def write(bit):
+            if not got:
+                mine_ref[0] = keep_ref[0, bit].astype(F32)
+                send_ref[0] = keep_ref[0, 1 - bit].astype(LOW)
             at = 0
             for ref, count in zip(got_refs, widths):
                 there = slice(at, at + count)
@@ -140,6 +146,16 @@
         start = pl.multiple_of(spots_ref[k] * w, 128)
         left = left_ref[pl.ds(0, right.shape[0]), pl.ds(start, w)]
         out_ref[k * w : (k + 1) * w, there] = tn(left, right).astype(LOW)
+
+
+def add_last(keep, got, after):
+    if keep.shape[0] % 16:
+        return keep + wide(got)
+
+    def body(keep_ref, got_ref, out_ref):
+        out_ref[...] = keep_ref[...] + got_ref[...].astype(F32)
+
+    return run(body, 1, [keep, got], [new(keep.shape, F32)], after=after)[0]
 
 
 def side_product(pairs_of, side, got=None, after=(), groups=None, others=False):
@@ -337,10 +353,29 @@
     def finish(self, after=()):
         while self.bit < lax.axis_size(RW):
             self.step(after)
-        return self.keep + wide(self.got[0])
-
-
-def scatter_small(parts):
+        return add_last(self.keep, self.got[0], after)
+
+
+class RowSum:
+    def __init__(self, keep):
+        self.keep, self.got, self.bit = keep, [], 1
+        self.z = lax.axis_index(RW)
+
+    def step(self, after=()):
+        pieces = lax.axis_size(RW) // self.bit
+        pick_bit = (self.z // self.bit) % 2
+        self.keep, self.sent = halve(self.keep, self.got, pick_bit, pieces, after)
+        self.got = [to_bit(self.sent, self.bit)]
+        self.bit *= 2
+        return self.got
+
+    def finish(self, after=()):
+        while self.bit < lax.axis_size(RW):
+            self.step(after)
+        return add_last(self.keep, self.got[0], after)
+
+
+def scatter_small(parts, after):
     pairs, rows = lax.axis_size(IT) // 2, lax.axis_size(RW)
     x, c, z = place()
     n = parts.shape[1]
@@ -353,11 +388,15 @@
         plane = plane + to_pair(
             lax.dynamic_index_in_dim(cube, (x + k) % pairs, 0, keepdims=False), k
         )
-    total = lax.dynamic_index_in_dim(plane, z, 0, keepdims=True)
+    terms = [lax.dynamic_index_in_dim(plane, z, 0, keepdims=True)]
     for k in range(1, rows):
         spot = jnp.bitwise_xor(z, k)
-        total = total + to_bit(lax.dynamic_index_in_dim(plane, spot, 0, keepdims=True), k)
-    return total
+        terms.append(to_bit(lax.dynamic_index_in_dim(plane, spot, 0, keepdims=True), k))
+
+    def body(*refs):
+        refs[-1][...] = sum(ref[...] for ref in refs[1:-1]) + refs[0][...]
+
+    return run(body, 1, terms, [new(terms[0].shape, F32)], after=after)[0]
 
 
 def attend_kernel(q_ref, kv_ref, wr_ref, basis_ref, out_ref, p_ref):
@@ -524,6 +563,22 @@
                 spot += KEY
 
 
+def pack_sums_kernel(shares, *refs):
+    rel_ref, out_ref = refs[-2:]
+    group = out_ref.shape[0]
+    heads, each = rel_ref.shape[0] // NB, NB // group
+    for g in range(group):
+        spot = 0
+        for (i, n), ref in zip(shares, refs):
+            out_ref[g : g + 1, spot : spot + n] = ref[i : i + 1, g * n : (g + 1) * n]
+            spot += n
+        for h in range(heads):
+            for j in range(each):
+                row = h * NB + g * each + j
+                out_ref[g : g + 1, spot : spot + KEY] = rel_ref[row : row + 1]
+                spot += KEY
+
+
 def project_kernel(rows, head_ref, *refs):
     own, other = refs[:rows], refs[rows : 2 * rows]
     gain_ref, bias_ref, qk_ref, v_ref, q_ref, kv_ref, normed_ref = refs[2 * rows :]
@@ -958,8 +1013,8 @@
         [pltpu.VMEM((width, model), F32)],
         after=[prev, later],
     )
-    grad_down, grad_up = (
-        lax.psum_scatter(t, (IT, RW), scatter_dimension=0, tiled=True) for t in theirs
+    for_down, for_up = (
+        RowSum(lax.psum_scatter(t, IT, scatter_dimension=0, tiled=True)) for t in theirs
     )
     mixed, grad_depth = run(
         section_kernel,
@@ -994,54 +1049,71 @@
         bit *= 2
     skip_across = [for_skip.across(0)]
     mixed_other = to_head(mixed)
+    skip_across = [for_skip.across(0)]
+    for_skip.take(skip_across)
     for_attn = Scatter(
         [(grad_proj_low, attended), (normed_all, dq), (normed_all, dkv)],
         theirs or None,
         [],
-        [],
-        [[0], [1, 2]],
-    )
-    attn_across = [for_attn.across(i) for i in range(2)]
+        summed[:1] + skip_across[0],
+        [[0, 1, 2]],
+    )
     mixed_full = both_halves(head, mixed, mixed_other)
-    for_point = Scatter([(mixed_full, grad_out)], None, for_attn.send)
-    for_skip.take(skip_across)
+    for_point = Scatter([(mixed_full, grad_out)], None, for_attn.send, for_attn.send)
+    for_down.step(for_point.theirs)
+    attn_across = [for_attn.across(0)]
+    for_attn.take(attn_across)
+    point_across = for_point.across(0)
+    for_point.take([point_across])
     (partial_one,) = run(
         functools.partial(project_back_kernel, len(dkv_parts)),
         1,
         [dq] + dkv_parts + [w_qk, w_value],
         [new((width, model), LOW)],
-        after=skip_across[0] + attn_across[0] + for_attn.send + for_point.theirs,
-    )
-    for_skip.step([partial_one])
-    point_across = for_point.across(0)
-    for_attn.take(attn_across)
-    for_attn.step(for_point.send)
+        after=for_point.send + [for_down.sent],
+    )
+    for_down.step([partial_one])
+    for_up.step([for_down.sent])
+    for_attn.step([for_up.sent])
+    for_skip.step([for_attn.sent])
     input_grad, grad_gain_one, grad_bias_one = run(
         outer_back_kernel,
         1,
         [at_head, own_blocks[0], other_blocks[0], partial_one, to_head(partial_one)]
         + [gain_one, resid],
         [new((width, chan), F32), new((1, model), F32), new((1, model), F32)],
-        after=point_across + for_skip.got + for_attn.got,
+        after=[for_skip.sent] + point_across + for_up.got + for_down.got,
     )
     input_grad = input_grad[None]
-    for_point.take([point_across])
-    for_attn.step()
-    for_point.step([for_attn.sent])
-    for_skip.step([for_attn.sent])
-    for_point.step([for_attn.sent])
-    grad_skip = for_skip.finish()
-    grad_attn, grad_point = for_attn.finish(), for_point.finish()
+    for_attn.step([grad_gain_one])
+    for_up.step([for_attn.sent] + for_skip.got)
+    for_point.step([for_up.sent])
+    for_skip.step([for_point.sent])
+    for_point.step([for_skip.sent] + for_attn.got)
+    last = [for_point.sent]
+    grad_down, grad_up, grad_skip = (part.finish(last) for part in (for_down, for_up, for_skip))
+    grad_attn, grad_point = for_attn.finish(last), for_point.finish(last)
     grad_out_w, grad_qkv = grad_attn[:, : heads * VAL], grad_attn[:, heads * VAL :]
     result = (nn(mixed_full, w_point[0][:, 2 * ff + chan : 2 * ff + 2 * chan]) + b_point).astype(LOW)
     block_output = tn(apart, result).astype(LOW)[None]
-    grad_depth = [grad_depth[k] for k in range(3)]
-
-    rel_parts = grad_rel.reshape(heads, group, rel_cols).transpose(1, 0, 2)
     parts = [grad_gain_one, grad_bias_one, grad_gain_two, grad_bias_two, grad_down_bias]
-    parts += [grad_up_bias, grad_skip_bias] + grad_depth + [grad_point_bias]
-    parts = jnp.concatenate([p.reshape(group, -1) for p in parts] + [rel_parts.reshape(group, -1)], axis=1)
-    sums = scatter_small(parts)
+    parts += [grad_up_bias, grad_skip_bias] + [grad_depth] * 3 + [grad_point_bias]
+    which = [0] * 7 + [0, 1, 2] + [0]
+    if NB % group == 0:
+        shares = [(i, p.shape[-1] // group) for i, p in zip(which, parts)]
+        total = sum(n for _, n in shares) + heads * rel_cols
+        (parts,) = run(
+            functools.partial(pack_sums_kernel, shares),
+            1,
+            [p.reshape(-1, p.shape[-1]) for p in parts] + [grad_rel],
+            [new((group, total), F32)],
+        )
+    else:
+        parts = [p.reshape(-1, p.shape[-1])[i] for i, p in zip(which, parts)]
+        rel_parts = grad_rel.reshape(heads, group, rel_cols).transpose(1, 0, 2)
+        parts = [p.reshape(group, -1) for p in parts + [rel_parts]]
+        parts = jnp.concatenate(parts, axis=1)
+    sums = scatter_small(parts, last)
 
     def own(start, count):
         return sums[0, start : start + count]
@@ -1059,9 +1131,9 @@
         grad_out_w.T,
         own(2 * shard, shard),
         own(3 * shard, shard),
-        wide(grad_up),
+        grad_up,
         own(5 * shard, shard)[None],
-        wide(grad_down).T,
+        grad_down.T,
         own(4 * shard, shard),
         grad_skip,
         own(at, small)[None],

time: 503 us -> 490 us (0.974)
  waiting for transfers between devices: 251 us -> 202 us
  Pallas kernels: 121 us -> 143 us
  starting transfers between devices: 52.2 us -> 67.5 us
    ppermute x5 -> x4, waiting for transfers between devices: 32.9 us -> 7.68 us  [to_pair(): return lax.ppermute(a, IT, [(i, (i + 2 * k) % n) for i in range(n)])]
    pallas_call x16 -> x27, Pallas kernels: 98.4 us -> 121 us  [run(): pl.pallas_call(kernel, grid=(grid,), in_specs=[spec(shape, index) for _,...]
    ppermute x14 -> x18, waiting for transfers between devices: 66.7 us -> 46.4 us  [to_bit(): return lax.ppermute(a, RW, [(i, i ^ bit) for i in range(n)])]
    ppermute x14 -> x18, starting transfers between devices: 20.7 us -> 34 us  [to_bit(): return lax.ppermute(a, RW, [(i, i ^ bit) for i in range(n)])]
    unnamed x111 -> x105, local copies, waits for them, and re-layouts: 12 us -> 13.5 us
  transfers between devices with their start and end apart: 42 -> 45, of which waited for: 17 -> 19; matrix products, arithmetic and copies ran while one was open for 8% -> 9% of each run, Pallas kernels for 17% -> 20%
where the time goes in v1:
time: 490 us; the launch traced here: 486 us
  waiting for transfers between devices  202 us (41%)
  Pallas kernels  143 us (29%)
  starting transfers between devices  67.5 us (14%)
  local copies, waits for them, and re-layouts  26.8 us (5%)
  other arithmetic  16.3 us (3%)
  matrix products  15.4 us (3%)
  between operations  14.7 us (3%)
    pallas_call x27, Pallas kernels, run(): pl.pallas_call(kernel, grid=(grid,), in_specs=[spec(shape, index) for _,...  121 us
    all_gather x1, waiting for transfers between devices, shards(): big = lax.all_gather(piece, (IT, RW), axis=0, tiled=True)  83.9 us
    ppermute x18, waiting for transfers between devices, to_bit(): return lax.ppermute(a, RW, [(i, i ^ bit) for i in range(n)])  46.4 us
    ppermute x11, waiting for transfers between devices, to_head(): return lax.ppermute(a, HD, [(0, 1), (1, 0)])  38.9 us
    ppermute x18, starting transfers between devices, to_bit(): return lax.ppermute(a, RW, [(i, i ^ bit) for i in range(n)])  34 us
    ppermute x2, waiting for transfers between devices, from_before(): return lax.ppermute(row, RW, [(i, i + 1) for i in range(n - 1)])  24.5 us
    ppermute x2, starting transfers between devices, from_before(): return lax.ppermute(row, RW, [(i, i + 1) for i in range(n - 1)])  13.7 us
    unnamed x105, local copies, waits for them, and re-layouts  13.5 us
  transfers between devices with their start and end apart: 45, of which 19 were waited for; matrix products, arithmetic and copies ran while one was open for 9% of the time, Pallas kernels for 20%

profile of v1, /device:TPU:0, one launch (start us, length us, event | category | flops | bytes accessed | tf_op | source)
XLA Modules:
  0.0 485.8 jit_solution(13080529760286553739)
XLA Ops:
  8.5 3.0 shard_map.401
  11.6 5.1 %collective-permute-start.3 = (bf16[256,768]{1,0:T(8,128)(2,1)S(1)}, bf16[256,768]{1,0:T(8,128)(2,1)S(1)}, u32[]{:S(2)}, u32[]{:S(2)}) collective-permute-start(bf16[256,768]{1,0:T(8,128)(2,1)S(1)} %bitcast.101), channel_id=1, source_target_pairs={{0,3},{1,2},{2,1},{3,0},{4,7},{5,6},{6,5},{7,4},{8,11},{9,10},{10,... | collective-permute-start | bytes 1179656 | tf_op jit(solution)/shard_map/ppermute | solution.py:71
  19.2 3.1 collective-permute-start.7
  24.9 3.7 convolution_convert_fusion.refs_13_
  29.2 23.8 %collective-permute-done.7 = bf16[1,768]{1,0:T(2,128)(2,1)S(1)} collective-permute-done((bf16[1,768]{1,0:T(2,128)(2,1)S(1)}, bf16[1,768]{1,0:T(2,128)(2,1)S(1)}, u32[]{:S(2)}, u32[]{:S(2)}) %collective-permute-start.7) | collective-permute-done | bytes 1568 | tf_op jit(solution)/shard_map/ppermute | solution.py:825
  62.5 83.9 %all-gather.2.cloned.1.call-done.refs_0_.refs_11_.refs_12_.refs_4_.refs_9_.refs_10_.refs_2_.refs_5_.refs_7_.refs_3_ = bf16[1536,6656]{1,0:T(8,128)(2,1)} async-done(((bf16[96,6656]{1,0:T(8,128)(2,1)}), bf16[1536,6656]{1,0:T(8,128)(2,1)}) %all-gather.2.cloned.1.call-update) | async-done | bytes 20447248 | tf_op jit(solution)/shard_map/all_gather | solution.py:894
  146.4 3.3 shard_map.402
  150.7 9.8 %shard_map.403 = (bf16[256,256]{1,0:T(8,128)(2,1)}, bf16[1024,1024]{1,0:T(8,128)(2,1)}, bf16[1024,1536]{1,0:T(8,128)(2,1)}) custom-call(s32[1]{0:T(128)} %bitcast.refs_0_, bf16[256,768]{1,0:T(8,128)(2,1)} %bitcast.98, bf16[256,768]{1,0:T(8,128)(2,1)} %copy-done.31, bf16[256,768]{1,0:T(8,128)(2,1)} %copy-done.30, bf16[256,768]{1,0:T(8,128)(2,1)} %copy-done.29, ...), custom_call_target="tpu_custom_call" | custom-call | flops 1 | bytes 1 | tf_op jit(solution)/shard_map/pallas_call | solution.py:485
  160.5 9.5 %shard_map.404 = (bf16[256,768]{1,0:T(8,128)(2,1)}, bf16[4,256,1024]{2,1,0:T(8,128)(2,1)}, bf16[256,1536]{1,0:T(8,128)(2,1)}) custom-call(bf16[256,256]{1,0:T(8,128)(2,1)} %get-tuple-element.94.refs_0_.refs_8_, bf16[1024,1024]{1,0:T(8,128)(2,1)} %get-tuple-element.95.refs_1_.refs_9_, f32[128,64]{1,0:T(8,128)} %get-tuple-element.96.refs_2_.refs_10_, ...), custom_call_target="tpu_custom_call" | custom-call | flops 1 | bytes 1 | tf_op jit(solution)/shard_map/pallas_call | solution.py:485
  171.5 4.8 shard_map.406
  176.8 4.4 convolution_add_fusion.refs_11_.refs_1_
  181.2 9.4 %collective-permute-done.9.refs_4_ = bf16[256,1536]{1,0:T(8,128)(2,1)S(1)} collective-permute-done((bf16[256,1536]{1,0:T(8,128)(2,1)}, bf16[256,1536]{1,0:T(8,128)(2,1)S(1)}, u32[]{:S(2)}, u32[]{:S(2)}) %collective-permute-start.9) | collective-permute-done | bytes 786464 | tf_op jit(solution)/shard_map/ppermute | solution.py:61
  191.5 10.9 %shard_map.405 = (f32[256,1536]{1,0:T(8,128)}, bf16[256,1536]{1,0:T(8,128)(2,1)}, bf16[256,1536]{1,0:T(8,128)(2,1)}, bf16[256,1536]{1,0:T(8,128)(2,1)}, f32[256,768]{1,0:T(8,128)}, /*index=5*/bf16[256,768]{1,0:T(8,128)(2,1)}) custom-call(s32[1]{0:T(128)} %bitcast.refs_0_, bf16[256,768]{1,0:T(8,128)(2,1)} %bitcast.99, bf16[256,768]{1,0:T(8,128)(2,1)} %copy-done.8, ...), custom_call_target="tpu_custom_call" | custom-call | flops 1 | bytes 1 | tf_op jit(solution)/shard_map/pallas_call | solution.py:485
  206.9 3.7 shard_map.407
  211.5 2.6 reduce-precision_convert_fusion.2
  217.7 10.6 %collective-permute-start.11 = (bf16[1,768]{1,0:T(2,128)(2,1)S(1)}, bf16[1,768]{1,0:T(2,128)(2,1)S(1)}, u32[]{:S(2)}, u32[]{:S(2)}) collective-permute-start(bf16[1,768]{1,0:T(2,128)(2,1)S(1)} %get-tuple-element.228), channel_id=1, source_target_pairs={{0,1},{1,2},{2,3},{4,5},{5,6},{6,7},{8,9},{9,10},{10,11},{12,13},{... | collective-permute-start | bytes 4616 | tf_op jit(solution)/shard_map/ppermute | solution.py:825
  230.9 13.7 %shard_map.409 = (bf16[256,1536]{1,0:T(8,128)(2,1)}, bf16[256,1536]{1,0:T(8,128)(2,1)}, bf16[256,1536]{1,0:T(8,128)(2,1)}, f32[1,1536]{1,0:T(1,128)}, f32[1,1536...) custom-call(s32[1]{0:T(128)} %bitcast.refs_0_, bf16[256,768]{1,0:T(8,128)(2,1)} %copy-done.17, ...), custom_call_target="tpu_custom_call" | custom-call | flops 1 | bytes 1 | tf_op jit(solution)/shard_map/pallas_call | solution.py:485
  248.7 4.1 shard_map.408
  254.9 12.5 %collective-permute-done.16.refs_2_ = bf16[256,1536]{1,0:T(8,128)(2,1)S(1)} collective-permute-done((bf16[256,1536]{1,0:T(8,128)(2,1)S(1)}, bf16[256,1536]{1,0:T(8,128)(2,1)S(1)}, u32[]{:S(2)}, u32[]{:S(2)}) %collective-permute-start.16) | collective-permute-done | bytes 786464 | tf_op jit(solution)/shard_map/ppermute | solution.py:61
  268.4 17.7 %shard_map.410 = (bf16[256,1536]{1,0:T(8,128)(2,1)}, f32[256,768]{1,0:T(8,128)}, f32[1,1536]{1,0:T(1,128)}, f32[1,1536]{1,0:T(1,128)}, bf16[256,256]{1,0:T(8,128...) custom-call(s32[1]{0:T(128)} %bitcast.refs_0_, ...), custom_call_target="tpu_custom_call" | custom-call | flops 1 | bytes 1 | tf_op jit(solution)/shard_map/pallas_call | solution.py:485
  286.6 2.3 slice.94
  289.0 2.3 collective-permute-start.18
  292.0 14.1 %collective-permute-done.14 = bf16[512,768]{1,0:T(8,128)(2,1)} collective-permute-done((bf16[512,768]{1,0:T(8,128)(2,1)S(1)}, bf16[512,768]{1,0:T(8,128)(2,1)}, u32[]{:S(2)}, u32[]{:S(2)}) %collective-permute-start.14) | collective-permute-done | bytes 786464 | tf_op jit(solution)/shard_map/ppermute | solution.py:61
  308.7 6.3 %collective-permute-done.18 = bf16[512,1024]{1,0:T(8,128)(2,1)} collective-permute-done((bf16[512,1024]{1,0:T(8,128)(2,1)}, bf16[512,1024]{1,0:T(8,128)(2,1)}, u32[]{:S(2)}, u32[]{:S(2)}) %collective-permute-start.18) | collective-permute-done | bytes 1048608 | tf_op jit(solution)/shard_map/ppermute | solution.py:71
  315.1 3.0 reduce-precision_convert_fusion.refs_8_
  319.2 5.0 %shard_map.411.refs_2_.refs_3_ = bf16[384,2048]{1,0:T(8,128)(2,1)} custom-call(s32[1]{0:T(128)} %bitcast.15.spot_ref, bf16[256,1536]{1,0:T(8,128)(2,1)} %get-tuple-element.127.refs_0_, bf16[1024,1536]{1,0:T(8,128)(2,1)} %get-tuple-element.122.refs_14_.refs_1_.refs_2_, bf16[1024,1536]{1,0:T(8,128)(2,1)} %get-tuple-element.122.refs_14_.refs_1_.refs_2_, ...), custom_call_target="tpu_custom_call" | custom-call | flops 1 | bytes 1 | tf_op jit(solution)/shard_map/pallas_call | solution.py:231
  324.3 4.0 shard_map.412.refs_2_
  329.9 4.0 collective-permute-start.19
  333.8 2.3 shard_map.414
  338.9 2.8 shard_map.413.refs_5_
  341.6 16.1 %collective-permute-done.19.refs_2_ = bf16[256,1024]{1,0:T(8,128)(2,1)} collective-permute-done((bf16[256,1024]{1,0:T(8,128)(2,1)}, bf16[256,1024]{1,0:T(8,128)(2,1)}, u32[]{:S(2)}, u32[]{:S(2)}) %collective-permute-start.19) | collective-permute-done | bytes 524320 | tf_op jit(solution)/shard_map/ppermute | solution.py:71
  357.8 4.6 shard_map.415.refs_3_
  364.7 2.4 shard_map.416
  367.1 2.3 shard_map.417
  369.9 3.4 collective-permute-start.29
  373.9 3.2 collective-permute-done.25.refs_8_
  377.1 6.6 %shard_map.418 = (f32[192,2048]{1,0:T(8,128)}, bf16[192,2048]{1,0:T(8,128)(2,1)}) custom-call(s32[2]{0:T(128)} %pad_add_fusion.2.at_ref, bf16[256,1536]{1,0:T(8,128)(2,1)} %get-tuple-element.127.refs_0_, bf16[1024,1536]{1,0:T(8,128)(2,1)} %get-tuple-element.122.refs_14_.refs_1_.refs_2_, bf16[1024,1536]{1,0:T(8,128)(2,1)} %get-tuple-element.122.refs_14_.refs_1_.refs_2_, ...), custom_call_target="tpu_custom_call" | custom-call | flops 1 | bytes 1 | tf_op jit(solution)/shard_map/pallas_call | solution.py:289
  385.9 3.6 collective-permute-done.27.refs_8_.refs_3_
  391.1 4.1 shard_map.420
  398.2 2.5 collective-permute-start.35
  409.7 9.6 %collective-permute-done.35 = bf16[192,2048]{1,0:T(8,128)(2,1)S(1)} collective-permute-done((bf16[192,2048]{1,0:T(8,128)(2,1)S(1)}, bf16[192,2048]{1,0:T(8,128)(2,1)S(1)}, u32[]{:S(2)}, u32[]{:S(2)}) %collective-permute-start.35) | collective-permute-done | bytes 786464 | tf_op jit(solution)/shard_map/ppermute | solution.py:71
  420.2 2.8 shard_map.422
  425.2 2.6 shard_map.423
  427.8 3.9 shard_map.424
  433.8 4.9 %fusion.16 = bf16[1,512,768]{2,1,0:T(8,128)(2,1)} fusion(bf16[1536,6656]{1,0:T(8,128)(2,1)} %all-gather.2.cloned.1.call-done.refs_0_.refs_11_.refs_12_.refs_4_.refs_9_.refs_10_.refs_2_.refs_5_.refs_7_.refs_3_, f32[768]{0:T(1024)S(1)} %reduce.2, pred[256,512]{1,0:T(32,128)(4,1)S(1)} %copy-done.39, pred[256,512]{1,0:T(32,128)(4,1)S(1)} %copy-done.41, ...), kind=kOutput, calls=%fused_computation.28 | convolution fusion | flops 1615200256 | bytes 4983808 | tf_op jit(solution)/shard_map/dot_general | solution.py:31
  440.6 7.2 %collective-permute-done.37 = bf16[192,768]{1,0:T(8,128)(2,1)S(1)} collective-permute-done((bf16[192,768]{1,0:T(8,128)(2,1)}, bf16[192,768]{1,0:T(8,128)(2,1)S(1)}, u32[]{:S(2)}, u32[]{:S(2)}) %collective-permute-start.37) | collective-permute-done | bytes 294944 | tf_op jit(solution)/shard_map/ppermute | solution.py:71
  458.5 2.2 shard_map.428
  465.9 4.4 collective-permute-done.39.refs_1_
  (233 shorter events, 98.9 us)
Async XLA Ops:
  7.2 139.2 %all-gather.2.cloned.1.call-start = ((), (), s32[]{:S(2)}) async-start(), calls=%async_computation.2 | async-start | bytes 21725184 | tf_op jit(solution)/shard_map/all_gather | solution.py:894
  11.5 322.3 %reduce-scatter.3.cloned.1.call-start = ((), (), s32[]{:S(2)}) async-start(), calls=%async_computation.3 | async-start | bytes 5898240 | tf_op jit(solution)/shard_map/reduce_scatter | solution.py:1017
  11.6 43.0 %collective-permute-start.3 = (bf16[256,768]{1,0:T(8,128)(2,1)S(1)}, bf16[256,768]{1,0:T(8,128)(2,1)S(1)}, u32[]{:S(2)}, u32[]{:S(2)}) collective-permute-start(bf16[256,768]{1,0:T(8,128)(2,1)S(1)} %bitcast.101), channel_id=1, source_target_pairs={{0,3},{1,2},{2,1},{3,0},{4,7},{5,6},{6,5},{7,4},{8,11},{9,10},{10,... | collective-permute-start | bytes 1179656 | tf_op jit(solution)/shard_map/ppermute | solution.py:71
  16.7 39.3 %collective-permute-start.2 = (bf16[256,768]{1,0:T(8,128)(2,1)S(1)}, bf16[256,768]{1,0:T(8,128)(2,1)S(1)}, u32[]{:S(2)}, u32[]{:S(2)}) collective-permute-start(bf16[256,768]{1,0:T(8,128)(2,1)S(1)} %bitcast.102), channel_id=1, source_target_pairs={{0,1},{1,0},{2,3},{3,2},{4,5},{5,4},{6,7},{7,6},{8,9},{9,8},{10,11... | collective-permute-start | bytes 1179656 | tf_op jit(solution)/shard_map/ppermute | solution.py:71
  16.7 42.0 %collective-permute-start.1 = (bf16[256,768]{1,0:T(8,128)(2,1)S(1)}, bf16[256,768]{1,0:T(8,128)(2,1)S(1)}, u32[]{:S(2)}, u32[]{:S(2)}) collective-permute-start(bf16[256,768]{1,0:T(8,128)(2,1)S(1)} %bitcast.103), channel_id=1, source_target_pairs={{0,2},{1,3},{2,0},{3,1},{4,6},{5,7},{6,4},{7,5},{8,10},{9,11},{10,... | collective-permute-start | bytes 1179656 | tf_op jit(solution)/shard_map/ppermute | solution.py:71
  17.3 132.4 %collective-permute-start = (bf16[256,768]{1,0:T(8,128)(2,1)S(1)}, bf16[256,768]{1,0:T(8,128)(2,1)S(1)}, u32[]{:S(2)}, u32[]{:S(2)}) collective-permute-start(bf16[256,768]{1,0:T(8,128)(2,1)S(1)} %bitcast.104), channel_id=1, source_target_pairs={{0,4},{4,0},{1,5},{5,1},{2,6},{6,2},{3,7},{7,3},{8,12},{12,8},{9,1... | collective-permute-start | bytes 1179656 | tf_op jit(solution)/shard_map/ppermute | solution.py:61
  19.2 33.8 %collective-permute-start.7 = (bf16[1,768]{1,0:T(2,128)(2,1)S(1)}, bf16[1,768]{1,0:T(2,128)(2,1)S(1)}, u32[]{:S(2)}, u32[]{:S(2)}) collective-permute-start(bf16[1,768]{1,0:T(2,128)(2,1)S(1)} %get-tuple-element.243), channel_id=1, source_target_pairs={{0,1},{1,2},{2,3},{4,5},{5,6},{6,7},{8,9},{9,10},{10,11},{12,13},{... | collective-permute-start | bytes 4616 | tf_op jit(solution)/shard_map/ppermute | solution.py:825
  29.2 120.4 %copy-start.2 = (bf16[512,768]{1,0:T(8,128)(2,1)}, bf16[512,768]{1,0:T(8,128)(2,1)S(1)}, u32[]{:S(2)}) copy-start(bf16[512,768]{1,0:T(8,128)(2,1)S(1)} %convolution_convert_fusion.2.refs_1_) | copy-start | bytes 2359300
  53.0 8.4 %collective-permute-start.8 = (bf16[1,768]{1,0:T(2,128)(2,1)S(1)}, bf16[1,768]{1,0:T(2,128)(2,1)S(1)}, u32[]{:S(2)}, u32[]{:S(2)}) collective-permute-start(bf16[1,768]{1,0:T(2,128)(2,1)S(1)} %get-tuple-element.244), channel_id=1, source_target_pairs={{1,0},{2,1},{3,2},{5,4},{6,5},{7,6},{9,8},{10,9},{11,10},{13,12},{... | collective-permute-start | bytes 4616 | tf_op jit(solution)/shard_map/ppermute | solution.py:830
  54.5 95.2 %copy-start.29 = (bf16[256,768]{1,0:T(8,128)(2,1)}, bf16[256,768]{1,0:T(8,128)(2,1)S(1)}, u32[]{:S(2)}) copy-start(bf16[256,768]{1,0:T(8,128)(2,1)S(1)} %collective-permute-done.3.refs_4_) | copy-start | bytes 1179652
  54.5 95.2 %collective-permute-start.6 = (bf16[256,768]{1,0:T(8,128)(2,1)S(1)}, bf16[256,768]{1,0:T(8,128)(2,1)S(1)}, u32[]{:S(2)}, u32[]{:S(2)}) collective-permute-start(bf16[256,768]{1,0:T(8,128)(2,1)S(1)} %collective-permute-done.3.refs_4_), channel_id=1, source_target_pairs={{0,4},{4,0},{1,5},{5,1},{2,6},{6,2},{3,7},{7,3},{8,12},{12,8},{9,1... | collective-permute-start | bytes 1179656 | tf_op jit(solution)/shard_map/ppermute | solution.py:61
  56.0 93.7 %copy-start.30 = (bf16[256,768]{1,0:T(8,128)(2,1)}, bf16[256,768]{1,0:T(8,128)(2,1)S(1)}, u32[]{:S(2)}) copy-start(bf16[256,768]{1,0:T(8,128)(2,1)S(1)} %collective-permute-done.2.refs_3_) | copy-start | bytes 1179652
  56.0 93.8 %collective-permute-start.5 = (bf16[256,768]{1,0:T(8,128)(2,1)S(1)}, bf16[256,768]{1,0:T(8,128)(2,1)}, u32[]{:S(2)}, u32[]{:S(2)}) collective-permute-start(bf16[256,768]{1,0:T(8,128)(2,1)S(1)} %collective-permute-done.2.refs_3_), channel_id=1, source_target_pairs={{0,4},{4,0},{1,5},{5,1},{2,6},{6,2},{3,7},{7,3},{8,12},{12,8},{9,1... | collective-permute-start | bytes 1179656 | tf_op jit(solution)/shard_map/ppermute | solution.py:61
  58.6 91.1 %collective-permute-start.4 = (bf16[256,768]{1,0:T(8,128)(2,1)S(1)}, bf16[256,768]{1,0:T(8,128)(2,1)}, u32[]{:S(2)}, u32[]{:S(2)}) collective-permute-start(bf16[256,768]{1,0:T(8,128)(2,1)S(1)} %collective-permute-done.1.refs_2_), channel_id=1, source_target_pairs={{0,4},{4,0},{1,5},{5,1},{2,6},{6,2},{3,7},{7,3},{8,12},{12,8},{9,1... | collective-permute-start | bytes 1179656 | tf_op jit(solution)/shard_map/ppermute | solution.py:61
  169.9 20.7 %collective-permute-start.9 = (bf16[256,1536]{1,0:T(8,128)(2,1)}, bf16[256,1536]{1,0:T(8,128)(2,1)S(1)}, u32[]{:S(2)}, u32[]{:S(2)}) collective-permute-start(bf16[256,1536]{1,0:T(8,128)(2,1)} %get-tuple-element.97.refs_3_), channel_id=1, source_target_pairs={{0,4},{4,0},{1,5},{5,1},{2,6},{6,2},{3,7},{7,3},{8,12},{12,8},{9,1... | collective-permute-start | bytes 2359304 | tf_op jit(solution)/shard_map/ppermute | solution.py:61
  176.3 29.8 %collective-permute-start.13 = (bf16[528,768]{1,0:T(8,128)(2,1)}, bf16[528,768]{1,0:T(8,128)(2,1)S(1)}, u32[]{:S(2)}, u32[]{:S(2)}) collective-permute-start(bf16[528,768]{1,0:T(8,128)(2,1)} %get-tuple-element.107), channel_id=1, source_target_pairs={{0,4},{4,0},{1,5},{5,1},{2,6},{6,2},{3,7},{7,3},{8,12},{12,8},{9,1... | collective-permute-start | bytes 2433032 | tf_op jit(solution)/shard_map/ppermute | solution.py:61
  202.4 9.1 %collective-permute-start.10 = (bf16[256,768]{1,0:T(8,128)(2,1)}, bf16[256,768]{1,0:T(8,128)(2,1)S(1)}, u32[]{:S(2)}, u32[]{:S(2)}) collective-permute-start(bf16[256,768]{1,0:T(8,128)(2,1)} %get-tuple-element.105), channel_id=1, source_target_pairs={{0,4},{4,0},{1,5},{5,1},{2,6},{6,2},{3,7},{7,3},{8,12},{12,8},{9,1... | collective-permute-start | bytes 1179656 | tf_op jit(solution)/shard_map/ppermute | solution.py:61
  214.1 16.1 %collective-permute-start.15 = (bf16[256,768]{1,0:T(8,128)(2,1)S(1)}, bf16[256,768]{1,0:T(8,128)(2,1)S(1)}, u32[]{:S(2)}, u32[]{:S(2)}) collective-permute-start(bf16[256,768]{1,0:T(8,128)(2,1)S(1)} %get-tuple-element.224.refs_1_), channel_id=1, source_target_pairs={{0,4},{4,0},{1,5},{5,1},{2,6},{6,2},{3,7},{7,3},{8,12},{12,8},{9,1... | collective-permute-start | bytes 1179656 | tf_op jit(solution)/shard_map/ppermute | solution.py:61
  216.4 11.9 %collective-permute-start.12 = (bf16[1,768]{1,0:T(2,128)(2,1)S(1)}, bf16[1,768]{1,0:T(2,128)(2,1)S(1)}, u32[]{:S(2)}, u32[]{:S(2)}) collective-permute-start(bf16[1,768]{1,0:T(2,128)(2,1)S(1)} %get-tuple-element.227), channel_id=1, source_target_pairs={{1,0},{2,1},{3,2},{5,4},{6,5},{7,6},{9,8},{10,9},{11,10},{13,12},{... | collective-permute-start | bytes 4616 | tf_op jit(solution)/shard_map/ppermute | solution.py:830
  217.7 11.9 %collective-permute-start.11 = (bf16[1,768]{1,0:T(2,128)(2,1)S(1)}, bf16[1,768]{1,0:T(2,128)(2,1)S(1)}, u32[]{:S(2)}, u32[]{:S(2)}) collective-permute-start(bf16[1,768]{1,0:T(2,128)(2,1)S(1)} %get-tuple-element.228), channel_id=1, source_target_pairs={{0,1},{1,2},{2,3},{4,5},{5,6},{6,7},{8,9},{9,10},{10,11},{12,13},{... | collective-permute-start | bytes 4616 | tf_op jit(solution)/shard_map/ppermute | solution.py:825
  244.6 122.5 %reduce-scatter.5.cloned.1.call-start = ((), (), s32[]{:S(2)}) async-start(), calls=%async_computation.4 | async-start | bytes 5898240 | tf_op jit(solution)/shard_map/reduce_scatter | solution.py:1017
  247.4 5.4 %collective-permute-start.17 = (bf16[640,768]{1,0:T(8,128)(2,1)S(1)}, bf16[640,768]{1,0:T(8,128)(2,1)S(1)}, u32[]{:S(2)}, u32[]{:S(2)}) collective-permute-start(bf16[640,768]{1,0:T(8,128)(2,1)S(1)} %reduce-precision_convert_fusion.1), channel_id=1, source_target_pairs={{0,8},{8,0},{16,24},{24,16},{1,9},{9,1},{17,25},{25,17},{2,10},{10... | collective-permute-start | bytes 2949128 | tf_op jit(solution)/shard_map/ppermute | solution.py:52
  247.6 19.8 %collective-permute-start.16 = (bf16[256,1536]{1,0:T(8,128)(2,1)S(1)}, bf16[256,1536]{1,0:T(8,128)(2,1)S(1)}, u32[]{:S(2)}, u32[]{:S(2)}) collective-permute-start(bf16[256,1536]{1,0:T(8,128)(2,1)S(1)} %copy-done.26), channel_id=1, source_target_pairs={{0,4},{4,0},{1,5},{5,1},{2,6},{6,2},{3,7},{7,3},{8,12},{12,8},{9,1... | collective-permute-start | bytes 2359304 | tf_op jit(solution)/shard_map/ppermute | solution.py:61
  286.0 32.0 %collective-permute-start.21 = (bf16[768,1280]{1,0:T(8,128)(2,1)}, bf16[768,1280]{1,0:T(8,128)(2,1)}, u32[]{:S(2)}, u32[]{:S(2)}) collective-permute-start(bf16[768,1280]{1,0:T(8,128)(2,1)} %get-tuple-element.129), channel_id=1, source_target_pairs={{0,8},{8,0},{16,24},{24,16},{1,9},{9,1},{17,25},{25,17},{2,10},{10... | collective-permute-start | bytes 5898248 | tf_op jit(solution)/shard_map/ppermute | solution.py:52
  286.1 20.1 %collective-permute-start.14 = (bf16[512,768]{1,0:T(8,128)(2,1)S(1)}, bf16[512,768]{1,0:T(8,128)(2,1)}, u32[]{:S(2)}, u32[]{:S(2)}) collective-permute-start(bf16[512,768]{1,0:T(8,128)(2,1)S(1)} %copy-done.13), channel_id=1, source_target_pairs={{0,4},{4,0},{1,5},{5,1},{2,6},{6,2},{3,7},{7,3},{8,12},{12,8},{9,1... | collective-permute-start | bytes 2359304 | tf_op jit(solution)/shard_map/ppermute | solution.py:61
  289.0 26.1 %collective-permute-start.18 = (bf16[512,1024]{1,0:T(8,128)(2,1)}, bf16[512,1024]{1,0:T(8,128)(2,1)}, u32[]{:S(2)}, u32[]{:S(2)}) collective-permute-start(bf16[512,1024]{1,0:T(8,128)(2,1)} %slice.94), channel_id=1, source_target_pairs={{0,1},{1,0},{2,3},{3,2},{4,5},{5,4},{6,7},{7,6},{8,9},{9,8},{10,11... | collective-permute-start | bytes 3145736 | tf_op jit(solution)/shard_map/ppermute | solution.py:71
  291.3 26.7 %collective-permute-start.20 = (bf16[768,768]{1,0:T(8,128)(2,1)}, bf16[768,768]{1,0:T(8,128)(2,1)S(1)}, u32[]{:S(2)}, u32[]{:S(2)}) collective-permute-start(bf16[768,768]{1,0:T(8,128)(2,1)} %get-tuple-element.128), channel_id=1, source_target_pairs={{0,8},{8,0},{16,24},{24,16},{1,9},{9,1},{17,25},{25,17},{2,10},{10... | collective-permute-start | bytes 3538952 | tf_op jit(solution)/shard_map/ppermute | solution.py:52
  291.3 26.7 %collective-permute-start.22 = (bf16[320,768]{1,0:T(8,128)(2,1)}, bf16[320,768]{1,0:T(8,128)(2,1)S(1)}, u32[]{:S(2)}, u32[]{:S(2)}) collective-permute-start(bf16[320,768]{1,0:T(8,128)(2,1)} %get-tuple-element.230.refs_16_), channel_id=1, source_target_pairs={{0,16},{8,24},{16,0},{24,8},{1,17},{9,25},{17,1},{25,9},{2,18},{10... | collective-permute-start | bytes 1474568 | tf_op jit(solution)/shard_map/ppermute | solution.py:57
  328.3 9.6 %collective-permute-start.23 = (bf16[768,768]{1,0:T(8,128)(2,1)}, bf16[768,768]{1,0:T(8,128)(2,1)S(1)}, u32[]{:S(2)}, u32[]{:S(2)}) collective-permute-start(bf16[768,768]{1,0:T(8,128)(2,1)} %shard_map.412.refs_2_), channel_id=1, source_target_pairs={{0,8},{8,0},{16,24},{24,16},{1,9},{9,1},{17,25},{25,17},{2,10},{10... | collective-permute-start | bytes 3538952 | tf_op jit(solution)/shard_map/ppermute | solution.py:52
  328.3 48.9 %collective-permute-start.25 = (bf16[384,2048]{1,0:T(8,128)(2,1)S(1)}, bf16[384,2048]{1,0:T(8,128)(2,1)}, u32[]{:S(2)}, u32[]{:S(2)}) collective-permute-start(bf16[384,2048]{1,0:T(8,128)(2,1)S(1)} %copy-done.1), channel_id=1, source_target_pairs={{0,16},{8,24},{16,0},{24,8},{1,17},{9,25},{17,1},{25,9},{2,18},{10... | collective-permute-start | bytes 4718600 | tf_op jit(solution)/shard_map/ppermute | solution.py:57
  329.9 27.9 %collective-permute-start.19 = (bf16[256,1024]{1,0:T(8,128)(2,1)}, bf16[256,1024]{1,0:T(8,128)(2,1)}, u32[]{:S(2)}, u32[]{:S(2)}) collective-permute-start(bf16[256,1024]{1,0:T(8,128)(2,1)} %get-tuple-element.237), channel_id=1, source_target_pairs={{0,2},{1,3},{2,0},{3,1},{4,6},{5,7},{6,4},{7,5},{8,10},{9,11},{10,... | collective-permute-start | bytes 1572872 | tf_op jit(solution)/shard_map/ppermute | solution.py:71
  336.2 28.5 %collective-permute-start.26 = (bf16[192,1536]{1,0:T(8,128)(2,1)}, bf16[192,1536]{1,0:T(8,128)(2,1)}, u32[]{:S(2)}, u32[]{:S(2)}) collective-permute-start(bf16[192,1536]{1,0:T(8,128)(2,1)} %bitcast.122), channel_id=1, source_target_pairs={{0,1},{1,0},{2,3},{3,2},{4,5},{5,4},{6,7},{7,6},{8,9},{9,8},{10,11... | collective-permute-start | bytes 1769480 | tf_op jit(solution)/shard_map/ppermute | solution.py:71
  362.4 27.1 %collective-permute-start.24 = (bf16[256,1536]{1,0:T(8,128)(2,1)}, bf16[256,1536]{1,0:T(8,128)(2,1)}, u32[]{:S(2)}, u32[]{:S(2)}) collective-permute-start(bf16[256,1536]{1,0:T(8,128)(2,1)} %shard_map.415.refs_3_), channel_id=1, source_target_pairs={{0,4},{4,0},{1,5},{5,1},{2,6},{6,2},{3,7},{7,3},{8,12},{12,8},{9,1... | collective-permute-start | bytes 2359304 | tf_op jit(solution)/shard_map/ppermute | solution.py:61
  364.0 25.5 %collective-permute-start.27 = (bf16[384,768]{1,0:T(8,128)(2,1)}, bf16[384,768]{1,0:T(8,128)(2,1)S(1)}, u32[]{:S(2)}, u32[]{:S(2)}) collective-permute-start(bf16[384,768]{1,0:T(8,128)(2,1)} %shard_map.413.refs_5_), channel_id=1, source_target_pairs={{0,16},{8,24},{16,0},{24,8},{1,17},{9,25},{17,1},{25,9},{2,18},{10... | collective-permute-start | bytes 1769480 | tf_op jit(solution)/shard_map/ppermute | solution.py:57
  369.4 20.8 %collective-permute-start.28 = (bf16[192,1536]{1,0:T(8,128)(2,1)}, bf16[192,1536]{1,0:T(8,128)(2,1)S(1)}, u32[]{:S(2)}, u32[]{:S(2)}) collective-permute-start(bf16[192,1536]{1,0:T(8,128)(2,1)} %bitcast.115), channel_id=1, source_target_pairs={{0,1},{1,0},{2,3},{3,2},{4,5},{5,4},{6,7},{7,6},{8,9},{9,8},{10,11... | collective-permute-start | bytes 1769480 | tf_op jit(solution)/shard_map/ppermute | solution.py:71
  369.9 19.6 %collective-permute-start.29 = (bf16[96,1536]{1,0:T(8,128)(2,1)}, bf16[96,1536]{1,0:T(8,128)(2,1)}, u32[]{:S(2)}, u32[]{:S(2)}) collective-permute-start(bf16[96,1536]{1,0:T(8,128)(2,1)} %bitcast.132), channel_id=1, source_target_pairs={{0,2},{1,3},{2,0},{3,1},{4,6},{5,7},{6,4},{7,5},{8,10},{9,11},{10,... | collective-permute-start | bytes 884744 | tf_op jit(solution)/shard_map/ppermute | solution.py:71
  398.1 2.6 collective-permute-start.30
  398.2 21.0 %collective-permute-start.35 = (bf16[192,2048]{1,0:T(8,128)(2,1)S(1)}, bf16[192,2048]{1,0:T(8,128)(2,1)S(1)}, u32[]{:S(2)}, u32[]{:S(2)}) collective-permute-start(bf16[192,2048]{1,0:T(8,128)(2,1)S(1)} %copy-done.21), channel_id=1, source_target_pairs={{0,1},{1,0},{2,3},{3,2},{4,5},{5,4},{6,7},{7,6},{8,9},{9,8},{10,11... | collective-permute-start | bytes 2359304 | tf_op jit(solution)/shard_map/ppermute | solution.py:71
  400.8 3.9 collective-permute-start.31
  402.6 21.9 %collective-permute-start.36 = (bf16[160,768]{1,0:T(8,128)(2,1)}, bf16[160,768]{1,0:T(8,128)(2,1)S(1)}, u32[]{:S(2)}, u32[]{:S(2)}) collective-permute-start(bf16[160,768]{1,0:T(8,128)(2,1)} %bitcast.28.refs_7_), channel_id=1, source_target_pairs={{0,1},{1,0},{2,3},{3,2},{4,5},{5,4},{6,7},{7,6},{8,9},{9,8},{10,11... | collective-permute-start | bytes 737288 | tf_op jit(solution)/shard_map/ppermute | solution.py:71
  405.3 47.5 %collective-permute-start.34 = (f32[1,1328]{1,0:T(1,128)S(1)}, f32[1,1328]{1,0:T(1,128)S(1)}, u32[]{:S(2)}, u32[]{:S(2)}) collective-permute-start(f32[1,1328]{1,0:T(1,128)S(1)} %get-tuple-element.245), channel_id=1, source_target_pairs={{0,3},{1,2},{2,1},{3,0},{4,7},{5,6},{6,5},{7,4},{8,11},{9,10},{10,... | collective-permute-start | bytes 15944 | tf_op jit(solution)/shard_map/ppermute | solution.py:71
  407.5 45.3 %collective-permute-start.33 = (f32[1,1328]{1,0:T(1,128)S(1)}, f32[1,1328]{1,0:T(1,128)S(1)}, u32[]{:S(2)}, u32[]{:S(2)}) collective-permute-start(f32[1,1328]{1,0:T(1,128)S(1)} %get-tuple-element.246), channel_id=1, source_target_pairs={{0,2},{1,3},{2,0},{3,1},{4,6},{5,7},{6,4},{7,5},{8,10},{9,11},{10,... | collective-permute-start | bytes 15944 | tf_op jit(solution)/shard_map/ppermute | solution.py:71
  407.9 45.0 %collective-permute-start.32 = (f32[1,1328]{1,0:T(1,128)S(1)}, f32[1,1328]{1,0:T(1,128)S(1)}, u32[]{:S(2)}, u32[]{:S(2)}) collective-permute-start(f32[1,1328]{1,0:T(1,128)S(1)} %get-tuple-element.247), channel_id=1, source_target_pairs={{0,1},{1,0},{2,3},{3,2},{4,5},{5,4},{6,7},{7,6},{8,9},{9,8},{10,11... | collective-permute-start | bytes 15944 | tf_op jit(solution)/shard_map/ppermute | solution.py:71
  423.0 26.6 %collective-permute-start.38 = (bf16[96,2048]{1,0:T(8,128)(2,1)}, bf16[96,2048]{1,0:T(8,128)(2,1)S(1)}, u32[]{:S(2)}, u32[]{:S(2)}) collective-permute-start(bf16[96,2048]{1,0:T(8,128)(2,1)} %bitcast.125), channel_id=1, source_target_pairs={{0,2},{1,3},{2,0},{3,1},{4,6},{5,7},{6,4},{7,5},{8,10},{9,11},{10,... | collective-permute-start | bytes 1179656 | tf_op jit(solution)/shard_map/ppermute | solution.py:71
  431.7 16.1 %collective-permute-start.37 = (bf16[192,768]{1,0:T(8,128)(2,1)}, bf16[192,768]{1,0:T(8,128)(2,1)S(1)}, u32[]{:S(2)}, u32[]{:S(2)}) collective-permute-start(bf16[192,768]{1,0:T(8,128)(2,1)} %get-tuple-element.155.refs_3_), channel_id=1, source_target_pairs={{0,1},{1,0},{2,3},{3,2},{4,5},{5,4},{6,7},{7,6},{8,9},{9,8},{10,11... | collective-permute-start | bytes 884744 | tf_op jit(solution)/shard_map/ppermute | solution.py:71
  447.9 22.5 %collective-permute-start.39 = (bf16[96,1536]{1,0:T(8,128)(2,1)S(1)}, bf16[96,1536]{1,0:T(8,128)(2,1)S(1)}, u32[]{:S(2)}, u32[]{:S(2)}) collective-permute-start(bf16[96,1536]{1,0:T(8,128)(2,1)S(1)} %bitcast.128), channel_id=1, source_target_pairs={{0,2},{1,3},{2,0},{3,1},{4,6},{5,7},{6,4},{7,5},{8,10},{9,11},{10,... | collective-permute-start | bytes 884744 | tf_op jit(solution)/shard_map/ppermute | solution.py:71
  449.6 24.1 %collective-permute-start.40 = (bf16[80,768]{1,0:T(8,128)(2,1)}, bf16[80,768]{1,0:T(8,128)(2,1)S(1)}, u32[]{:S(2)}, u32[]{:S(2)}) collective-permute-start(bf16[80,768]{1,0:T(8,128)(2,1)} %bitcast.135), channel_id=1, source_target_pairs={{0,2},{1,3},{2,0},{3,1},{4,6},{5,7},{6,4},{7,5},{8,10},{9,11},{10,... | collective-permute-start | bytes 368648 | tf_op jit(solution)/shard_map/ppermute | solution.py:71
  456.8 19.8 %collective-permute-start.41 = (bf16[96,768]{1,0:T(8,128)(2,1)}, bf16[96,768]{1,0:T(8,128)(2,1)S(1)}, u32[]{:S(2)}, u32[]{:S(2)}) collective-permute-start(bf16[96,768]{1,0:T(8,128)(2,1)} %bitcast.91), channel_id=1, source_target_pairs={{0,2},{1,3},{2,0},{3,1},{4,6},{5,7},{6,4},{7,5},{8,10},{9,11},{10,... | collective-permute-start | bytes 442376 | tf_op jit(solution)/shard_map/ppermute | solution.py:71
  (48 other events, 338.6 us)
Sparse Core Ops, SparseCore 0:
  11.6 134.7 all-gather.1
  244.7 49.2 reduce-scatter.2
  296.7 59.6 reduce-scatter.4

commit v2 on v1

--- a/solution.py
+++ b/solution.py
@@ -148,14 +148,18 @@
         out_ref[k * w : (k + 1) * w, there] = tn(left, right).astype(LOW)
 
 
-def add_last(keep, got, after):
+def add_last(keep, got, after, widths):
+    ends = [int(e) for e in np.cumsum([0] + widths)]
+    cuts = [slice(i, j) for i, j in zip(ends, ends[1:])]
     if keep.shape[0] % 16:
-        return keep + wide(got)
-
-    def body(keep_ref, got_ref, out_ref):
-        out_ref[...] = keep_ref[...] + got_ref[...].astype(F32)
-
-    return run(body, 1, [keep, got], [new(keep.shape, F32)], after=after)[0]
+        return [(keep + wide(got))[:, cut] for cut in cuts]
+
+    def body(keep_ref, got_ref, *outs):
+        for cut, out_ref in zip(cuts, outs):
+            out_ref[...] = keep_ref[:, cut] + got_ref[:, cut].astype(F32)
+
+    outs = [new((keep.shape[0], n), F32) for n in widths]
+    return list(run(body, 1, [keep, got], outs, after=after))
 
 
 def side_product(pairs_of, side, got=None, after=(), groups=None, others=False):
@@ -350,10 +354,10 @@
         self.bit *= 2
         return self.got
 
-    def finish(self, after=()):
+    def finish(self, after=(), widths=None):
         while self.bit < lax.axis_size(RW):
             self.step(after)
-        return add_last(self.keep, self.got[0], after)
+        return add_last(self.keep, self.got[0], after, widths or [self.keep.shape[1]])
 
 
 class RowSum:
@@ -369,10 +373,10 @@
         self.bit *= 2
         return self.got
 
-    def finish(self, after=()):
+    def finish(self, after=(), widths=None):
         while self.bit < lax.axis_size(RW):
             self.step(after)
-        return add_last(self.keep, self.got[0], after)
+        return add_last(self.keep, self.got[0], after, widths or [self.keep.shape[1]])
 
 
 def scatter_small(parts, after):
@@ -670,7 +674,7 @@
 ):
     spots_ref, normed_ref, out_ref = refs[:3] if fused else (None, None, None)
     outs = refs[3 * fused :]
-    proj_ref, resid_ref, gain_sum_ref, bias_sum_ref, dq_ref, dkv_ref, dwr_ref = outs[:7]
+    proj_ref, resid_ref, gain_sum_ref, bias_sum_ref, dq_ref, dkv_ref, dwr_ref, far_ref = outs[:8]
     attended = outs[-1]
     grad_normed = p_ref[...].astype(F32) + po_ref[...].astype(F32)
     hat, scale = normalize(hidden_ref[...])
@@ -684,11 +688,12 @@
     attend_back_kernel(
         q_ref, kv_ref, wr_ref, basis_ref, probs_ref, attended, dq_ref, dkv_ref, dwr_ref
     )
+    far_ref[...] = dkv_ref[far_ref.shape[0] :]
     if fused:
         kw = dq_ref.shape[1]
-        columns_product(spots_ref, proj_ref, out_ref[...], outs[7], slice(None))
-        columns_product(spots_ref, normed_ref, dq_ref[...], outs[8], slice(0, kw))
-        columns_product(spots_ref, normed_ref, dkv_ref[...], outs[8], slice(kw, None))
+        columns_product(spots_ref, proj_ref, out_ref[...], outs[8], slice(None))
+        columns_product(spots_ref, normed_ref, dq_ref[...], outs[9], slice(0, kw))
+        columns_product(spots_ref, normed_ref, dkv_ref[...], outs[9], slice(kw, None))
 
 
 def point_back_kernel(head_ref, grad_ref, point_ref, mine_ref, send_ref, bias_ref):
@@ -1022,7 +1027,7 @@
         [trans, skip_term, prev, later, grad_mixed, tap0, tap1, tap2],
         [new((2 * width, chan), LOW), new((3, chan), F32)],
     )
-    grad_proj_low, resid, grad_gain_two, grad_bias_two, dq, dkv, grad_rel, *theirs = run(
+    grad_proj_low, resid, grad_gain_two, grad_bias_two, dq, dkv, grad_rel, far, *theirs = run(
         functools.partial(inner_back_kernel, fused),
         1,
         [at_head, partial_two, to_head(partial_two), hidden, grad_ff_low, grad_trans, gain_two]
@@ -1031,6 +1036,7 @@
         [new((width, model), LOW), new((width, chan), F32)]
         + [new((1, model), F32), new((1, model), F32)]
         + [new(queries.shape, LOW), new(kv.shape, LOW), new(w_rel.shape, F32)]
+        + [new((kv.shape[0] // 2, kv.shape[1]), LOW)]
         + [new((core_rows, heads * VAL), LOW), new((core_rows, kw + kv.shape[1]), LOW)][: 2 * fused],
         [pltpu.VMEM((width, heads * VAL), LOW)],
         after=for_skip.send + [mixed],
@@ -1039,7 +1045,7 @@
     summed = []
     while bit < rows:
         n = rest.shape[0] // 2
-        got = to_bit(rest[n:], bit)
+        got = to_bit(far if bit == 1 else rest[n:], bit)
         dkv_parts.append(got[:width])
         arrived.append(got)
         if n > width:
@@ -1055,11 +1061,11 @@
         [(grad_proj_low, attended), (normed_all, dq), (normed_all, dkv)],
         theirs or None,
         [],
-        summed[:1] + skip_across[0],
+        skip_across[0],
         [[0, 1, 2]],
     )
     mixed_full = both_halves(head, mixed, mixed_other)
-    for_point = Scatter([(mixed_full, grad_out)], None, for_attn.send, for_attn.send)
+    for_point = Scatter([(mixed_full, grad_out)], None, [], for_attn.send)
     for_down.step(for_point.theirs)
     attn_across = [for_attn.across(0)]
     for_attn.take(attn_across)
@@ -1076,24 +1082,24 @@
     for_up.step([for_down.sent])
     for_attn.step([for_up.sent])
     for_skip.step([for_attn.sent])
+    for_point.step([for_skip.sent])
     input_grad, grad_gain_one, grad_bias_one = run(
         outer_back_kernel,
         1,
         [at_head, own_blocks[0], other_blocks[0], partial_one, to_head(partial_one)]
         + [gain_one, resid],
         [new((width, chan), F32), new((1, model), F32), new((1, model), F32)],
-        after=[for_skip.sent] + point_across + for_up.got + for_down.got,
+        after=[for_point.sent] + for_up.got + for_down.got,
     )
     input_grad = input_grad[None]
     for_attn.step([grad_gain_one])
     for_up.step([for_attn.sent] + for_skip.got)
     for_point.step([for_up.sent])
     for_skip.step([for_point.sent])
-    for_point.step([for_skip.sent] + for_attn.got)
-    last = [for_point.sent]
-    grad_down, grad_up, grad_skip = (part.finish(last) for part in (for_down, for_up, for_skip))
-    grad_attn, grad_point = for_attn.finish(last), for_point.finish(last)
-    grad_out_w, grad_qkv = grad_attn[:, : heads * VAL], grad_attn[:, heads * VAL :]
+    early = last = [for_skip.sent]
+    (grad_down,), (grad_up,) = for_down.finish(early), for_up.finish(early)
+    (grad_skip,), (grad_point,) = for_skip.finish(last), for_point.finish(last)
+    grad_out_w, *grad_qkv = for_attn.finish(early, [heads * VAL, kw, kw, heads * VAL])
     result = (nn(mixed_full, w_point[0][:, 2 * ff + chan : 2 * ff + 2 * chan]) + b_point).astype(LOW)
     block_output = tn(apart, result).astype(LOW)[None]
     parts = [grad_gain_one, grad_bias_one, grad_gain_two, grad_bias_two, grad_down_bias]
@@ -1124,9 +1130,7 @@
         input_grad,
         own(0, shard),
         own(shard, shard),
-        grad_qkv[:, :kw],
-        grad_qkv[:, kw : 2 * kw],
-        grad_qkv[:, 2 * kw :],
+        *grad_qkv,
         own(at + 5 * small, heads * rel_cols).reshape(heads, rel_cols),
         grad_out_w.T,
         own(2 * shard, shard),

time: 490 us -> 501 us (1.022)
  waiting for transfers between devices: 202 us -> 223 us
    ppermute x18, waiting for transfers between devices: 46.4 us -> 54 us  [to_bit(): return lax.ppermute(a, RW, [(i, i ^ bit) for i in range(n)])]
    ppermute x4, waiting for transfers between devices: 7.68 us -> 12.8 us  [to_pair(): return lax.ppermute(a, IT, [(i, (i + 2 * k) % n) for i in range(n)])]
    unnamed x105 -> x107, local copies, waits for them, and re-layouts: 13.5 us -> 14.5 us
  transfers between devices with their start and end apart: 45 -> 45, of which waited for: 19 -> 16; matrix products, arithmetic and copies ran while one was open for 9% -> 7% of each run, Pallas kernels for 20% -> 20%
where the time goes in v2:
time: 501 us; the launch traced here: 496 us
  waiting for transfers between devices  223 us (45%)
  Pallas kernels  143 us (29%)
  starting transfers between devices  62.6 us (12%)
  local copies, waits for them, and re-layouts  24 us (5%)
  matrix products  15.5 us (3%)
  between operations  14.7 us (3%)
  other arithmetic  13.3 us (3%)
    pallas_call x27, Pallas kernels, run(): pl.pallas_call(kernel, grid=(grid,), in_specs=[spec(shape, index) for _,...  121 us
    all_gather x1, waiting for transfers between devices, shards(): big = lax.all_gather(piece, (IT, RW), axis=0, tiled=True)  83.9 us
    ppermute x18, waiting for transfers between devices, to_bit(): return lax.ppermute(a, RW, [(i, i ^ bit) for i in range(n)])  54 us
    ppermute x11, waiting for transfers between devices, to_head(): return lax.ppermute(a, HD, [(0, 1), (1, 0)])  41.4 us
    ppermute x18, starting transfers between devices, to_bit(): return lax.ppermute(a, RW, [(i, i ^ bit) for i in range(n)])  30.6 us
    ppermute x2, waiting for transfers between devices, from_before(): return lax.ppermute(row, RW, [(i, i + 1) for i in range(n - 1)])  26.3 us
    unnamed x107, local copies, waits for them, and re-layouts  14.5 us
    ppermute x2, starting transfers between devices, from_before(): return lax.ppermute(row, RW, [(i, i + 1) for i in range(n - 1)])  13.7 us
  transfers between devices with their start and end apart: 45, of which 16 were waited for; matrix products, arithmetic and copies ran while one was open for 7% of the time, Pallas kernels for 20%

profile of v2, /device:TPU:0, one launch (start us, length us, event | category | flops | bytes accessed | tf_op | source)
XLA Modules:
  0.0 496.2 jit_solution(567319601238972284)
XLA Ops:
  8.5 3.0 shard_map.401
  11.6 5.1 %collective-permute-start.3 = (bf16[256,768]{1,0:T(8,128)(2,1)S(1)}, bf16[256,768]{1,0:T(8,128)(2,1)S(1)}, u32[]{:S(2)}, u32[]{:S(2)}) collective-permute-start(bf16[256,768]{1,0:T(8,128)(2,1)S(1)} %bitcast.100), channel_id=1, source_target_pairs={{0,3},{1,2},{2,1},{3,0},{4,7},{5,6},{6,5},{7,4},{8,11},{9,10},{10,... | collective-permute-start | bytes 1179656 | tf_op jit(solution)/shard_map/ppermute | solution.py:71
  19.2 3.1 collective-permute-start.7
  23.0 3.8 convolution_convert_fusion.refs_13_
  27.4 25.6 %collective-permute-done.7 = bf16[1,768]{1,0:T(2,128)(2,1)S(1)} collective-permute-done((bf16[1,768]{1,0:T(2,128)(2,1)S(1)}, bf16[1,768]{1,0:T(2,128)(2,1)S(1)}, u32[]{:S(2)}, u32[]{:S(2)}) %collective-permute-start.7) | collective-permute-done | bytes 1568 | tf_op jit(solution)/shard_map/ppermute | solution.py:830
  56.7 2.1 collective-permute-done.1.refs_2_
  62.5 83.9 %all-gather.2.cloned.1.call-done.refs_0_.refs_11_.refs_12_.refs_4_.refs_9_.refs_10_.refs_2_.refs_5_.refs_7_.refs_3_ = bf16[1536,6656]{1,0:T(8,128)(2,1)} async-done(((bf16[96,6656]{1,0:T(8,128)(2,1)}), bf16[1536,6656]{1,0:T(8,128)(2,1)}) %all-gather.2.cloned.1.call-update) | async-done | bytes 20447248 | tf_op jit(solution)/shard_map/all_gather | solution.py:899
  146.4 3.3 shard_map.402
  150.7 9.8 %shard_map.403 = (bf16[256,256]{1,0:T(8,128)(2,1)}, bf16[1024,1024]{1,0:T(8,128)(2,1)}, bf16[1024,1536]{1,0:T(8,128)(2,1)}) custom-call(s32[1]{0:T(128)} %bitcast.refs_0_, bf16[256,768]{1,0:T(8,128)(2,1)} %bitcast.97, bf16[256,768]{1,0:T(8,128)(2,1)} %collective-permute-done.1.refs_2_, bf16[256,768]{1,0:T(8,128)(2,1)} %copy-done.28, ...), custom_call_target="tpu_custom_call" | custom-call | flops 1 | bytes 1 | tf_op jit(solution)/shard_map/pallas_call | solution.py:489
  160.5 9.5 %shard_map.404 = (bf16[256,768]{1,0:T(8,128)(2,1)}, bf16[4,256,1024]{2,1,0:T(8,128)(2,1)}, bf16[256,1536]{1,0:T(8,128)(2,1)}) custom-call(bf16[256,256]{1,0:T(8,128)(2,1)} %get-tuple-element.99.refs_0_.refs_8_, bf16[1024,1024]{1,0:T(8,128)(2,1)} %get-tuple-element.100.refs_1_.refs_9_, f32[128,64]{1,0:T(8,128)} %get-tuple-element.101.refs_2_.refs_10_, ...), custom_call_target="tpu_custom_call" | custom-call | flops 1 | bytes 1 | tf_op jit(solution)/shard_map/pallas_call | solution.py:489
  171.5 4.9 shard_map.406
  176.9 4.3 convolution_add_fusion.refs_11_.refs_1_
  181.3 9.4 %collective-permute-done.9.refs_4_ = bf16[256,1536]{1,0:T(8,128)(2,1)S(1)} collective-permute-done((bf16[256,1536]{1,0:T(8,128)(2,1)}, bf16[256,1536]{1,0:T(8,128)(2,1)S(1)}, u32[]{:S(2)}, u32[]{:S(2)}) %collective-permute-start.9) | collective-permute-done | bytes 786464 | tf_op jit(solution)/shard_map/ppermute | solution.py:61
  191.6 10.9 %shard_map.405 = (f32[256,1536]{1,0:T(8,128)}, bf16[256,1536]{1,0:T(8,128)(2,1)}, bf16[256,1536]{1,0:T(8,128)(2,1)}, bf16[256,1536]{1,0:T(8,128)(2,1)}, f32[256,768]{1,0:T(8,128)}, /*index=5*/bf16[256,768]{1,0:T(8,128)(2,1)}) custom-call(s32[1]{0:T(128)} %bitcast.refs_0_, bf16[256,768]{1,0:T(8,128)(2,1)} %bitcast.98, bf16[256,768]{1,0:T(8,128)(2,1)} %copy-done.6, ...), custom_call_target="tpu_custom_call" | custom-call | flops 1 | bytes 1 | tf_op jit(solution)/shard_map/pallas_call | solution.py:489
  207.0 3.7 shard_map.407
  211.6 2.6 reduce-precision_convert_fusion.2
  217.8 10.6 %collective-permute-start.11 = (bf16[1,768]{1,0:T(2,128)(2,1)S(1)}, bf16[1,768]{1,0:T(2,128)(2,1)S(1)}, u32[]{:S(2)}, u32[]{:S(2)}) collective-permute-start(bf16[1,768]{1,0:T(2,128)(2,1)S(1)} %get-tuple-element.238), channel_id=1, source_target_pairs={{0,1},{1,2},{2,3},{4,5},{5,6},{6,7},{8,9},{9,10},{10,11},{12,13},{... | collective-permute-start | bytes 4616 | tf_op jit(solution)/shard_map/ppermute | solution.py:830
  231.0 13.6 %shard_map.409 = (bf16[256,1536]{1,0:T(8,128)(2,1)}, bf16[256,1536]{1,0:T(8,128)(2,1)}, bf16[256,1536]{1,0:T(8,128)(2,1)}, f32[1,1536]{1,0:T(1,128)}, f32[1,1536...) custom-call(s32[1]{0:T(128)} %bitcast.refs_0_, bf16[256,768]{1,0:T(8,128)(2,1)} %copy-done.14, ...), custom_call_target="tpu_custom_call" | custom-call | flops 1 | bytes 1 | tf_op jit(solution)/shard_map/pallas_call | solution.py:489
  248.8 4.1 shard_map.408
  255.0 12.5 %collective-permute-done.16.refs_2_ = bf16[256,1536]{1,0:T(8,128)(2,1)S(1)} collective-permute-done((bf16[256,1536]{1,0:T(8,128)(2,1)S(1)}, bf16[256,1536]{1,0:T(8,128)(2,1)S(1)}, u32[]{:S(2)}, u32[]{:S(2)}) %collective-permute-start.16) | collective-permute-done | bytes 786464 | tf_op jit(solution)/shard_map/ppermute | solution.py:61
  268.4 18.1 %shard_map.410 = (bf16[256,1536]{1,0:T(8,128)(2,1)}, f32[256,768]{1,0:T(8,128)}, f32[1,1536]{1,0:T(1,128)}, f32[1,1536]{1,0:T(1,128)}, bf16[256,256]{1,0:T(8,128...) custom-call(s32[1]{0:T(128)} %bitcast.refs_0_, ...), custom_call_target="tpu_custom_call" | custom-call | flops 1 | bytes 1 | tf_op jit(solution)/shard_map/pallas_call | solution.py:489
  287.0 2.3 collective-permute-start.18
  290.1 16.5 %collective-permute-done.14 = bf16[512,768]{1,0:T(8,128)(2,1)} collective-permute-done((bf16[512,768]{1,0:T(8,128)(2,1)S(1)}, bf16[512,768]{1,0:T(8,128)(2,1)}, u32[]{:S(2)}, u32[]{:S(2)}) %collective-permute-start.14) | collective-permute-done | bytes 786464 | tf_op jit(solution)/shard_map/ppermute | solution.py:61
  309.6 4.0 shard_map.411.refs_2_
  316.4 5.2 %shard_map.412.refs_3_ = bf16[384,2048]{1,0:T(8,128)(2,1)} custom-call(s32[1]{0:T(128)} %bitcast.15.spot_ref, bf16[256,1536]{1,0:T(8,128)(2,1)} %get-tuple-element.133.refs_0_, bf16[1024,1536]{1,0:T(8,128)(2,1)} %get-tuple-element.127.refs_14_.refs_1_.refs_2_, bf16[1024,1536]{1,0:T(8,128)(2,1)} %get-tuple-element.127.refs_14_.refs_1_.refs_2_, ...), custom_call_target="tpu_custom_call" | custom-call | flops 1 | bytes 1 | tf_op jit(solution)/shard_map/pallas_call | solution.py:235
  323.3 3.7 collective-permute-start.19
  327.0 2.3 shard_map.414
  332.4 2.8 shard_map.413.refs_5_
  335.2 15.5 %collective-permute-done.19.refs_2_ = bf16[256,1024]{1,0:T(8,128)(2,1)S(1)} collective-permute-done((bf16[256,1024]{1,0:T(8,128)(2,1)S(1)}, bf16[256,1024]{1,0:T(8,128)(2,1)S(1)}, u32[]{:S(2)}, u32[]{:S(2)}) %collective-permute-start.19) | collective-permute-done | bytes 524320 | tf_op jit(solution)/shard_map/ppermute | solution.py:71
  351.5 4.7 shard_map.415.refs_3_
  357.8 2.4 shard_map.416
  360.2 3.5 reduce-scatter.5.cloned.1.call-done
  363.7 2.3 shard_map.417
  369.5 8.0 %collective-permute-done.26.refs_8_ = bf16[384,2048]{1,0:T(8,128)(2,1)} collective-permute-done((bf16[384,2048]{1,0:T(8,128)(2,1)}, bf16[384,2048]{1,0:T(8,128)(2,1)}, u32[]{:S(2)}, u32[]{:S(2)}) %collective-permute-start.26) | collective-permute-done | bytes 1572896 | tf_op jit(solution)/shard_map/ppermute | solution.py:57
  377.5 6.6 %shard_map.418 = (f32[192,2048]{1,0:T(8,128)}, bf16[192,2048]{1,0:T(8,128)(2,1)}) custom-call(s32[2]{0:T(128)} %pad_add_fusion.2.at_ref, bf16[256,1536]{1,0:T(8,128)(2,1)} %get-tuple-element.133.refs_0_, bf16[1024,1536]{1,0:T(8,128)(2,1)} %get-tuple-element.127.refs_14_.refs_1_.refs_2_, bf16[1024,1536]{1,0:T(8,128)(2,1)} %get-tuple-element.127.refs_14_.refs_1_.refs_2_, ...), custom_call_target="tpu_custom_call" | custom-call | flops 1 | bytes 1 | tf_op jit(solution)/shard_map/pallas_call | solution.py:293
  384.1 2.1 shard_map.419
  386.2 3.7 collective-permute-done.25.refs_3_
  390.0 4.0 shard_map.420
  395.1 4.1 shard_map.421
  408.4 3.0 collective-permute-start.34
  411.4 11.7 %collective-permute-done.37 = bf16[192,2048]{1,0:T(8,128)(2,1)S(1)} collective-permute-done((bf16[192,2048]{1,0:T(8,128)(2,1)}, bf16[192,2048]{1,0:T(8,128)(2,1)S(1)}, u32[]{:S(2)}, u32[]{:S(2)}) %collective-permute-start.37) | collective-permute-done | bytes 786464 | tf_op jit(solution)/shard_map/ppermute | solution.py:71
  424.4 5.0 %fusion.16 = bf16[1,512,768]{2,1,0:T(8,128)(2,1)} fusion(bf16[1536,6656]{1,0:T(8,128)(2,1)} %all-gather.2.cloned.1.call-done.refs_0_.refs_11_.refs_12_.refs_4_.refs_9_.refs_10_.refs_2_.refs_5_.refs_7_.refs_3_, f32[768]{0:T(1024)S(1)} %reduce.2, pred[256,512]{1,0:T(32,128)(4,1)S(1)} %copy-done.39, pred[256,512]{1,0:T(32,128)(4,1)} %copy-done.40, ...), kind=kOutput, calls=%fused_computation.28 | convolution fusion | flops 1615200256 | bytes 4983808 | tf_op jit(solution)/shard_map/dot_general | solution.py:31
  429.5 2.8 shard_map.423
  432.9 2.4 shard_map.424
  435.4 2.5 collective-permute-start.39
  442.1 2.6 collective-permute-start.38
  454.3 24.7 %collective-permute-done.40.refs_1_ = bf16[80,768]{1,0:T(8,128)(2,1)S(1)} collective-permute-done((bf16[80,768]{1,0:T(8,128)(2,1)}, bf16[80,768]{1,0:T(8,128)(2,1)S(1)}, u32[]{:S(2)}, u32[]{:S(2)}) %collective-permute-start.40) | collective-permute-done | bytes 122912 | tf_op jit(solution)/shard_map/ppermute | solution.py:71
  487.3 2.1 shard_map.428
  (232 shorter events, 87.1 us)
Async XLA Ops:
  7.2 139.2 %all-gather.2.cloned.1.call-start = ((), (), s32[]{:S(2)}) async-start(), calls=%async_computation.2 | async-start | bytes 21725184 | tf_op jit(solution)/shard_map/all_gather | solution.py:899
  11.5 315.5 %reduce-scatter.3.cloned.1.call-start = ((), (), s32[]{:S(2)}) async-start(), calls=%async_computation.3 | async-start | bytes 5898240 | tf_op jit(solution)/shard_map/reduce_scatter | solution.py:1022
  11.6 43.0 %collective-permute-start.3 = (bf16[256,768]{1,0:T(8,128)(2,1)S(1)}, bf16[256,768]{1,0:T(8,128)(2,1)S(1)}, u32[]{:S(2)}, u32[]{:S(2)}) collective-permute-start(bf16[256,768]{1,0:T(8,128)(2,1)S(1)} %bitcast.100), channel_id=1, source_target_pairs={{0,3},{1,2},{2,1},{3,0},{4,7},{5,6},{6,5},{7,4},{8,11},{9,10},{10,... | collective-permute-start | bytes 1179656 | tf_op jit(solution)/shard_map/ppermute | solution.py:71
  16.7 39.3 %collective-permute-start.2 = (bf16[256,768]{1,0:T(8,128)(2,1)S(1)}, bf16[256,768]{1,0:T(8,128)(2,1)S(1)}, u32[]{:S(2)}, u32[]{:S(2)}) collective-permute-start(bf16[256,768]{1,0:T(8,128)(2,1)S(1)} %bitcast.101), channel_id=1, source_target_pairs={{0,1},{1,0},{2,3},{3,2},{4,5},{5,4},{6,7},{7,6},{8,9},{9,8},{10,11... | collective-permute-start | bytes 1179656 | tf_op jit(solution)/shard_map/ppermute | solution.py:71
  16.7 42.1 %collective-permute-start.1 = (bf16[256,768]{1,0:T(8,128)(2,1)S(1)}, bf16[256,768]{1,0:T(8,128)(2,1)}, u32[]{:S(2)}, u32[]{:S(2)}) collective-permute-start(bf16[256,768]{1,0:T(8,128)(2,1)S(1)} %bitcast.102), channel_id=1, source_target_pairs={{0,2},{1,3},{2,0},{3,1},{4,6},{5,7},{6,4},{7,5},{8,10},{9,11},{10,... | collective-permute-start | bytes 1179656 | tf_op jit(solution)/shard_map/ppermute | solution.py:71
  17.3 132.4 %collective-permute-start = (bf16[256,768]{1,0:T(8,128)(2,1)S(1)}, bf16[256,768]{1,0:T(8,128)(2,1)S(1)}, u32[]{:S(2)}, u32[]{:S(2)}) collective-permute-start(bf16[256,768]{1,0:T(8,128)(2,1)S(1)} %bitcast.103), channel_id=1, source_target_pairs={{0,4},{4,0},{1,5},{5,1},{2,6},{6,2},{3,7},{7,3},{8,12},{12,8},{9,1... | collective-permute-start | bytes 1179656 | tf_op jit(solution)/shard_map/ppermute | solution.py:61
  19.2 33.8 %collective-permute-start.7 = (bf16[1,768]{1,0:T(2,128)(2,1)S(1)}, bf16[1,768]{1,0:T(2,128)(2,1)S(1)}, u32[]{:S(2)}, u32[]{:S(2)}) collective-permute-start(bf16[1,768]{1,0:T(2,128)(2,1)S(1)} %get-tuple-element.249), channel_id=1, source_target_pairs={{0,1},{1,2},{2,3},{4,5},{5,6},{6,7},{8,9},{9,10},{10,11},{12,13},{... | collective-permute-start | bytes 4616 | tf_op jit(solution)/shard_map/ppermute | solution.py:830
  27.4 122.3 %copy-start.1 = (bf16[512,768]{1,0:T(8,128)(2,1)}, bf16[512,768]{1,0:T(8,128)(2,1)S(1)}, u32[]{:S(2)}) copy-start(bf16[512,768]{1,0:T(8,128)(2,1)S(1)} %convolution_convert_fusion.2.refs_1_) | copy-start | bytes 2359300
  53.0 8.4 %collective-permute-start.8 = (bf16[1,768]{1,0:T(2,128)(2,1)S(1)}, bf16[1,768]{1,0:T(2,128)(2,1)S(1)}, u32[]{:S(2)}, u32[]{:S(2)}) collective-permute-start(bf16[1,768]{1,0:T(2,128)(2,1)S(1)} %get-tuple-element.250), channel_id=1, source_target_pairs={{1,0},{2,1},{3,2},{5,4},{6,5},{7,6},{9,8},{10,9},{11,10},{13,12},{... | collective-permute-start | bytes 4616 | tf_op jit(solution)/shard_map/ppermute | solution.py:835
  54.6 95.2 %copy-start.27 = (bf16[256,768]{1,0:T(8,128)(2,1)}, bf16[256,768]{1,0:T(8,128)(2,1)S(1)}, u32[]{:S(2)}) copy-start(bf16[256,768]{1,0:T(8,128)(2,1)S(1)} %collective-permute-done.3.refs_4_) | copy-start | bytes 1179652
  54.6 95.2 %collective-permute-start.6 = (bf16[256,768]{1,0:T(8,128)(2,1)S(1)}, bf16[256,768]{1,0:T(8,128)(2,1)S(1)}, u32[]{:S(2)}, u32[]{:S(2)}) collective-permute-start(bf16[256,768]{1,0:T(8,128)(2,1)S(1)} %collective-permute-done.3.refs_4_), channel_id=1, source_target_pairs={{0,4},{4,0},{1,5},{5,1},{2,6},{6,2},{3,7},{7,3},{8,12},{12,8},{9,1... | collective-permute-start | bytes 1179656 | tf_op jit(solution)/shard_map/ppermute | solution.py:61
  56.0 93.7 %copy-start.28 = (bf16[256,768]{1,0:T(8,128)(2,1)}, bf16[256,768]{1,0:T(8,128)(2,1)S(1)}, u32[]{:S(2)}) copy-start(bf16[256,768]{1,0:T(8,128)(2,1)S(1)} %collective-permute-done.2.refs_3_) | copy-start | bytes 1179652
  56.0 93.8 %collective-permute-start.5 = (bf16[256,768]{1,0:T(8,128)(2,1)S(1)}, bf16[256,768]{1,0:T(8,128)(2,1)S(1)}, u32[]{:S(2)}, u32[]{:S(2)}) collective-permute-start(bf16[256,768]{1,0:T(8,128)(2,1)S(1)} %collective-permute-done.2.refs_3_), channel_id=1, source_target_pairs={{0,4},{4,0},{1,5},{5,1},{2,6},{6,2},{3,7},{7,3},{8,12},{12,8},{9,1... | collective-permute-start | bytes 1179656 | tf_op jit(solution)/shard_map/ppermute | solution.py:61
  58.8 91.0 %collective-permute-start.4 = (bf16[256,768]{1,0:T(8,128)(2,1)}, bf16[256,768]{1,0:T(8,128)(2,1)}, u32[]{:S(2)}, u32[]{:S(2)}) collective-permute-start(bf16[256,768]{1,0:T(8,128)(2,1)} %collective-permute-done.1.refs_2_), channel_id=1, source_target_pairs={{0,4},{4,0},{1,5},{5,1},{2,6},{6,2},{3,7},{7,3},{8,12},{12,8},{9,1... | collective-permute-start | bytes 1179656 | tf_op jit(solution)/shard_map/ppermute | solution.py:61
  170.0 20.7 %collective-permute-start.9 = (bf16[256,1536]{1,0:T(8,128)(2,1)}, bf16[256,1536]{1,0:T(8,128)(2,1)S(1)}, u32[]{:S(2)}, u32[]{:S(2)}) collective-permute-start(bf16[256,1536]{1,0:T(8,128)(2,1)} %get-tuple-element.102.refs_3_), channel_id=1, source_target_pairs={{0,4},{4,0},{1,5},{5,1},{2,6},{6,2},{3,7},{7,3},{8,12},{12,8},{9,1... | collective-permute-start | bytes 2359304 | tf_op jit(solution)/shard_map/ppermute | solution.py:61
  176.4 29.7 %collective-permute-start.13 = (bf16[528,768]{1,0:T(8,128)(2,1)}, bf16[528,768]{1,0:T(8,128)(2,1)S(1)}, u32[]{:S(2)}, u32[]{:S(2)}) collective-permute-start(bf16[528,768]{1,0:T(8,128)(2,1)} %get-tuple-element.112), channel_id=1, source_target_pairs={{0,4},{4,0},{1,5},{5,1},{2,6},{6,2},{3,7},{7,3},{8,12},{12,8},{9,1... | collective-permute-start | bytes 2433032 | tf_op jit(solution)/shard_map/ppermute | solution.py:61
  202.5 9.1 %collective-permute-start.10 = (bf16[256,768]{1,0:T(8,128)(2,1)}, bf16[256,768]{1,0:T(8,128)(2,1)S(1)}, u32[]{:S(2)}, u32[]{:S(2)}) collective-permute-start(bf16[256,768]{1,0:T(8,128)(2,1)} %get-tuple-element.110), channel_id=1, source_target_pairs={{0,4},{4,0},{1,5},{5,1},{2,6},{6,2},{3,7},{7,3},{8,12},{12,8},{9,1... | collective-permute-start | bytes 1179656 | tf_op jit(solution)/shard_map/ppermute | solution.py:61
  214.2 16.1 %collective-permute-start.15 = (bf16[256,768]{1,0:T(8,128)(2,1)S(1)}, bf16[256,768]{1,0:T(8,128)(2,1)S(1)}, u32[]{:S(2)}, u32[]{:S(2)}) collective-permute-start(bf16[256,768]{1,0:T(8,128)(2,1)S(1)} %get-tuple-element.234.refs_1_), channel_id=1, source_target_pairs={{0,4},{4,0},{1,5},{5,1},{2,6},{6,2},{3,7},{7,3},{8,12},{12,8},{9,1... | collective-permute-start | bytes 1179656 | tf_op jit(solution)/shard_map/ppermute | solution.py:61
  216.5 11.9 %collective-permute-start.12 = (bf16[1,768]{1,0:T(2,128)(2,1)S(1)}, bf16[1,768]{1,0:T(2,128)(2,1)S(1)}, u32[]{:S(2)}, u32[]{:S(2)}) collective-permute-start(bf16[1,768]{1,0:T(2,128)(2,1)S(1)} %get-tuple-element.237), channel_id=1, source_target_pairs={{1,0},{2,1},{3,2},{5,4},{6,5},{7,6},{9,8},{10,9},{11,10},{13,12},{... | collective-permute-start | bytes 4616 | tf_op jit(solution)/shard_map/ppermute | solution.py:835
  217.8 11.9 %collective-permute-start.11 = (bf16[1,768]{1,0:T(2,128)(2,1)S(1)}, bf16[1,768]{1,0:T(2,128)(2,1)S(1)}, u32[]{:S(2)}, u32[]{:S(2)}) collective-permute-start(bf16[1,768]{1,0:T(2,128)(2,1)S(1)} %get-tuple-element.238), channel_id=1, source_target_pairs={{0,1},{1,2},{2,3},{4,5},{5,6},{6,7},{8,9},{9,10},{10,11},{12,13},{... | collective-permute-start | bytes 4616 | tf_op jit(solution)/shard_map/ppermute | solution.py:830
  244.7 119.0 %reduce-scatter.5.cloned.1.call-start = ((), (), s32[]{:S(2)}) async-start(), calls=%async_computation.4 | async-start | bytes 5898240 | tf_op jit(solution)/shard_map/reduce_scatter | solution.py:1022
  247.5 5.4 %collective-permute-start.17 = (bf16[640,768]{1,0:T(8,128)(2,1)S(1)}, bf16[640,768]{1,0:T(8,128)(2,1)S(1)}, u32[]{:S(2)}, u32[]{:S(2)}) collective-permute-start(bf16[640,768]{1,0:T(8,128)(2,1)S(1)} %reduce-precision_convert_fusion.1), channel_id=1, source_target_pairs={{0,8},{8,0},{16,24},{24,16},{1,9},{9,1},{17,25},{25,17},{2,10},{10... | collective-permute-start | bytes 2949128 | tf_op jit(solution)/shard_map/ppermute | solution.py:52
  247.7 19.8 %collective-permute-start.16 = (bf16[256,1536]{1,0:T(8,128)(2,1)S(1)}, bf16[256,1536]{1,0:T(8,128)(2,1)S(1)}, u32[]{:S(2)}, u32[]{:S(2)}) collective-permute-start(bf16[256,1536]{1,0:T(8,128)(2,1)S(1)} %copy-done.23), channel_id=1, source_target_pairs={{0,4},{4,0},{1,5},{5,1},{2,6},{6,2},{3,7},{7,3},{8,12},{12,8},{9,1... | collective-permute-start | bytes 2359304 | tf_op jit(solution)/shard_map/ppermute | solution.py:61
  286.5 28.7 %collective-permute-start.22 = (bf16[768,1280]{1,0:T(8,128)(2,1)}, bf16[768,1280]{1,0:T(8,128)(2,1)}, u32[]{:S(2)}, u32[]{:S(2)}) collective-permute-start(bf16[768,1280]{1,0:T(8,128)(2,1)} %get-tuple-element.135), channel_id=1, source_target_pairs={{0,8},{8,0},{16,24},{24,16},{1,9},{9,1},{17,25},{25,17},{2,10},{10... | collective-permute-start | bytes 5898248 | tf_op jit(solution)/shard_map/ppermute | solution.py:52
  286.5 20.1 %collective-permute-start.14 = (bf16[512,768]{1,0:T(8,128)(2,1)S(1)}, bf16[512,768]{1,0:T(8,128)(2,1)}, u32[]{:S(2)}, u32[]{:S(2)}) collective-permute-start(bf16[512,768]{1,0:T(8,128)(2,1)S(1)} %copy-done.10), channel_id=1, source_target_pairs={{0,4},{4,0},{1,5},{5,1},{2,6},{6,2},{3,7},{7,3},{8,12},{12,8},{9,1... | collective-permute-start | bytes 2359304 | tf_op jit(solution)/shard_map/ppermute | solution.py:61
  287.0 26.5 %collective-permute-start.18 = (bf16[512,1024]{1,0:T(8,128)(2,1)}, bf16[512,1024]{1,0:T(8,128)(2,1)}, u32[]{:S(2)}, u32[]{:S(2)}) collective-permute-start(bf16[512,1024]{1,0:T(8,128)(2,1)} %get-tuple-element.132), channel_id=1, source_target_pairs={{0,1},{1,0},{2,3},{3,2},{4,5},{5,4},{6,7},{7,6},{8,9},{9,8},{10,11... | collective-permute-start | bytes 3145736 | tf_op jit(solution)/shard_map/ppermute | solution.py:71
  289.3 25.9 %collective-permute-start.21 = (bf16[768,768]{1,0:T(8,128)(2,1)}, bf16[768,768]{1,0:T(8,128)(2,1)S(1)}, u32[]{:S(2)}, u32[]{:S(2)}) collective-permute-start(bf16[768,768]{1,0:T(8,128)(2,1)} %get-tuple-element.134), channel_id=1, source_target_pairs={{0,8},{8,0},{16,24},{24,16},{1,9},{9,1},{17,25},{25,17},{2,10},{10... | collective-permute-start | bytes 3538952 | tf_op jit(solution)/shard_map/ppermute | solution.py:52
  289.3 25.8 %collective-permute-start.23 = (bf16[320,768]{1,0:T(8,128)(2,1)}, bf16[320,768]{1,0:T(8,128)(2,1)S(1)}, u32[]{:S(2)}, u32[]{:S(2)}) collective-permute-start(bf16[320,768]{1,0:T(8,128)(2,1)} %get-tuple-element.240.refs_16_), channel_id=1, source_target_pairs={{0,16},{8,24},{16,0},{24,8},{1,17},{9,25},{17,1},{25,9},{2,18},{10... | collective-permute-start | bytes 1474568 | tf_op jit(solution)/shard_map/ppermute | solution.py:57
  313.5 17.9 %collective-permute-start.20 = (bf16[768,768]{1,0:T(8,128)(2,1)}, bf16[768,768]{1,0:T(8,128)(2,1)S(1)}, u32[]{:S(2)}, u32[]{:S(2)}) collective-permute-start(bf16[768,768]{1,0:T(8,128)(2,1)} %shard_map.411.refs_2_), channel_id=1, source_target_pairs={{0,8},{8,0},{16,24},{24,16},{1,9},{9,1},{17,25},{25,17},{2,10},{10... | collective-permute-start | bytes 3538952 | tf_op jit(solution)/shard_map/ppermute | solution.py:52
  321.6 55.9 %collective-permute-start.26 = (bf16[384,2048]{1,0:T(8,128)(2,1)}, bf16[384,2048]{1,0:T(8,128)(2,1)}, u32[]{:S(2)}, u32[]{:S(2)}) collective-permute-start(bf16[384,2048]{1,0:T(8,128)(2,1)} %shard_map.412.refs_3_), channel_id=1, source_target_pairs={{0,16},{8,24},{16,0},{24,8},{1,17},{9,25},{17,1},{25,9},{2,18},{10... | collective-permute-start | bytes 4718600 | tf_op jit(solution)/shard_map/ppermute | solution.py:57
  323.3 27.3 %collective-permute-start.19 = (bf16[256,1024]{1,0:T(8,128)(2,1)S(1)}, bf16[256,1024]{1,0:T(8,128)(2,1)S(1)}, u32[]{:S(2)}, u32[]{:S(2)}) collective-permute-start(bf16[256,1024]{1,0:T(8,128)(2,1)S(1)} %get-tuple-element.247), channel_id=1, source_target_pairs={{0,2},{1,3},{2,0},{3,1},{4,6},{5,7},{6,4},{7,5},{8,10},{9,11},{10,... | collective-permute-start | bytes 1572872 | tf_op jit(solution)/shard_map/ppermute | solution.py:71
  329.4 28.4 %collective-permute-start.27 = (bf16[192,1536]{1,0:T(8,128)(2,1)}, bf16[192,1536]{1,0:T(8,128)(2,1)}, u32[]{:S(2)}, u32[]{:S(2)}) collective-permute-start(bf16[192,1536]{1,0:T(8,128)(2,1)} %bitcast.121), channel_id=1, source_target_pairs={{0,1},{1,0},{2,3},{3,2},{4,5},{5,4},{6,7},{7,6},{8,9},{9,8},{10,11... | collective-permute-start | bytes 1769480 | tf_op jit(solution)/shard_map/ppermute | solution.py:71
  356.2 37.8 %collective-permute-start.24 = (bf16[256,1536]{1,0:T(8,128)(2,1)}, bf16[256,1536]{1,0:T(8,128)(2,1)S(1)}, u32[]{:S(2)}, u32[]{:S(2)}) collective-permute-start(bf16[256,1536]{1,0:T(8,128)(2,1)} %shard_map.415.refs_3_), channel_id=1, source_target_pairs={{0,4},{4,0},{1,5},{5,1},{2,6},{6,2},{3,7},{7,3},{8,12},{12,8},{9,1... | collective-permute-start | bytes 2359304 | tf_op jit(solution)/shard_map/ppermute | solution.py:61
  357.0 32.9 %collective-permute-start.25 = (bf16[384,768]{1,0:T(8,128)(2,1)S(1)}, bf16[384,768]{1,0:T(8,128)(2,1)}, u32[]{:S(2)}, u32[]{:S(2)}) collective-permute-start(bf16[384,768]{1,0:T(8,128)(2,1)S(1)} %copy-done.12), channel_id=1, source_target_pairs={{0,16},{8,24},{16,0},{24,8},{1,17},{9,25},{17,1},{25,9},{2,18},{10... | collective-permute-start | bytes 1769480 | tf_op jit(solution)/shard_map/ppermute | solution.py:57
  366.1 27.9 %collective-permute-start.28 = (bf16[192,1536]{1,0:T(8,128)(2,1)}, bf16[192,1536]{1,0:T(8,128)(2,1)S(1)}, u32[]{:S(2)}, u32[]{:S(2)}) collective-permute-start(bf16[192,1536]{1,0:T(8,128)(2,1)} %bitcast.114), channel_id=1, source_target_pairs={{0,1},{1,0},{2,3},{3,2},{4,5},{5,4},{6,7},{7,6},{8,9},{9,8},{10,11... | collective-permute-start | bytes 1769480 | tf_op jit(solution)/shard_map/ppermute | solution.py:71
  366.9 27.0 %collective-permute-start.29 = (bf16[96,1536]{1,0:T(8,128)(2,1)}, bf16[96,1536]{1,0:T(8,128)(2,1)S(1)}, u32[]{:S(2)}, u32[]{:S(2)}) collective-permute-start(bf16[96,1536]{1,0:T(8,128)(2,1)} %bitcast.130), channel_id=1, source_target_pairs={{0,2},{1,3},{2,0},{3,1},{4,6},{5,7},{6,4},{7,5},{8,10},{9,11},{10,... | collective-permute-start | bytes 884744 | tf_op jit(solution)/shard_map/ppermute | solution.py:71
  402.2 1.6 collective-permute-start.30
  402.3 20.7 %collective-permute-start.37 = (bf16[192,2048]{1,0:T(8,128)(2,1)}, bf16[192,2048]{1,0:T(8,128)(2,1)S(1)}, u32[]{:S(2)}, u32[]{:S(2)}) collective-permute-start(bf16[192,2048]{1,0:T(8,128)(2,1)} %get-tuple-element.143.refs_3_), channel_id=1, source_target_pairs={{0,1},{1,0},{2,3},{3,2},{4,5},{5,4},{6,7},{7,6},{8,9},{9,8},{10,11... | collective-permute-start | bytes 2359304 | tf_op jit(solution)/shard_map/ppermute | solution.py:71
  403.9 3.9 collective-permute-start.31
  404.6 27.7 %collective-permute-start.35 = (bf16[160,768]{1,0:T(8,128)(2,1)S(1)}, bf16[160,768]{1,0:T(8,128)(2,1)S(1)}, u32[]{:S(2)}, u32[]{:S(2)}) collective-permute-start(bf16[160,768]{1,0:T(8,128)(2,1)S(1)} %bitcast.133), channel_id=1, source_target_pairs={{0,1},{1,0},{2,3},{3,2},{4,5},{5,4},{6,7},{7,6},{8,9},{9,8},{10,11... | collective-permute-start | bytes 737288 | tf_op jit(solution)/shard_map/ppermute | solution.py:71
  405.8 32.1 %collective-permute-start.36 = (bf16[192,768]{1,0:T(8,128)(2,1)S(1)}, bf16[192,768]{1,0:T(8,128)(2,1)}, u32[]{:S(2)}, u32[]{:S(2)}) collective-permute-start(bf16[192,768]{1,0:T(8,128)(2,1)S(1)} %copy-done.34), channel_id=1, source_target_pairs={{0,1},{1,0},{2,3},{3,2},{4,5},{5,4},{6,7},{7,6},{8,9},{9,8},{10,11... | collective-permute-start | bytes 884744 | tf_op jit(solution)/shard_map/ppermute | solution.py:71
  408.4 33.7 %collective-permute-start.34 = (f32[1,1328]{1,0:T(1,128)S(1)}, f32[1,1328]{1,0:T(1,128)S(1)}, u32[]{:S(2)}, u32[]{:S(2)}) collective-permute-start(f32[1,1328]{1,0:T(1,128)S(1)} %get-tuple-element.251), channel_id=1, source_target_pairs={{0,3},{1,2},{2,1},{3,0},{4,7},{5,6},{6,5},{7,4},{8,11},{9,10},{10,... | collective-permute-start | bytes 15944 | tf_op jit(solution)/shard_map/ppermute | solution.py:71
  411.4 33.3 %collective-permute-start.33 = (f32[1,1328]{1,0:T(1,128)S(1)}, f32[1,1328]{1,0:T(1,128)S(1)}, u32[]{:S(2)}, u32[]{:S(2)}) collective-permute-start(f32[1,1328]{1,0:T(1,128)S(1)} %get-tuple-element.252), channel_id=1, source_target_pairs={{0,2},{1,3},{2,0},{3,1},{4,6},{5,7},{6,4},{7,5},{8,10},{9,11},{10,... | collective-permute-start | bytes 15944 | tf_op jit(solution)/shard_map/ppermute | solution.py:71
  423.1 22.0 %collective-permute-start.32 = (f32[1,1328]{1,0:T(1,128)S(1)}, f32[1,1328]{1,0:T(1,128)S(1)}, u32[]{:S(2)}, u32[]{:S(2)}) collective-permute-start(f32[1,1328]{1,0:T(1,128)S(1)} %get-tuple-element.253), channel_id=1, source_target_pairs={{0,1},{1,0},{2,3},{3,2},{4,5},{5,4},{6,7},{7,6},{8,9},{9,8},{10,11... | collective-permute-start | bytes 15944 | tf_op jit(solution)/shard_map/ppermute | solution.py:71
  435.4 48.5 %collective-permute-start.39 = (bf16[96,1536]{1,0:T(8,128)(2,1)}, bf16[96,1536]{1,0:T(8,128)(2,1)S(1)}, u32[]{:S(2)}, u32[]{:S(2)}) collective-permute-start(bf16[96,1536]{1,0:T(8,128)(2,1)} %bitcast.127), channel_id=1, source_target_pairs={{0,2},{1,3},{2,0},{3,1},{4,6},{5,7},{6,4},{7,5},{8,10},{9,11},{10,... | collective-permute-start | bytes 884744 | tf_op jit(solution)/shard_map/ppermute | solution.py:71
  439.8 41.6 %collective-permute-start.41 = (bf16[96,768]{1,0:T(8,128)(2,1)}, bf16[96,768]{1,0:T(8,128)(2,1)S(1)}, u32[]{:S(2)}, u32[]{:S(2)}) collective-permute-start(bf16[96,768]{1,0:T(8,128)(2,1)} %bitcast.135), channel_id=1, source_target_pairs={{0,2},{1,3},{2,0},{3,1},{4,6},{5,7},{6,4},{7,5},{8,10},{9,11},{10,... | collective-permute-start | bytes 442376 | tf_op jit(solution)/shard_map/ppermute | solution.py:71
  442.1 44.4 %collective-permute-start.38 = (bf16[96,2048]{1,0:T(8,128)(2,1)S(1)}, bf16[96,2048]{1,0:T(8,128)(2,1)S(1)}, u32[]{:S(2)}, u32[]{:S(2)}) collective-permute-start(bf16[96,2048]{1,0:T(8,128)(2,1)S(1)} %bitcast.125), channel_id=1, source_target_pairs={{0,2},{1,3},{2,0},{3,1},{4,6},{5,7},{6,4},{7,5},{8,10},{9,11},{10,... | collective-permute-start | bytes 1179656 | tf_op jit(solution)/shard_map/ppermute | solution.py:71
  444.7 34.3 %collective-permute-start.40 = (bf16[80,768]{1,0:T(8,128)(2,1)}, bf16[80,768]{1,0:T(8,128)(2,1)S(1)}, u32[]{:S(2)}, u32[]{:S(2)}) collective-permute-start(bf16[80,768]{1,0:T(8,128)(2,1)} %bitcast.89), channel_id=1, source_target_pairs={{0,2},{1,3},{2,0},{3,1},{4,6},{5,7},{6,4},{7,5},{8,10},{9,11},{10,... | collective-permute-start | bytes 368648 | tf_op jit(solution)/shard_map/ppermute | solution.py:71
  (49 other events, 299.3 us)
Sparse Core Ops, SparseCore 0:
  11.6 134.7 all-gather.1
  244.8 49.2 reduce-scatter.2
  296.8 66.9 reduce-scatter.4

commit v3 on v2

--- a/solution.py
+++ b/solution.py
@@ -1082,21 +1082,22 @@
     for_up.step([for_down.sent])
     for_attn.step([for_up.sent])
     for_skip.step([for_attn.sent])
-    for_point.step([for_skip.sent])
     input_grad, grad_gain_one, grad_bias_one = run(
         outer_back_kernel,
         1,
         [at_head, own_blocks[0], other_blocks[0], partial_one, to_head(partial_one)]
         + [gain_one, resid],
         [new((width, chan), F32), new((1, model), F32), new((1, model), F32)],
-        after=[for_point.sent] + for_up.got + for_down.got,
+        after=[for_skip.sent] + point_across + for_up.got + for_down.got,
     )
     input_grad = input_grad[None]
     for_attn.step([grad_gain_one])
     for_up.step([for_attn.sent] + for_skip.got)
     for_point.step([for_up.sent])
     for_skip.step([for_point.sent])
-    early = last = [for_skip.sent]
+    early = [for_point.sent]
+    for_point.step([for_skip.sent] + for_attn.got + for_up.got)
+    last = [for_point.sent]
     (grad_down,), (grad_up,) = for_down.finish(early), for_up.finish(early)
     (grad_skip,), (grad_point,) = for_skip.finish(last), for_point.finish(last)
     grad_out_w, *grad_qkv = for_attn.finish(early, [heads * VAL, kw, kw, heads * VAL])

time: 501 us -> 483 us (0.964)
  waiting for transfers between devices: 223 us -> 205 us
    ppermute x18, waiting for transfers between devices: 54 us -> 40.5 us  [to_bit(): return lax.ppermute(a, RW, [(i, i ^ bit) for i in range(n)])]
    unnamed x107 -> x103, local copies, waits for them, and re-layouts: 14.5 us -> 14.4 us
  transfers between devices with their start and end apart: 45 -> 45, of which waited for: 16 -> 19; matrix products, arithmetic and copies ran while one was open for 7% -> 8% of each run, Pallas kernels for 20% -> 22%
where the time goes in v3:
time: 483 us; the launch traced here: 479 us
  waiting for transfers between devices  205 us (42%)
  Pallas kernels  143 us (30%)
  starting transfers between devices  61.5 us (13%)
  local copies, waits for them, and re-layouts  24 us (5%)
  matrix products  15.5 us (3%)
  other arithmetic  14.9 us (3%)
  between operations  14.7 us (3%)
    pallas_call x27, Pallas kernels, run(): pl.pallas_call(kernel, grid=(grid,), in_specs=[spec(shape, index) for _,...  121 us
    all_gather x1, waiting for transfers between devices, shards(): big = lax.all_gather(piece, (IT, RW), axis=0, tiled=True)  83.9 us
    ppermute x11, waiting for transfers between devices, to_head(): return lax.ppermute(a, HD, [(0, 1), (1, 0)])  41.2 us
    ppermute x18, waiting for transfers between devices, to_bit(): return lax.ppermute(a, RW, [(i, i ^ bit) for i in range(n)])  40.5 us
    ppermute x18, starting transfers between devices, to_bit(): return lax.ppermute(a, RW, [(i, i ^ bit) for i in range(n)])  29.6 us
    ppermute x2, waiting for transfers between devices, from_before(): return lax.ppermute(row, RW, [(i, i + 1) for i in range(n - 1)])  24.5 us
    unnamed x103, local copies, waits for them, and re-layouts  14.4 us
    ppermute x2, starting transfers between devices, from_before(): return lax.ppermute(row, RW, [(i, i + 1) for i in range(n - 1)])  13.7 us
  transfers between devices with their start and end apart: 45, of which 19 were waited for; matrix products, arithmetic and copies ran while one was open for 8% of the time, Pallas kernels for 22%

profile of v3, /device:TPU:0, one launch (start us, length us, event | category | flops | bytes accessed | tf_op | source)
XLA Modules:
  0.0 478.6 jit_solution(2239264282295878669)
XLA Ops:
  8.5 3.0 shard_map.401
  11.6 5.1 %collective-permute-start.3 = (bf16[256,768]{1,0:T(8,128)(2,1)S(1)}, bf16[256,768]{1,0:T(8,128)(2,1)S(1)}, u32[]{:S(2)}, u32[]{:S(2)}) collective-permute-start(bf16[256,768]{1,0:T(8,128)(2,1)S(1)} %bitcast.93), channel_id=1, source_target_pairs={{0,3},{1,2},{2,1},{3,0},{4,7},{5,6},{6,5},{7,4},{8,11},{9,10},{10,... | collective-permute-start | bytes 1179656 | tf_op jit(solution)/shard_map/ppermute | solution.py:71
  19.2 3.1 collective-permute-start.7
  24.9 3.7 convolution_convert_fusion.refs_13_
  29.3 23.8 %collective-permute-done.7 = bf16[1,768]{1,0:T(2,128)(2,1)S(1)} collective-permute-done((bf16[1,768]{1,0:T(2,128)(2,1)S(1)}, bf16[1,768]{1,0:T(2,128)(2,1)S(1)}, u32[]{:S(2)}, u32[]{:S(2)}) %collective-permute-start.7) | collective-permute-done | bytes 1568 | tf_op jit(solution)/shard_map/ppermute | solution.py:830
  62.5 83.9 %all-gather.2.cloned.1.call-done.refs_0_.refs_11_.refs_12_.refs_4_.refs_9_.refs_10_.refs_2_.refs_5_.refs_7_.refs_3_ = bf16[1536,6656]{1,0:T(8,128)(2,1)} async-done(((bf16[96,6656]{1,0:T(8,128)(2,1)}), bf16[1536,6656]{1,0:T(8,128)(2,1)}) %all-gather.2.cloned.1.call-update) | async-done | bytes 20447248 | tf_op jit(solution)/shard_map/all_gather | solution.py:899
  146.4 3.3 shard_map.402
  150.7 9.8 %shard_map.403 = (bf16[256,256]{1,0:T(8,128)(2,1)}, bf16[1024,1024]{1,0:T(8,128)(2,1)}, bf16[1024,1536]{1,0:T(8,128)(2,1)}) custom-call(s32[1]{0:T(128)} %bitcast.refs_0_, bf16[256,768]{1,0:T(8,128)(2,1)} %bitcast.90, bf16[256,768]{1,0:T(8,128)(2,1)} %copy-done.30, bf16[256,768]{1,0:T(8,128)(2,1)} %copy-done.29, bf16[256,768]{1,0:T(8,128)(2,1)} %copy-done.28, ...), custom_call_target="tpu_custom_call" | custom-call | flops 1 | bytes 1 | tf_op jit(solution)/shard_map/pallas_call | solution.py:489
  160.5 9.5 %shard_map.404 = (bf16[256,768]{1,0:T(8,128)(2,1)}, bf16[4,256,1024]{2,1,0:T(8,128)(2,1)}, bf16[256,1536]{1,0:T(8,128)(2,1)}) custom-call(bf16[256,256]{1,0:T(8,128)(2,1)} %get-tuple-element.99.refs_0_.refs_8_, bf16[1024,1024]{1,0:T(8,128)(2,1)} %get-tuple-element.100.refs_1_.refs_9_, f32[128,64]{1,0:T(8,128)} %get-tuple-element.101.refs_2_.refs_10_, ...), custom_call_target="tpu_custom_call" | custom-call | flops 1 | bytes 1 | tf_op jit(solution)/shard_map/pallas_call | solution.py:489
  171.5 4.8 %shard_map.406 = (f32[528,768]{1,0:T(8,128)}, bf16[528,768]{1,0:T(8,128)(2,1)}, f32[1,768]{1,0:T(1,128)}) custom-call(s32[1]{0:T(128)} %bitcast.refs_0_, bf16[528,768]{1,0:T(8,128)(2,1)} %maximum_maximum_fusion.refs_14_.refs_1_, ...), custom_call_target="tpu_custom_call" | custom-call | flops 1 | bytes 1 | tf_op jit(solution)/shard_map/pallas_call | solution.py:489
  176.8 4.4 convolution_add_fusion.refs_11_.refs_1_
  181.2 9.4 %collective-permute-done.9.refs_4_ = bf16[256,1536]{1,0:T(8,128)(2,1)S(1)} collective-permute-done((bf16[256,1536]{1,0:T(8,128)(2,1)}, bf16[256,1536]{1,0:T(8,128)(2,1)S(1)}, u32[]{:S(2)}, u32[]{:S(2)}) %collective-permute-start.9) | collective-permute-done | bytes 786464 | tf_op jit(solution)/shard_map/ppermute | solution.py:61
  191.5 10.9 %shard_map.405 = (f32[256,1536]{1,0:T(8,128)}, bf16[256,1536]{1,0:T(8,128)(2,1)}, bf16[256,1536]{1,0:T(8,128)(2,1)}, bf16[256,1536]{1,0:T(8,128)(2,1)}, f32[256,768]{1,0:T(8,128)}, /*index=5*/bf16[256,768]{1,0:T(8,128)(2,1)}) custom-call(s32[1]{0:T(128)} %bitcast.refs_0_, bf16[256,768]{1,0:T(8,128)(2,1)} %bitcast.91, bf16[256,768]{1,0:T(8,128)(2,1)} %copy-done.6, ...), custom_call_target="tpu_custom_call" | custom-call | flops 1 | bytes 1 | tf_op jit(solution)/shard_map/pallas_call | solution.py:489
  204.0 2.0 collective-permute-done.13.refs_1_
  206.9 3.7 shard_map.407
  211.5 2.6 reduce-precision_convert_fusion.2
  217.7 10.6 %collective-permute-start.11 = (bf16[1,768]{1,0:T(2,128)(2,1)S(1)}, bf16[1,768]{1,0:T(2,128)(2,1)S(1)}, u32[]{:S(2)}, u32[]{:S(2)}) collective-permute-start(bf16[1,768]{1,0:T(2,128)(2,1)S(1)} %get-tuple-element.238), channel_id=1, source_target_pairs={{0,1},{1,2},{2,3},{4,5},{5,6},{6,7},{8,9},{9,10},{10,11},{12,13},{... | collective-permute-start | bytes 4616 | tf_op jit(solution)/shard_map/ppermute | solution.py:830
  230.9 13.7 %shard_map.409 = (bf16[256,1536]{1,0:T(8,128)(2,1)}, bf16[256,1536]{1,0:T(8,128)(2,1)}, bf16[256,1536]{1,0:T(8,128)(2,1)}, f32[1,1536]{1,0:T(1,128)}, f32[1,1536...) custom-call(s32[1]{0:T(128)} %bitcast.refs_0_, bf16[256,768]{1,0:T(8,128)(2,1)} %copy-done.15, ...), custom_call_target="tpu_custom_call" | custom-call | flops 1 | bytes 1 | tf_op jit(solution)/shard_map/pallas_call | solution.py:489
  248.8 4.1 shard_map.408
  255.0 12.5 %collective-permute-done.16.refs_2_ = bf16[256,1536]{1,0:T(8,128)(2,1)S(1)} collective-permute-done((bf16[256,1536]{1,0:T(8,128)(2,1)S(1)}, bf16[256,1536]{1,0:T(8,128)(2,1)S(1)}, u32[]{:S(2)}, u32[]{:S(2)}) %collective-permute-start.16) | collective-permute-done | bytes 786464 | tf_op jit(solution)/shard_map/ppermute | solution.py:61
  268.3 18.1 %shard_map.410 = (bf16[256,1536]{1,0:T(8,128)(2,1)}, f32[256,768]{1,0:T(8,128)}, f32[1,1536]{1,0:T(1,128)}, f32[1,1536]{1,0:T(1,128)}, bf16[256,256]{1,0:T(8,128...) custom-call(s32[1]{0:T(128)} %bitcast.refs_0_, ...), custom_call_target="tpu_custom_call" | custom-call | flops 1 | bytes 1 | tf_op jit(solution)/shard_map/pallas_call | solution.py:489
  287.1 2.3 collective-permute-start.18
  290.1 16.4 %collective-permute-done.14 = bf16[512,768]{1,0:T(8,128)(2,1)} collective-permute-done((bf16[512,768]{1,0:T(8,128)(2,1)S(1)}, bf16[512,768]{1,0:T(8,128)(2,1)}, u32[]{:S(2)}, u32[]{:S(2)}) %collective-permute-start.14) | collective-permute-done | bytes 786464 | tf_op jit(solution)/shard_map/ppermute | solution.py:61
  310.0 3.9 shard_map.411.refs_2_
  316.8 5.1 %shard_map.412.refs_3_ = bf16[384,2048]{1,0:T(8,128)(2,1)} custom-call(s32[1]{0:T(128)} %bitcast.15.spot_ref, bf16[256,1536]{1,0:T(8,128)(2,1)} %get-tuple-element.133.refs_0_, bf16[1024,1536]{1,0:T(8,128)(2,1)} %get-tuple-element.127.refs_14_.refs_1_.refs_2_, bf16[1024,1536]{1,0:T(8,128)(2,1)} %get-tuple-element.127.refs_14_.refs_1_.refs_2_, ...), custom_call_target="tpu_custom_call" | custom-call | flops 1 | bytes 1 | tf_op jit(solution)/shard_map/pallas_call | solution.py:235
  323.4 4.1 collective-permute-start.19
  327.5 2.3 shard_map.414
  329.9 2.2 collective-permute-start.26
  333.1 2.8 shard_map.413.refs_5_
  335.9 15.3 %collective-permute-done.19.refs_2_ = bf16[256,1024]{1,0:T(8,128)(2,1)S(1)} collective-permute-done((bf16[256,1024]{1,0:T(8,128)(2,1)S(1)}, bf16[256,1024]{1,0:T(8,128)(2,1)S(1)}, u32[]{:S(2)}, u32[]{:S(2)}) %collective-permute-start.19) | collective-permute-done | bytes 524320 | tf_op jit(solution)/shard_map/ppermute | solution.py:71
  352.0 4.7 shard_map.415.refs_3_
  358.1 2.4 shard_map.416
  360.6 2.9 reduce-scatter.5.cloned.1.call-done
  363.5 2.3 shard_map.417
  369.0 8.6 %collective-permute-done.25.refs_8_ = bf16[384,2048]{1,0:T(8,128)(2,1)} collective-permute-done((bf16[384,2048]{1,0:T(8,128)(2,1)}, bf16[384,2048]{1,0:T(8,128)(2,1)}, u32[]{:S(2)}, u32[]{:S(2)}) %collective-permute-start.25) | collective-permute-done | bytes 1572896 | tf_op jit(solution)/shard_map/ppermute | solution.py:57
  377.5 6.7 %shard_map.418 = (f32[192,2048]{1,0:T(8,128)}, bf16[192,2048]{1,0:T(8,128)(2,1)}) custom-call(s32[2]{0:T(128)} %pad_add_fusion.2.at_ref, bf16[256,1536]{1,0:T(8,128)(2,1)} %get-tuple-element.133.refs_0_, bf16[1024,1536]{1,0:T(8,128)(2,1)} %get-tuple-element.127.refs_14_.refs_1_.refs_2_, bf16[1024,1536]{1,0:T(8,128)(2,1)} %get-tuple-element.127.refs_14_.refs_1_.refs_2_, ...), custom_call_target="tpu_custom_call" | custom-call | flops 1 | bytes 1 | tf_op jit(solution)/shard_map/pallas_call | solution.py:293
  385.7 2.1 shard_map.419
  387.8 2.1 collective-permute-done.27.refs_8_.refs_3_
  391.0 4.1 shard_map.420
  400.4 4.6 collective-permute-done.35
  405.0 2.8 shard_map.422
  409.8 2.6 shard_map.423
  412.4 2.3 collective-permute-start.39
  419.9 3.8 shard_map.424
  423.7 13.9 %collective-permute-done.39.refs_5_.refs_1_ = bf16[96,1536]{1,0:T(8,128)(2,1)S(1)} collective-permute-done((bf16[96,1536]{1,0:T(8,128)(2,1)}, bf16[96,1536]{1,0:T(8,128)(2,1)S(1)}, u32[]{:S(2)}, u32[]{:S(2)}) %collective-permute-start.39) | collective-permute-done | bytes 294944 | tf_op jit(solution)/shard_map/ppermute | solution.py:71
  437.5 5.0 %fusion.16 = bf16[1,512,768]{2,1,0:T(8,128)(2,1)} fusion(bf16[1536,6656]{1,0:T(8,128)(2,1)} %all-gather.2.cloned.1.call-done.refs_0_.refs_11_.refs_12_.refs_4_.refs_9_.refs_10_.refs_2_.refs_5_.refs_7_.refs_3_, f32[768]{0:T(1024)S(1)} %reduce.2, pred[256,512]{1,0:T(32,128)(4,1)S(1)} %copy-done.38, pred[256,512]{1,0:T(32,128)(4,1)S(1)} %copy-done.40, ...), kind=kOutput, calls=%fused_computation.28 | convolution fusion | flops 1615200256 | bytes 4983808 | tf_op jit(solution)/shard_map/dot_general | solution.py:31
  448.5 3.1 collective-permute-done.37
  461.9 2.1 shard_map.428
  (228 shorter events, 91.4 us)
Async XLA Ops:
  7.2 139.2 %all-gather.2.cloned.1.call-start = ((), (), s32[]{:S(2)}) async-start(), calls=%async_computation.2 | async-start | bytes 21725184 | tf_op jit(solution)/shard_map/all_gather | solution.py:899
  11.5 316.0 %reduce-scatter.3.cloned.1.call-start = ((), (), s32[]{:S(2)}) async-start(), calls=%async_computation.3 | async-start | bytes 5898240 | tf_op jit(solution)/shard_map/reduce_scatter | solution.py:1022
  11.6 43.0 %collective-permute-start.3 = (bf16[256,768]{1,0:T(8,128)(2,1)S(1)}, bf16[256,768]{1,0:T(8,128)(2,1)S(1)}, u32[]{:S(2)}, u32[]{:S(2)}) collective-permute-start(bf16[256,768]{1,0:T(8,128)(2,1)S(1)} %bitcast.93), channel_id=1, source_target_pairs={{0,3},{1,2},{2,1},{3,0},{4,7},{5,6},{6,5},{7,4},{8,11},{9,10},{10,... | collective-permute-start | bytes 1179656 | tf_op jit(solution)/shard_map/ppermute | solution.py:71
  16.7 39.3 %collective-permute-start.2 = (bf16[256,768]{1,0:T(8,128)(2,1)S(1)}, bf16[256,768]{1,0:T(8,128)(2,1)S(1)}, u32[]{:S(2)}, u32[]{:S(2)}) collective-permute-start(bf16[256,768]{1,0:T(8,128)(2,1)S(1)} %bitcast.94), channel_id=1, source_target_pairs={{0,1},{1,0},{2,3},{3,2},{4,5},{5,4},{6,7},{7,6},{8,9},{9,8},{10,11... | collective-permute-start | bytes 1179656 | tf_op jit(solution)/shard_map/ppermute | solution.py:71
  16.7 42.0 %collective-permute-start.1 = (bf16[256,768]{1,0:T(8,128)(2,1)S(1)}, bf16[256,768]{1,0:T(8,128)(2,1)S(1)}, u32[]{:S(2)}, u32[]{:S(2)}) collective-permute-start(bf16[256,768]{1,0:T(8,128)(2,1)S(1)} %bitcast.95), channel_id=1, source_target_pairs={{0,2},{1,3},{2,0},{3,1},{4,6},{5,7},{6,4},{7,5},{8,10},{9,11},{10,... | collective-permute-start | bytes 1179656 | tf_op jit(solution)/shard_map/ppermute | solution.py:71
  17.3 132.4 %collective-permute-start = (bf16[256,768]{1,0:T(8,128)(2,1)S(1)}, bf16[256,768]{1,0:T(8,128)(2,1)S(1)}, u32[]{:S(2)}, u32[]{:S(2)}) collective-permute-start(bf16[256,768]{1,0:T(8,128)(2,1)S(1)} %bitcast.96), channel_id=1, source_target_pairs={{0,4},{4,0},{1,5},{5,1},{2,6},{6,2},{3,7},{7,3},{8,12},{12,8},{9,1... | collective-permute-start | bytes 1179656 | tf_op jit(solution)/shard_map/ppermute | solution.py:61
  19.2 33.8 %collective-permute-start.7 = (bf16[1,768]{1,0:T(2,128)(2,1)S(1)}, bf16[1,768]{1,0:T(2,128)(2,1)S(1)}, u32[]{:S(2)}, u32[]{:S(2)}) collective-permute-start(bf16[1,768]{1,0:T(2,128)(2,1)S(1)} %get-tuple-element.249), channel_id=1, source_target_pairs={{0,1},{1,2},{2,3},{4,5},{5,6},{6,7},{8,9},{9,10},{10,11},{12,13},{... | collective-permute-start | bytes 4616 | tf_op jit(solution)/shard_map/ppermute | solution.py:830
  29.3 120.5 %copy-start.1 = (bf16[512,768]{1,0:T(8,128)(2,1)}, bf16[512,768]{1,0:T(8,128)(2,1)S(1)}, u32[]{:S(2)}) copy-start(bf16[512,768]{1,0:T(8,128)(2,1)S(1)} %convolution_convert_fusion.2.refs_1_) | copy-start | bytes 2359300
  53.0 8.4 %collective-permute-start.8 = (bf16[1,768]{1,0:T(2,128)(2,1)S(1)}, bf16[1,768]{1,0:T(2,128)(2,1)S(1)}, u32[]{:S(2)}, u32[]{:S(2)}) collective-permute-start(bf16[1,768]{1,0:T(2,128)(2,1)S(1)} %get-tuple-element.250), channel_id=1, source_target_pairs={{1,0},{2,1},{3,2},{5,4},{6,5},{7,6},{9,8},{10,9},{11,10},{13,12},{... | collective-permute-start | bytes 4616 | tf_op jit(solution)/shard_map/ppermute | solution.py:835
  54.5 95.2 %copy-start.28 = (bf16[256,768]{1,0:T(8,128)(2,1)}, bf16[256,768]{1,0:T(8,128)(2,1)S(1)}, u32[]{:S(2)}) copy-start(bf16[256,768]{1,0:T(8,128)(2,1)S(1)} %collective-permute-done.3.refs_4_) | copy-start | bytes 1179652
  54.6 95.2 %collective-permute-start.6 = (bf16[256,768]{1,0:T(8,128)(2,1)S(1)}, bf16[256,768]{1,0:T(8,128)(2,1)S(1)}, u32[]{:S(2)}, u32[]{:S(2)}) collective-permute-start(bf16[256,768]{1,0:T(8,128)(2,1)S(1)} %collective-permute-done.3.refs_4_), channel_id=1, source_target_pairs={{0,4},{4,0},{1,5},{5,1},{2,6},{6,2},{3,7},{7,3},{8,12},{12,8},{9,1... | collective-permute-start | bytes 1179656 | tf_op jit(solution)/shard_map/ppermute | solution.py:61
  56.0 93.8 %copy-start.29 = (bf16[256,768]{1,0:T(8,128)(2,1)}, bf16[256,768]{1,0:T(8,128)(2,1)S(1)}, u32[]{:S(2)}) copy-start(bf16[256,768]{1,0:T(8,128)(2,1)S(1)} %collective-permute-done.2.refs_3_) | copy-start | bytes 1179652
  56.0 93.8 %collective-permute-start.5 = (bf16[256,768]{1,0:T(8,128)(2,1)S(1)}, bf16[256,768]{1,0:T(8,128)(2,1)}, u32[]{:S(2)}, u32[]{:S(2)}) collective-permute-start(bf16[256,768]{1,0:T(8,128)(2,1)S(1)} %collective-permute-done.2.refs_3_), channel_id=1, source_target_pairs={{0,4},{4,0},{1,5},{5,1},{2,6},{6,2},{3,7},{7,3},{8,12},{12,8},{9,1... | collective-permute-start | bytes 1179656 | tf_op jit(solution)/shard_map/ppermute | solution.py:61
  58.7 91.2 %collective-permute-start.4 = (bf16[256,768]{1,0:T(8,128)(2,1)S(1)}, bf16[256,768]{1,0:T(8,128)(2,1)}, u32[]{:S(2)}, u32[]{:S(2)}) collective-permute-start(bf16[256,768]{1,0:T(8,128)(2,1)S(1)} %collective-permute-done.1.refs_2_), channel_id=1, source_target_pairs={{0,4},{4,0},{1,5},{5,1},{2,6},{6,2},{3,7},{7,3},{8,12},{12,8},{9,1... | collective-permute-start | bytes 1179656 | tf_op jit(solution)/shard_map/ppermute | solution.py:61
  169.9 20.7 %collective-permute-start.9 = (bf16[256,1536]{1,0:T(8,128)(2,1)}, bf16[256,1536]{1,0:T(8,128)(2,1)S(1)}, u32[]{:S(2)}, u32[]{:S(2)}) collective-permute-start(bf16[256,1536]{1,0:T(8,128)(2,1)} %get-tuple-element.102.refs_3_), channel_id=1, source_target_pairs={{0,4},{4,0},{1,5},{5,1},{2,6},{6,2},{3,7},{7,3},{8,12},{12,8},{9,1... | collective-permute-start | bytes 2359304 | tf_op jit(solution)/shard_map/ppermute | solution.py:61
  176.3 29.7 %collective-permute-start.13 = (bf16[528,768]{1,0:T(8,128)(2,1)}, bf16[528,768]{1,0:T(8,128)(2,1)S(1)}, u32[]{:S(2)}, u32[]{:S(2)}) collective-permute-start(bf16[528,768]{1,0:T(8,128)(2,1)} %get-tuple-element.112), channel_id=1, source_target_pairs={{0,4},{4,0},{1,5},{5,1},{2,6},{6,2},{3,7},{7,3},{8,12},{12,8},{9,1... | collective-permute-start | bytes 2433032 | tf_op jit(solution)/shard_map/ppermute | solution.py:61
  202.4 9.1 %collective-permute-start.10 = (bf16[256,768]{1,0:T(8,128)(2,1)}, bf16[256,768]{1,0:T(8,128)(2,1)S(1)}, u32[]{:S(2)}, u32[]{:S(2)}) collective-permute-start(bf16[256,768]{1,0:T(8,128)(2,1)} %get-tuple-element.110), channel_id=1, source_target_pairs={{0,4},{4,0},{1,5},{5,1},{2,6},{6,2},{3,7},{7,3},{8,12},{12,8},{9,1... | collective-permute-start | bytes 1179656 | tf_op jit(solution)/shard_map/ppermute | solution.py:61
  214.1 16.1 %collective-permute-start.15 = (bf16[256,768]{1,0:T(8,128)(2,1)S(1)}, bf16[256,768]{1,0:T(8,128)(2,1)S(1)}, u32[]{:S(2)}, u32[]{:S(2)}) collective-permute-start(bf16[256,768]{1,0:T(8,128)(2,1)S(1)} %get-tuple-element.234.refs_1_), channel_id=1, source_target_pairs={{0,4},{4,0},{1,5},{5,1},{2,6},{6,2},{3,7},{7,3},{8,12},{12,8},{9,1... | collective-permute-start | bytes 1179656 | tf_op jit(solution)/shard_map/ppermute | solution.py:61
  216.4 11.9 %collective-permute-start.12 = (bf16[1,768]{1,0:T(2,128)(2,1)S(1)}, bf16[1,768]{1,0:T(2,128)(2,1)S(1)}, u32[]{:S(2)}, u32[]{:S(2)}) collective-permute-start(bf16[1,768]{1,0:T(2,128)(2,1)S(1)} %get-tuple-element.237), channel_id=1, source_target_pairs={{1,0},{2,1},{3,2},{5,4},{6,5},{7,6},{9,8},{10,9},{11,10},{13,12},{... | collective-permute-start | bytes 4616 | tf_op jit(solution)/shard_map/ppermute | solution.py:835
  217.7 11.9 %collective-permute-start.11 = (bf16[1,768]{1,0:T(2,128)(2,1)S(1)}, bf16[1,768]{1,0:T(2,128)(2,1)S(1)}, u32[]{:S(2)}, u32[]{:S(2)}) collective-permute-start(bf16[1,768]{1,0:T(2,128)(2,1)S(1)} %get-tuple-element.238), channel_id=1, source_target_pairs={{0,1},{1,2},{2,3},{4,5},{5,6},{6,7},{8,9},{9,10},{10,11},{12,13},{... | collective-permute-start | bytes 4616 | tf_op jit(solution)/shard_map/ppermute | solution.py:830
  244.6 118.9 %reduce-scatter.5.cloned.1.call-start = ((), (), s32[]{:S(2)}) async-start(), calls=%async_computation.4 | async-start | bytes 5898240 | tf_op jit(solution)/shard_map/reduce_scatter | solution.py:1022
  247.4 5.4 %collective-permute-start.17 = (bf16[640,768]{1,0:T(8,128)(2,1)S(1)}, bf16[640,768]{1,0:T(8,128)(2,1)S(1)}, u32[]{:S(2)}, u32[]{:S(2)}) collective-permute-start(bf16[640,768]{1,0:T(8,128)(2,1)S(1)} %reduce-precision_convert_fusion.1), channel_id=1, source_target_pairs={{0,8},{8,0},{16,24},{24,16},{1,9},{9,1},{17,25},{25,17},{2,10},{10... | collective-permute-start | bytes 2949128 | tf_op jit(solution)/shard_map/ppermute | solution.py:52
  247.7 19.8 %collective-permute-start.16 = (bf16[256,1536]{1,0:T(8,128)(2,1)S(1)}, bf16[256,1536]{1,0:T(8,128)(2,1)S(1)}, u32[]{:S(2)}, u32[]{:S(2)}) collective-permute-start(bf16[256,1536]{1,0:T(8,128)(2,1)S(1)} %copy-done.24), channel_id=1, source_target_pairs={{0,4},{4,0},{1,5},{5,1},{2,6},{6,2},{3,7},{7,3},{8,12},{12,8},{9,1... | collective-permute-start | bytes 2359304 | tf_op jit(solution)/shard_map/ppermute | solution.py:61
  286.5 29.2 %collective-permute-start.22 = (bf16[768,1280]{1,0:T(8,128)(2,1)}, bf16[768,1280]{1,0:T(8,128)(2,1)}, u32[]{:S(2)}, u32[]{:S(2)}) collective-permute-start(bf16[768,1280]{1,0:T(8,128)(2,1)} %get-tuple-element.135), channel_id=1, source_target_pairs={{0,8},{8,0},{16,24},{24,16},{1,9},{9,1},{17,25},{25,17},{2,10},{10... | collective-permute-start | bytes 5898248 | tf_op jit(solution)/shard_map/ppermute | solution.py:52
  286.5 20.1 %collective-permute-start.14 = (bf16[512,768]{1,0:T(8,128)(2,1)S(1)}, bf16[512,768]{1,0:T(8,128)(2,1)}, u32[]{:S(2)}, u32[]{:S(2)}) collective-permute-start(bf16[512,768]{1,0:T(8,128)(2,1)S(1)} %copy-done.10), channel_id=1, source_target_pairs={{0,4},{4,0},{1,5},{5,1},{2,6},{6,2},{3,7},{7,3},{8,12},{12,8},{9,1... | collective-permute-start | bytes 2359304 | tf_op jit(solution)/shard_map/ppermute | solution.py:61
  287.1 26.9 %collective-permute-start.18 = (bf16[512,1024]{1,0:T(8,128)(2,1)}, bf16[512,1024]{1,0:T(8,128)(2,1)}, u32[]{:S(2)}, u32[]{:S(2)}) collective-permute-start(bf16[512,1024]{1,0:T(8,128)(2,1)} %get-tuple-element.132), channel_id=1, source_target_pairs={{0,1},{1,0},{2,3},{3,2},{4,5},{5,4},{6,7},{7,6},{8,9},{9,8},{10,11... | collective-permute-start | bytes 3145736 | tf_op jit(solution)/shard_map/ppermute | solution.py:71
  289.3 26.3 %collective-permute-start.21 = (bf16[768,768]{1,0:T(8,128)(2,1)}, bf16[768,768]{1,0:T(8,128)(2,1)S(1)}, u32[]{:S(2)}, u32[]{:S(2)}) collective-permute-start(bf16[768,768]{1,0:T(8,128)(2,1)} %get-tuple-element.134), channel_id=1, source_target_pairs={{0,8},{8,0},{16,24},{24,16},{1,9},{9,1},{17,25},{25,17},{2,10},{10... | collective-permute-start | bytes 3538952 | tf_op jit(solution)/shard_map/ppermute | solution.py:52
  289.3 26.3 %collective-permute-start.23 = (bf16[320,768]{1,0:T(8,128)(2,1)}, bf16[320,768]{1,0:T(8,128)(2,1)S(1)}, u32[]{:S(2)}, u32[]{:S(2)}) collective-permute-start(bf16[320,768]{1,0:T(8,128)(2,1)} %get-tuple-element.240.refs_16_), channel_id=1, source_target_pairs={{0,16},{8,24},{16,0},{24,8},{1,17},{9,25},{17,1},{25,9},{2,18},{10... | collective-permute-start | bytes 1474568 | tf_op jit(solution)/shard_map/ppermute | solution.py:57
  314.0 18.1 %collective-permute-start.20 = (bf16[768,768]{1,0:T(8,128)(2,1)}, bf16[768,768]{1,0:T(8,128)(2,1)S(1)}, u32[]{:S(2)}, u32[]{:S(2)}) collective-permute-start(bf16[768,768]{1,0:T(8,128)(2,1)} %shard_map.411.refs_2_), channel_id=1, source_target_pairs={{0,8},{8,0},{16,24},{24,16},{1,9},{9,1},{17,25},{25,17},{2,10},{10... | collective-permute-start | bytes 3538952 | tf_op jit(solution)/shard_map/ppermute | solution.py:52
  321.9 55.6 %collective-permute-start.25 = (bf16[384,2048]{1,0:T(8,128)(2,1)}, bf16[384,2048]{1,0:T(8,128)(2,1)}, u32[]{:S(2)}, u32[]{:S(2)}) collective-permute-start(bf16[384,2048]{1,0:T(8,128)(2,1)} %shard_map.412.refs_3_), channel_id=1, source_target_pairs={{0,16},{8,24},{16,0},{24,8},{1,17},{9,25},{17,1},{25,9},{2,18},{10... | collective-permute-start | bytes 4718600 | tf_op jit(solution)/shard_map/ppermute | solution.py:57
  323.4 27.7 %collective-permute-start.19 = (bf16[256,1024]{1,0:T(8,128)(2,1)S(1)}, bf16[256,1024]{1,0:T(8,128)(2,1)S(1)}, u32[]{:S(2)}, u32[]{:S(2)}) collective-permute-start(bf16[256,1024]{1,0:T(8,128)(2,1)S(1)} %get-tuple-element.247), channel_id=1, source_target_pairs={{0,2},{1,3},{2,0},{3,1},{4,6},{5,7},{6,4},{7,5},{8,10},{9,11},{10,... | collective-permute-start | bytes 1572872 | tf_op jit(solution)/shard_map/ppermute | solution.py:71
  329.9 28.3 %collective-permute-start.26 = (bf16[192,1536]{1,0:T(8,128)(2,1)}, bf16[192,1536]{1,0:T(8,128)(2,1)}, u32[]{:S(2)}, u32[]{:S(2)}) collective-permute-start(bf16[192,1536]{1,0:T(8,128)(2,1)} %bitcast.117), channel_id=1, source_target_pairs={{0,1},{1,0},{2,3},{3,2},{4,5},{5,4},{6,7},{7,6},{8,9},{9,8},{10,11... | collective-permute-start | bytes 1769480 | tf_op jit(solution)/shard_map/ppermute | solution.py:71
  356.7 33.3 %collective-permute-start.24 = (bf16[256,1536]{1,0:T(8,128)(2,1)}, bf16[256,1536]{1,0:T(8,128)(2,1)}, u32[]{:S(2)}, u32[]{:S(2)}) collective-permute-start(bf16[256,1536]{1,0:T(8,128)(2,1)} %shard_map.415.refs_3_), channel_id=1, source_target_pairs={{0,4},{4,0},{1,5},{5,1},{2,6},{6,2},{3,7},{7,3},{8,12},{12,8},{9,1... | collective-permute-start | bytes 2359304 | tf_op jit(solution)/shard_map/ppermute | solution.py:61
  357.3 32.6 %collective-permute-start.27 = (bf16[384,768]{1,0:T(8,128)(2,1)S(1)}, bf16[384,768]{1,0:T(8,128)(2,1)S(1)}, u32[]{:S(2)}, u32[]{:S(2)}) collective-permute-start(bf16[384,768]{1,0:T(8,128)(2,1)S(1)} %copy-done.13), channel_id=1, source_target_pairs={{0,16},{8,24},{16,0},{24,8},{1,17},{9,25},{17,1},{25,9},{2,18},{10... | collective-permute-start | bytes 1769480 | tf_op jit(solution)/shard_map/ppermute | solution.py:57
  365.8 24.1 %collective-permute-start.28 = (bf16[192,1536]{1,0:T(8,128)(2,1)}, bf16[192,1536]{1,0:T(8,128)(2,1)S(1)}, u32[]{:S(2)}, u32[]{:S(2)}) collective-permute-start(bf16[192,1536]{1,0:T(8,128)(2,1)} %bitcast.110), channel_id=1, source_target_pairs={{0,1},{1,0},{2,3},{3,2},{4,5},{5,4},{6,7},{7,6},{8,9},{9,8},{10,11... | collective-permute-start | bytes 1769480 | tf_op jit(solution)/shard_map/ppermute | solution.py:71
  366.6 23.4 %collective-permute-start.29 = (bf16[96,1536]{1,0:T(8,128)(2,1)}, bf16[96,1536]{1,0:T(8,128)(2,1)S(1)}, u32[]{:S(2)}, u32[]{:S(2)}) collective-permute-start(bf16[96,1536]{1,0:T(8,128)(2,1)} %bitcast.126), channel_id=1, source_target_pairs={{0,2},{1,3},{2,0},{3,1},{4,6},{5,7},{6,4},{7,5},{8,10},{9,11},{10,... | collective-permute-start | bytes 884744 | tf_op jit(solution)/shard_map/ppermute | solution.py:71
  384.2 20.8 %collective-permute-start.35 = (bf16[192,2048]{1,0:T(8,128)(2,1)}, bf16[192,2048]{1,0:T(8,128)(2,1)}, u32[]{:S(2)}, u32[]{:S(2)}) collective-permute-start(bf16[192,2048]{1,0:T(8,128)(2,1)} %get-tuple-element.143.refs_3_), channel_id=1, source_target_pairs={{0,1},{1,0},{2,3},{3,2},{4,5},{5,4},{6,7},{7,6},{8,9},{9,8},{10,11... | collective-permute-start | bytes 2359304 | tf_op jit(solution)/shard_map/ppermute | solution.py:71
  398.1 1.7 collective-permute-start.30
  398.2 10.9 %collective-permute-start.36 = (bf16[160,768]{1,0:T(8,128)(2,1)S(1)}, bf16[160,768]{1,0:T(8,128)(2,1)S(1)}, u32[]{:S(2)}, u32[]{:S(2)}) collective-permute-start(bf16[160,768]{1,0:T(8,128)(2,1)S(1)} %bitcast.131), channel_id=1, source_target_pairs={{0,1},{1,0},{2,3},{3,2},{4,5},{5,4},{6,7},{7,6},{8,9},{9,8},{10,11... | collective-permute-start | bytes 737288 | tf_op jit(solution)/shard_map/ppermute | solution.py:71
  399.8 15.0 %collective-permute-start.31 = (f32[4,1328]{1,0:T(4,128)S(1)}, f32[4,1328]{1,0:T(4,128)S(1)}, u32[]{:S(2)}, u32[]{:S(2)}) collective-permute-start(f32[4,1328]{1,0:T(4,128)S(1)} %dynamic-slice_bitcast_fusion.1), channel_id=1, source_target_pairs={{0,16},{8,24},{16,0},{24,8},{1,17},{9,25},{17,1},{25,9},{2,18},{10... | collective-permute-start | bytes 63752 | tf_op jit(solution)/shard_map/ppermute | solution.py:57
  412.4 25.1 %collective-permute-start.39 = (bf16[96,1536]{1,0:T(8,128)(2,1)}, bf16[96,1536]{1,0:T(8,128)(2,1)S(1)}, u32[]{:S(2)}, u32[]{:S(2)}) collective-permute-start(bf16[96,1536]{1,0:T(8,128)(2,1)} %bitcast.122), channel_id=1, source_target_pairs={{0,2},{1,3},{2,0},{3,1},{4,6},{5,7},{6,4},{7,5},{8,10},{9,11},{10,... | collective-permute-start | bytes 884744 | tf_op jit(solution)/shard_map/ppermute | solution.py:71
  415.4 40.3 %collective-permute-start.34 = (f32[1,1328]{1,0:T(1,128)S(1)}, f32[1,1328]{1,0:T(1,128)S(1)}, u32[]{:S(2)}, u32[]{:S(2)}) collective-permute-start(f32[1,1328]{1,0:T(1,128)S(1)} %get-tuple-element.251), channel_id=1, source_target_pairs={{0,3},{1,2},{2,1},{3,0},{4,7},{5,6},{6,5},{7,4},{8,11},{9,10},{10,... | collective-permute-start | bytes 15944 | tf_op jit(solution)/shard_map/ppermute | solution.py:71
  416.8 38.9 %collective-permute-start.33 = (f32[1,1328]{1,0:T(1,128)S(1)}, f32[1,1328]{1,0:T(1,128)S(1)}, u32[]{:S(2)}, u32[]{:S(2)}) collective-permute-start(f32[1,1328]{1,0:T(1,128)S(1)} %get-tuple-element.252), channel_id=1, source_target_pairs={{0,2},{1,3},{2,0},{3,1},{4,6},{5,7},{6,4},{7,5},{8,10},{9,11},{10,... | collective-permute-start | bytes 15944 | tf_op jit(solution)/shard_map/ppermute | solution.py:71
  418.4 37.3 %collective-permute-start.32 = (f32[1,1328]{1,0:T(1,128)S(1)}, f32[1,1328]{1,0:T(1,128)S(1)}, u32[]{:S(2)}, u32[]{:S(2)}) collective-permute-start(f32[1,1328]{1,0:T(1,128)S(1)} %get-tuple-element.253), channel_id=1, source_target_pairs={{0,1},{1,0},{2,3},{3,2},{4,5},{5,4},{6,7},{7,6},{8,9},{9,8},{10,11... | collective-permute-start | bytes 15944 | tf_op jit(solution)/shard_map/ppermute | solution.py:71
  419.8 33.1 %collective-permute-start.38 = (bf16[96,2048]{1,0:T(8,128)(2,1)S(1)}, bf16[96,2048]{1,0:T(8,128)(2,1)S(1)}, u32[]{:S(2)}, u32[]{:S(2)}) collective-permute-start(bf16[96,2048]{1,0:T(8,128)(2,1)S(1)} %bitcast.121), channel_id=1, source_target_pairs={{0,2},{1,3},{2,0},{3,1},{4,6},{5,7},{6,4},{7,5},{8,10},{9,11},{10,... | collective-permute-start | bytes 1179656 | tf_op jit(solution)/shard_map/ppermute | solution.py:71
  437.5 14.0 %collective-permute-start.37 = (bf16[192,768]{1,0:T(8,128)(2,1)}, bf16[192,768]{1,0:T(8,128)(2,1)S(1)}, u32[]{:S(2)}, u32[]{:S(2)}) collective-permute-start(bf16[192,768]{1,0:T(8,128)(2,1)} %get-tuple-element.161.refs_3_.refs_2_), channel_id=1, source_target_pairs={{0,1},{1,0},{2,3},{3,2},{4,5},{5,4},{6,7},{7,6},{8,9},{9,8},{10,11... | collective-permute-start | bytes 884744 | tf_op jit(solution)/shard_map/ppermute | solution.py:71
  451.5 13.8 %collective-permute-start.40 = (bf16[80,768]{1,0:T(8,128)(2,1)S(1)}, bf16[80,768]{1,0:T(8,128)(2,1)S(1)}, u32[]{:S(2)}, u32[]{:S(2)}) collective-permute-start(bf16[80,768]{1,0:T(8,128)(2,1)S(1)} %bitcast.133), channel_id=1, source_target_pairs={{0,2},{1,3},{2,0},{3,1},{4,6},{5,7},{6,4},{7,5},{8,10},{9,11},{10,... | collective-permute-start | bytes 368648 | tf_op jit(solution)/shard_map/ppermute | solution.py:71
  459.7 9.8 %collective-permute-start.41 = (bf16[96,768]{1,0:T(8,128)(2,1)}, bf16[96,768]{1,0:T(8,128)(2,1)S(1)}, u32[]{:S(2)}, u32[]{:S(2)}) collective-permute-start(bf16[96,768]{1,0:T(8,128)(2,1)} %bitcast.101), channel_id=1, source_target_pairs={{0,2},{1,3},{2,0},{3,1},{4,6},{5,7},{6,4},{7,5},{8,10},{9,11},{10,... | collective-permute-start | bytes 442376 | tf_op jit(solution)/shard_map/ppermute | solution.py:71
  (47 other events, 353.2 us)
Sparse Core Ops, SparseCore 0:
  11.6 134.7 all-gather.1
  244.8 49.2 reduce-scatter.2
  296.8 66.6 reduce-scatter.4

commit v4 on v3

--- a/solution.py
+++ b/solution.py
@@ -1096,7 +1096,7 @@
     for_point.step([for_up.sent])
     for_skip.step([for_point.sent])
     early = [for_point.sent]
-    for_point.step([for_skip.sent] + for_attn.got + for_up.got)
+    for_point.step([for_skip.sent] + for_attn.got)
     last = [for_point.sent]
     (grad_down,), (grad_up,) = for_down.finish(early), for_up.finish(early)
     (grad_skip,), (grad_point,) = for_skip.finish(last), for_point.finish(last)

time: 483 us -> 483 us (level)
  no operation moved by 1% of the time
where the time goes in v4:
time: 483 us; the launch traced here: 479 us
  waiting for transfers between devices  205 us (42%)
  Pallas kernels  143 us (30%)
  starting transfers between devices  61.5 us (13%)
  local copies, waits for them, and re-layouts  24 us (5%)
  matrix products  15.5 us (3%)
  other arithmetic  14.9 us (3%)
  between operations  14.7 us (3%)
    pallas_call x27, Pallas kernels, run(): pl.pallas_call(kernel, grid=(grid,), in_specs=[spec(shape, index) for _,...  121 us
    all_gather x1, waiting for transfers between devices, shards(): big = lax.all_gather(piece, (IT, RW), axis=0, tiled=True)  83.9 us
    ppermute x11, waiting for transfers between devices, to_head(): return lax.ppermute(a, HD, [(0, 1), (1, 0)])  41.2 us
    ppermute x18, waiting for transfers between devices, to_bit(): return lax.ppermute(a, RW, [(i, i ^ bit) for i in range(n)])  40.5 us
    ppermute x18, starting transfers between devices, to_bit(): return lax.ppermute(a, RW, [(i, i ^ bit) for i in range(n)])  29.6 us
    ppermute x2, waiting for transfers between devices, from_before(): return lax.ppermute(row, RW, [(i, i + 1) for i in range(n - 1)])  24.5 us
    unnamed x103, local copies, waits for them, and re-layouts  14.4 us
    ppermute x2, starting transfers between devices, from_before(): return lax.ppermute(row, RW, [(i, i + 1) for i in range(n - 1)])  13.7 us
  transfers between devices with their start and end apart: 45, of which 19 were waited for; matrix products, arithmetic and copies ran while one was open for 8% of the time, Pallas kernels for 22%

profile of v4, /device:TPU:0, one launch (start us, length us, event | category | flops | bytes accessed | tf_op | source)
XLA Modules:
  0.0 478.6 jit_solution(7118125131305246973)
XLA Ops:
  8.5 3.0 shard_map.401
  11.6 5.1 %collective-permute-start.3 = (bf16[256,768]{1,0:T(8,128)(2,1)S(1)}, bf16[256,768]{1,0:T(8,128)(2,1)S(1)}, u32[]{:S(2)}, u32[]{:S(2)}) collective-permute-start(bf16[256,768]{1,0:T(8,128)(2,1)S(1)} %bitcast.93), channel_id=1, source_target_pairs={{0,3},{1,2},{2,1},{3,0},{4,7},{5,6},{6,5},{7,4},{8,11},{9,10},{10,... | collective-permute-start | bytes 1179656 | tf_op jit(solution)/shard_map/ppermute | solution.py:71
  19.2 3.1 collective-permute-start.7
  24.9 3.7 convolution_convert_fusion.refs_13_
  29.3 23.8 %collective-permute-done.7 = bf16[1,768]{1,0:T(2,128)(2,1)S(1)} collective-permute-done((bf16[1,768]{1,0:T(2,128)(2,1)S(1)}, bf16[1,768]{1,0:T(2,128)(2,1)S(1)}, u32[]{:S(2)}, u32[]{:S(2)}) %collective-permute-start.7) | collective-permute-done | bytes 1568 | tf_op jit(solution)/shard_map/ppermute | solution.py:830
  62.5 83.9 %all-gather.2.cloned.1.call-done.refs_0_.refs_11_.refs_12_.refs_4_.refs_9_.refs_10_.refs_2_.refs_5_.refs_7_.refs_3_ = bf16[1536,6656]{1,0:T(8,128)(2,1)} async-done(((bf16[96,6656]{1,0:T(8,128)(2,1)}), bf16[1536,6656]{1,0:T(8,128)(2,1)}) %all-gather.2.cloned.1.call-update) | async-done | bytes 20447248 | tf_op jit(solution)/shard_map/all_gather | solution.py:899
  146.4 3.3 shard_map.402
  150.7 9.8 %shard_map.403 = (bf16[256,256]{1,0:T(8,128)(2,1)}, bf16[1024,1024]{1,0:T(8,128)(2,1)}, bf16[1024,1536]{1,0:T(8,128)(2,1)}) custom-call(s32[1]{0:T(128)} %bitcast.refs_0_, bf16[256,768]{1,0:T(8,128)(2,1)} %bitcast.90, bf16[256,768]{1,0:T(8,128)(2,1)} %copy-done.29, bf16[256,768]{1,0:T(8,128)(2,1)} %copy-done.28, bf16[256,768]{1,0:T(8,128)(2,1)} %copy-done.27, ...), custom_call_target="tpu_custom_call" | custom-call | flops 1 | bytes 1 | tf_op jit(solution)/shard_map/pallas_call | solution.py:489
  160.5 9.5 %shard_map.404 = (bf16[256,768]{1,0:T(8,128)(2,1)}, bf16[4,256,1024]{2,1,0:T(8,128)(2,1)}, bf16[256,1536]{1,0:T(8,128)(2,1)}) custom-call(bf16[256,256]{1,0:T(8,128)(2,1)} %get-tuple-element.99.refs_0_.refs_8_, bf16[1024,1024]{1,0:T(8,128)(2,1)} %get-tuple-element.100.refs_1_.refs_9_, f32[128,64]{1,0:T(8,128)} %get-tuple-element.101.refs_2_.refs_10_, ...), custom_call_target="tpu_custom_call" | custom-call | flops 1 | bytes 1 | tf_op jit(solution)/shard_map/pallas_call | solution.py:489
  171.5 4.8 %shard_map.406 = (f32[528,768]{1,0:T(8,128)}, bf16[528,768]{1,0:T(8,128)(2,1)}, f32[1,768]{1,0:T(1,128)}) custom-call(s32[1]{0:T(128)} %bitcast.refs_0_, bf16[528,768]{1,0:T(8,128)(2,1)} %maximum_maximum_fusion.refs_14_.refs_1_, ...), custom_call_target="tpu_custom_call" | custom-call | flops 1 | bytes 1 | tf_op jit(solution)/shard_map/pallas_call | solution.py:489
  176.8 4.4 convolution_add_fusion.refs_11_.refs_1_
  181.2 9.4 %collective-permute-done.9.refs_4_ = bf16[256,1536]{1,0:T(8,128)(2,1)S(1)} collective-permute-done((bf16[256,1536]{1,0:T(8,128)(2,1)}, bf16[256,1536]{1,0:T(8,128)(2,1)S(1)}, u32[]{:S(2)}, u32[]{:S(2)}) %collective-permute-start.9) | collective-permute-done | bytes 786464 | tf_op jit(solution)/shard_map/ppermute | solution.py:61
  191.5 10.9 %shard_map.405 = (f32[256,1536]{1,0:T(8,128)}, bf16[256,1536]{1,0:T(8,128)(2,1)}, bf16[256,1536]{1,0:T(8,128)(2,1)}, bf16[256,1536]{1,0:T(8,128)(2,1)}, f32[256,768]{1,0:T(8,128)}, /*index=5*/bf16[256,768]{1,0:T(8,128)(2,1)}) custom-call(s32[1]{0:T(128)} %bitcast.refs_0_, bf16[256,768]{1,0:T(8,128)(2,1)} %bitcast.91, bf16[256,768]{1,0:T(8,128)(2,1)} %copy-done.6, ...), custom_call_target="tpu_custom_call" | custom-call | flops 1 | bytes 1 | tf_op jit(solution)/shard_map/pallas_call | solution.py:489
  204.0 2.0 collective-permute-done.13.refs_1_
  206.9 3.7 shard_map.407
  211.5 2.6 reduce-precision_convert_fusion.2
  217.7 10.6 %collective-permute-start.11 = (bf16[1,768]{1,0:T(2,128)(2,1)S(1)}, bf16[1,768]{1,0:T(2,128)(2,1)S(1)}, u32[]{:S(2)}, u32[]{:S(2)}) collective-permute-start(bf16[1,768]{1,0:T(2,128)(2,1)S(1)} %get-tuple-element.238), channel_id=1, source_target_pairs={{0,1},{1,2},{2,3},{4,5},{5,6},{6,7},{8,9},{9,10},{10,11},{12,13},{... | collective-permute-start | bytes 4616 | tf_op jit(solution)/shard_map/ppermute | solution.py:830
  230.9 13.7 %shard_map.409 = (bf16[256,1536]{1,0:T(8,128)(2,1)}, bf16[256,1536]{1,0:T(8,128)(2,1)}, bf16[256,1536]{1,0:T(8,128)(2,1)}, f32[1,1536]{1,0:T(1,128)}, f32[1,1536...) custom-call(s32[1]{0:T(128)} %bitcast.refs_0_, bf16[256,768]{1,0:T(8,128)(2,1)} %copy-done.15, ...), custom_call_target="tpu_custom_call" | custom-call | flops 1 | bytes 1 | tf_op jit(solution)/shard_map/pallas_call | solution.py:489
  248.8 4.1 shard_map.408
  255.0 12.5 %collective-permute-done.16.refs_2_ = bf16[256,1536]{1,0:T(8,128)(2,1)S(1)} collective-permute-done((bf16[256,1536]{1,0:T(8,128)(2,1)S(1)}, bf16[256,1536]{1,0:T(8,128)(2,1)S(1)}, u32[]{:S(2)}, u32[]{:S(2)}) %collective-permute-start.16) | collective-permute-done | bytes 786464 | tf_op jit(solution)/shard_map/ppermute | solution.py:61
  268.3 18.1 %shard_map.410 = (bf16[256,1536]{1,0:T(8,128)(2,1)}, f32[256,768]{1,0:T(8,128)}, f32[1,1536]{1,0:T(1,128)}, f32[1,1536]{1,0:T(1,128)}, bf16[256,256]{1,0:T(8,128...) custom-call(s32[1]{0:T(128)} %bitcast.refs_0_, ...), custom_call_target="tpu_custom_call" | custom-call | flops 1 | bytes 1 | tf_op jit(solution)/shard_map/pallas_call | solution.py:489
  287.1 2.3 collective-permute-start.18
  290.1 16.4 %collective-permute-done.14 = bf16[512,768]{1,0:T(8,128)(2,1)} collective-permute-done((bf16[512,768]{1,0:T(8,128)(2,1)S(1)}, bf16[512,768]{1,0:T(8,128)(2,1)}, u32[]{:S(2)}, u32[]{:S(2)}) %collective-permute-start.14) | collective-permute-done | bytes 786464 | tf_op jit(solution)/shard_map/ppermute | solution.py:61
  310.0 3.9 shard_map.411.refs_2_
  316.8 5.1 %shard_map.412.refs_3_ = bf16[384,2048]{1,0:T(8,128)(2,1)} custom-call(s32[1]{0:T(128)} %bitcast.15.spot_ref, bf16[256,1536]{1,0:T(8,128)(2,1)} %get-tuple-element.133.refs_0_, bf16[1024,1536]{1,0:T(8,128)(2,1)} %get-tuple-element.127.refs_14_.refs_1_.refs_2_, bf16[1024,1536]{1,0:T(8,128)(2,1)} %get-tuple-element.127.refs_14_.refs_1_.refs_2_, ...), custom_call_target="tpu_custom_call" | custom-call | flops 1 | bytes 1 | tf_op jit(solution)/shard_map/pallas_call | solution.py:235
  323.4 4.1 collective-permute-start.19
  327.5 2.3 shard_map.414
  329.9 2.2 collective-permute-start.26
  333.1 2.8 shard_map.413.refs_5_
  335.9 15.3 %collective-permute-done.19.refs_2_ = bf16[256,1024]{1,0:T(8,128)(2,1)S(1)} collective-permute-done((bf16[256,1024]{1,0:T(8,128)(2,1)S(1)}, bf16[256,1024]{1,0:T(8,128)(2,1)S(1)}, u32[]{:S(2)}, u32[]{:S(2)}) %collective-permute-start.19) | collective-permute-done | bytes 524320 | tf_op jit(solution)/shard_map/ppermute | solution.py:71
  352.0 4.7 shard_map.415.refs_3_
  358.1 2.4 shard_map.416
  360.6 2.9 reduce-scatter.5.cloned.1.call-done
  363.5 2.3 shard_map.417
  369.0 8.6 %collective-permute-done.25.refs_8_ = bf16[384,2048]{1,0:T(8,128)(2,1)} collective-permute-done((bf16[384,2048]{1,0:T(8,128)(2,1)}, bf16[384,2048]{1,0:T(8,128)(2,1)}, u32[]{:S(2)}, u32[]{:S(2)}) %collective-permute-start.25) | collective-permute-done | bytes 1572896 | tf_op jit(solution)/shard_map/ppermute | solution.py:57
  377.5 6.7 %shard_map.418 = (f32[192,2048]{1,0:T(8,128)}, bf16[192,2048]{1,0:T(8,128)(2,1)}) custom-call(s32[2]{0:T(128)} %pad_add_fusion.2.at_ref, bf16[256,1536]{1,0:T(8,128)(2,1)} %get-tuple-element.133.refs_0_, bf16[1024,1536]{1,0:T(8,128)(2,1)} %get-tuple-element.127.refs_14_.refs_1_.refs_2_, bf16[1024,1536]{1,0:T(8,128)(2,1)} %get-tuple-element.127.refs_14_.refs_1_.refs_2_, ...), custom_call_target="tpu_custom_call" | custom-call | flops 1 | bytes 1 | tf_op jit(solution)/shard_map/pallas_call | solution.py:293
  385.7 2.1 shard_map.419
  387.8 2.1 collective-permute-done.27.refs_8_.refs_3_
  391.0 4.1 shard_map.420
  400.4 4.6 collective-permute-done.35
  405.0 2.8 shard_map.422
  409.8 2.6 shard_map.423
  412.4 2.3 collective-permute-start.39
  419.9 3.8 shard_map.424
  423.7 13.9 %collective-permute-done.39.refs_1_ = bf16[96,1536]{1,0:T(8,128)(2,1)S(1)} collective-permute-done((bf16[96,1536]{1,0:T(8,128)(2,1)}, bf16[96,1536]{1,0:T(8,128)(2,1)S(1)}, u32[]{:S(2)}, u32[]{:S(2)}) %collective-permute-start.39) | collective-permute-done | bytes 294944 | tf_op jit(solution)/shard_map/ppermute | solution.py:71
  437.5 5.0 %fusion.16 = bf16[1,512,768]{2,1,0:T(8,128)(2,1)} fusion(bf16[1536,6656]{1,0:T(8,128)(2,1)} %all-gather.2.cloned.1.call-done.refs_0_.refs_11_.refs_12_.refs_4_.refs_9_.refs_10_.refs_2_.refs_5_.refs_7_.refs_3_, f32[768]{0:T(1024)S(1)} %reduce.2, pred[256,512]{1,0:T(32,128)(4,1)S(1)} %copy-done.38, pred[256,512]{1,0:T(32,128)(4,1)S(1)} %copy-done.40, ...), kind=kOutput, calls=%fused_computation.28 | convolution fusion | flops 1615200256 | bytes 4983808 | tf_op jit(solution)/shard_map/dot_general | solution.py:31
  448.5 3.1 collective-permute-done.37
  461.9 2.1 shard_map.428
  (228 shorter events, 91.4 us)
Async XLA Ops:
  7.2 139.2 %all-gather.2.cloned.1.call-start = ((), (), s32[]{:S(2)}) async-start(), calls=%async_computation.2 | async-start | bytes 21725184 | tf_op jit(solution)/shard_map/all_gather | solution.py:899
  11.5 316.0 %reduce-scatter.3.cloned.1.call-start = ((), (), s32[]{:S(2)}) async-start(), calls=%async_computation.3 | async-start | bytes 5898240 | tf_op jit(solution)/shard_map/reduce_scatter | solution.py:1022
  11.6 43.0 %collective-permute-start.3 = (bf16[256,768]{1,0:T(8,128)(2,1)S(1)}, bf16[256,768]{1,0:T(8,128)(2,1)S(1)}, u32[]{:S(2)}, u32[]{:S(2)}) collective-permute-start(bf16[256,768]{1,0:T(8,128)(2,1)S(1)} %bitcast.93), channel_id=1, source_target_pairs={{0,3},{1,2},{2,1},{3,0},{4,7},{5,6},{6,5},{7,4},{8,11},{9,10},{10,... | collective-permute-start | bytes 1179656 | tf_op jit(solution)/shard_map/ppermute | solution.py:71
  16.7 39.3 %collective-permute-start.2 = (bf16[256,768]{1,0:T(8,128)(2,1)S(1)}, bf16[256,768]{1,0:T(8,128)(2,1)S(1)}, u32[]{:S(2)}, u32[]{:S(2)}) collective-permute-start(bf16[256,768]{1,0:T(8,128)(2,1)S(1)} %bitcast.94), channel_id=1, source_target_pairs={{0,1},{1,0},{2,3},{3,2},{4,5},{5,4},{6,7},{7,6},{8,9},{9,8},{10,11... | collective-permute-start | bytes 1179656 | tf_op jit(solution)/shard_map/ppermute | solution.py:71
  16.7 42.0 %collective-permute-start.1 = (bf16[256,768]{1,0:T(8,128)(2,1)S(1)}, bf16[256,768]{1,0:T(8,128)(2,1)S(1)}, u32[]{:S(2)}, u32[]{:S(2)}) collective-permute-start(bf16[256,768]{1,0:T(8,128)(2,1)S(1)} %bitcast.95), channel_id=1, source_target_pairs={{0,2},{1,3},{2,0},{3,1},{4,6},{5,7},{6,4},{7,5},{8,10},{9,11},{10,... | collective-permute-start | bytes 1179656 | tf_op jit(solution)/shard_map/ppermute | solution.py:71
  17.3 132.4 %collective-permute-start = (bf16[256,768]{1,0:T(8,128)(2,1)S(1)}, bf16[256,768]{1,0:T(8,128)(2,1)S(1)}, u32[]{:S(2)}, u32[]{:S(2)}) collective-permute-start(bf16[256,768]{1,0:T(8,128)(2,1)S(1)} %bitcast.96), channel_id=1, source_target_pairs={{0,4},{4,0},{1,5},{5,1},{2,6},{6,2},{3,7},{7,3},{8,12},{12,8},{9,1... | collective-permute-start | bytes 1179656 | tf_op jit(solution)/shard_map/ppermute | solution.py:61
  19.2 33.8 %collective-permute-start.7 = (bf16[1,768]{1,0:T(2,128)(2,1)S(1)}, bf16[1,768]{1,0:T(2,128)(2,1)S(1)}, u32[]{:S(2)}, u32[]{:S(2)}) collective-permute-start(bf16[1,768]{1,0:T(2,128)(2,1)S(1)} %get-tuple-element.249), channel_id=1, source_target_pairs={{0,1},{1,2},{2,3},{4,5},{5,6},{6,7},{8,9},{9,10},{10,11},{12,13},{... | collective-permute-start | bytes 4616 | tf_op jit(solution)/shard_map/ppermute | solution.py:830
  29.3 120.5 %copy-start.1 = (bf16[512,768]{1,0:T(8,128)(2,1)}, bf16[512,768]{1,0:T(8,128)(2,1)S(1)}, u32[]{:S(2)}) copy-start(bf16[512,768]{1,0:T(8,128)(2,1)S(1)} %convolution_convert_fusion.2.refs_1_) | copy-start | bytes 2359300
  53.0 8.4 %collective-permute-start.8 = (bf16[1,768]{1,0:T(2,128)(2,1)S(1)}, bf16[1,768]{1,0:T(2,128)(2,1)S(1)}, u32[]{:S(2)}, u32[]{:S(2)}) collective-permute-start(bf16[1,768]{1,0:T(2,128)(2,1)S(1)} %get-tuple-element.250), channel_id=1, source_target_pairs={{1,0},{2,1},{3,2},{5,4},{6,5},{7,6},{9,8},{10,9},{11,10},{13,12},{... | collective-permute-start | bytes 4616 | tf_op jit(solution)/shard_map/ppermute | solution.py:835
  54.5 95.2 %copy-start.27 = (bf16[256,768]{1,0:T(8,128)(2,1)}, bf16[256,768]{1,0:T(8,128)(2,1)S(1)}, u32[]{:S(2)}) copy-start(bf16[256,768]{1,0:T(8,128)(2,1)S(1)} %collective-permute-done.3.refs_4_) | copy-start | bytes 1179652
  54.6 95.2 %collective-permute-start.6 = (bf16[256,768]{1,0:T(8,128)(2,1)S(1)}, bf16[256,768]{1,0:T(8,128)(2,1)S(1)}, u32[]{:S(2)}, u32[]{:S(2)}) collective-permute-start(bf16[256,768]{1,0:T(8,128)(2,1)S(1)} %collective-permute-done.3.refs_4_), channel_id=1, source_target_pairs={{0,4},{4,0},{1,5},{5,1},{2,6},{6,2},{3,7},{7,3},{8,12},{12,8},{9,1... | collective-permute-start | bytes 1179656 | tf_op jit(solution)/shard_map/ppermute | solution.py:61
  56.0 93.8 %copy-start.28 = (bf16[256,768]{1,0:T(8,128)(2,1)}, bf16[256,768]{1,0:T(8,128)(2,1)S(1)}, u32[]{:S(2)}) copy-start(bf16[256,768]{1,0:T(8,128)(2,1)S(1)} %collective-permute-done.2.refs_3_) | copy-start | bytes 1179652
  56.0 93.8 %collective-permute-start.5 = (bf16[256,768]{1,0:T(8,128)(2,1)S(1)}, bf16[256,768]{1,0:T(8,128)(2,1)}, u32[]{:S(2)}, u32[]{:S(2)}) collective-permute-start(bf16[256,768]{1,0:T(8,128)(2,1)S(1)} %collective-permute-done.2.refs_3_), channel_id=1, source_target_pairs={{0,4},{4,0},{1,5},{5,1},{2,6},{6,2},{3,7},{7,3},{8,12},{12,8},{9,1... | collective-permute-start | bytes 1179656 | tf_op jit(solution)/shard_map/ppermute | solution.py:61
  58.7 91.2 %collective-permute-start.4 = (bf16[256,768]{1,0:T(8,128)(2,1)S(1)}, bf16[256,768]{1,0:T(8,128)(2,1)}, u32[]{:S(2)}, u32[]{:S(2)}) collective-permute-start(bf16[256,768]{1,0:T(8,128)(2,1)S(1)} %collective-permute-done.1.refs_2_), channel_id=1, source_target_pairs={{0,4},{4,0},{1,5},{5,1},{2,6},{6,2},{3,7},{7,3},{8,12},{12,8},{9,1... | collective-permute-start | bytes 1179656 | tf_op jit(solution)/shard_map/ppermute | solution.py:61
  169.9 20.7 %collective-permute-start.9 = (bf16[256,1536]{1,0:T(8,128)(2,1)}, bf16[256,1536]{1,0:T(8,128)(2,1)S(1)}, u32[]{:S(2)}, u32[]{:S(2)}) collective-permute-start(bf16[256,1536]{1,0:T(8,128)(2,1)} %get-tuple-element.102.refs_3_), channel_id=1, source_target_pairs={{0,4},{4,0},{1,5},{5,1},{2,6},{6,2},{3,7},{7,3},{8,12},{12,8},{9,1... | collective-permute-start | bytes 2359304 | tf_op jit(solution)/shard_map/ppermute | solution.py:61
  176.3 29.7 %collective-permute-start.13 = (bf16[528,768]{1,0:T(8,128)(2,1)}, bf16[528,768]{1,0:T(8,128)(2,1)S(1)}, u32[]{:S(2)}, u32[]{:S(2)}) collective-permute-start(bf16[528,768]{1,0:T(8,128)(2,1)} %get-tuple-element.112), channel_id=1, source_target_pairs={{0,4},{4,0},{1,5},{5,1},{2,6},{6,2},{3,7},{7,3},{8,12},{12,8},{9,1... | collective-permute-start | bytes 2433032 | tf_op jit(solution)/shard_map/ppermute | solution.py:61
  202.4 9.1 %collective-permute-start.10 = (bf16[256,768]{1,0:T(8,128)(2,1)}, bf16[256,768]{1,0:T(8,128)(2,1)S(1)}, u32[]{:S(2)}, u32[]{:S(2)}) collective-permute-start(bf16[256,768]{1,0:T(8,128)(2,1)} %get-tuple-element.110), channel_id=1, source_target_pairs={{0,4},{4,0},{1,5},{5,1},{2,6},{6,2},{3,7},{7,3},{8,12},{12,8},{9,1... | collective-permute-start | bytes 1179656 | tf_op jit(solution)/shard_map/ppermute | solution.py:61
  214.1 16.1 %collective-permute-start.15 = (bf16[256,768]{1,0:T(8,128)(2,1)S(1)}, bf16[256,768]{1,0:T(8,128)(2,1)S(1)}, u32[]{:S(2)}, u32[]{:S(2)}) collective-permute-start(bf16[256,768]{1,0:T(8,128)(2,1)S(1)} %get-tuple-element.234.refs_1_), channel_id=1, source_target_pairs={{0,4},{4,0},{1,5},{5,1},{2,6},{6,2},{3,7},{7,3},{8,12},{12,8},{9,1... | collective-permute-start | bytes 1179656 | tf_op jit(solution)/shard_map/ppermute | solution.py:61
  216.4 11.9 %collective-permute-start.12 = (bf16[1,768]{1,0:T(2,128)(2,1)S(1)}, bf16[1,768]{1,0:T(2,128)(2,1)S(1)}, u32[]{:S(2)}, u32[]{:S(2)}) collective-permute-start(bf16[1,768]{1,0:T(2,128)(2,1)S(1)} %get-tuple-element.237), channel_id=1, source_target_pairs={{1,0},{2,1},{3,2},{5,4},{6,5},{7,6},{9,8},{10,9},{11,10},{13,12},{... | collective-permute-start | bytes 4616 | tf_op jit(solution)/shard_map/ppermute | solution.py:835
  217.7 11.9 %collective-permute-start.11 = (bf16[1,768]{1,0:T(2,128)(2,1)S(1)}, bf16[1,768]{1,0:T(2,128)(2,1)S(1)}, u32[]{:S(2)}, u32[]{:S(2)}) collective-permute-start(bf16[1,768]{1,0:T(2,128)(2,1)S(1)} %get-tuple-element.238), channel_id=1, source_target_pairs={{0,1},{1,2},{2,3},{4,5},{5,6},{6,7},{8,9},{9,10},{10,11},{12,13},{... | collective-permute-start | bytes 4616 | tf_op jit(solution)/shard_map/ppermute | solution.py:830
  244.6 118.9 %reduce-scatter.5.cloned.1.call-start = ((), (), s32[]{:S(2)}) async-start(), calls=%async_computation.4 | async-start | bytes 5898240 | tf_op jit(solution)/shard_map/reduce_scatter | solution.py:1022
  247.4 5.4 %collective-permute-start.17 = (bf16[640,768]{1,0:T(8,128)(2,1)S(1)}, bf16[640,768]{1,0:T(8,128)(2,1)S(1)}, u32[]{:S(2)}, u32[]{:S(2)}) collective-permute-start(bf16[640,768]{1,0:T(8,128)(2,1)S(1)} %reduce-precision_convert_fusion.1), channel_id=1, source_target_pairs={{0,8},{8,0},{16,24},{24,16},{1,9},{9,1},{17,25},{25,17},{2,10},{10... | collective-permute-start | bytes 2949128 | tf_op jit(solution)/shard_map/ppermute | solution.py:52
  247.7 19.8 %collective-permute-start.16 = (bf16[256,1536]{1,0:T(8,128)(2,1)S(1)}, bf16[256,1536]{1,0:T(8,128)(2,1)S(1)}, u32[]{:S(2)}, u32[]{:S(2)}) collective-permute-start(bf16[256,1536]{1,0:T(8,128)(2,1)S(1)} %copy-done.23), channel_id=1, source_target_pairs={{0,4},{4,0},{1,5},{5,1},{2,6},{6,2},{3,7},{7,3},{8,12},{12,8},{9,1... | collective-permute-start | bytes 2359304 | tf_op jit(solution)/shard_map/ppermute | solution.py:61
  286.5 29.2 %collective-permute-start.22 = (bf16[768,1280]{1,0:T(8,128)(2,1)}, bf16[768,1280]{1,0:T(8,128)(2,1)}, u32[]{:S(2)}, u32[]{:S(2)}) collective-permute-start(bf16[768,1280]{1,0:T(8,128)(2,1)} %get-tuple-element.135), channel_id=1, source_target_pairs={{0,8},{8,0},{16,24},{24,16},{1,9},{9,1},{17,25},{25,17},{2,10},{10... | collective-permute-start | bytes 5898248 | tf_op jit(solution)/shard_map/ppermute | solution.py:52
  286.5 20.1 %collective-permute-start.14 = (bf16[512,768]{1,0:T(8,128)(2,1)S(1)}, bf16[512,768]{1,0:T(8,128)(2,1)}, u32[]{:S(2)}, u32[]{:S(2)}) collective-permute-start(bf16[512,768]{1,0:T(8,128)(2,1)S(1)} %copy-done.10), channel_id=1, source_target_pairs={{0,4},{4,0},{1,5},{5,1},{2,6},{6,2},{3,7},{7,3},{8,12},{12,8},{9,1... | collective-permute-start | bytes 2359304 | tf_op jit(solution)/shard_map/ppermute | solution.py:61
  287.1 26.9 %collective-permute-start.18 = (bf16[512,1024]{1,0:T(8,128)(2,1)}, bf16[512,1024]{1,0:T(8,128)(2,1)}, u32[]{:S(2)}, u32[]{:S(2)}) collective-permute-start(bf16[512,1024]{1,0:T(8,128)(2,1)} %get-tuple-element.132), channel_id=1, source_target_pairs={{0,1},{1,0},{2,3},{3,2},{4,5},{5,4},{6,7},{7,6},{8,9},{9,8},{10,11... | collective-permute-start | bytes 3145736 | tf_op jit(solution)/shard_map/ppermute | solution.py:71
  289.3 26.3 %collective-permute-start.21 = (bf16[768,768]{1,0:T(8,128)(2,1)}, bf16[768,768]{1,0:T(8,128)(2,1)S(1)}, u32[]{:S(2)}, u32[]{:S(2)}) collective-permute-start(bf16[768,768]{1,0:T(8,128)(2,1)} %get-tuple-element.134), channel_id=1, source_target_pairs={{0,8},{8,0},{16,24},{24,16},{1,9},{9,1},{17,25},{25,17},{2,10},{10... | collective-permute-start | bytes 3538952 | tf_op jit(solution)/shard_map/ppermute | solution.py:52
  289.3 26.3 %collective-permute-start.23 = (bf16[320,768]{1,0:T(8,128)(2,1)}, bf16[320,768]{1,0:T(8,128)(2,1)S(1)}, u32[]{:S(2)}, u32[]{:S(2)}) collective-permute-start(bf16[320,768]{1,0:T(8,128)(2,1)} %get-tuple-element.240.refs_16_), channel_id=1, source_target_pairs={{0,16},{8,24},{16,0},{24,8},{1,17},{9,25},{17,1},{25,9},{2,18},{10... | collective-permute-start | bytes 1474568 | tf_op jit(solution)/shard_map/ppermute | solution.py:57
  314.0 18.1 %collective-permute-start.20 = (bf16[768,768]{1,0:T(8,128)(2,1)}, bf16[768,768]{1,0:T(8,128)(2,1)S(1)}, u32[]{:S(2)}, u32[]{:S(2)}) collective-permute-start(bf16[768,768]{1,0:T(8,128)(2,1)} %shard_map.411.refs_2_), channel_id=1, source_target_pairs={{0,8},{8,0},{16,24},{24,16},{1,9},{9,1},{17,25},{25,17},{2,10},{10... | collective-permute-start | bytes 3538952 | tf_op jit(solution)/shard_map/ppermute | solution.py:52
  321.9 55.6 %collective-permute-start.25 = (bf16[384,2048]{1,0:T(8,128)(2,1)}, bf16[384,2048]{1,0:T(8,128)(2,1)}, u32[]{:S(2)}, u32[]{:S(2)}) collective-permute-start(bf16[384,2048]{1,0:T(8,128)(2,1)} %shard_map.412.refs_3_), channel_id=1, source_target_pairs={{0,16},{8,24},{16,0},{24,8},{1,17},{9,25},{17,1},{25,9},{2,18},{10... | collective-permute-start | bytes 4718600 | tf_op jit(solution)/shard_map/ppermute | solution.py:57
  323.4 27.7 %collective-permute-start.19 = (bf16[256,1024]{1,0:T(8,128)(2,1)S(1)}, bf16[256,1024]{1,0:T(8,128)(2,1)S(1)}, u32[]{:S(2)}, u32[]{:S(2)}) collective-permute-start(bf16[256,1024]{1,0:T(8,128)(2,1)S(1)} %get-tuple-element.247), channel_id=1, source_target_pairs={{0,2},{1,3},{2,0},{3,1},{4,6},{5,7},{6,4},{7,5},{8,10},{9,11},{10,... | collective-permute-start | bytes 1572872 | tf_op jit(solution)/shard_map/ppermute | solution.py:71
  329.9 28.3 %collective-permute-start.26 = (bf16[192,1536]{1,0:T(8,128)(2,1)}, bf16[192,1536]{1,0:T(8,128)(2,1)}, u32[]{:S(2)}, u32[]{:S(2)}) collective-permute-start(bf16[192,1536]{1,0:T(8,128)(2,1)} %bitcast.117), channel_id=1, source_target_pairs={{0,1},{1,0},{2,3},{3,2},{4,5},{5,4},{6,7},{7,6},{8,9},{9,8},{10,11... | collective-permute-start | bytes 1769480 | tf_op jit(solution)/shard_map/ppermute | solution.py:71
  356.7 33.3 %collective-permute-start.24 = (bf16[256,1536]{1,0:T(8,128)(2,1)}, bf16[256,1536]{1,0:T(8,128)(2,1)}, u32[]{:S(2)}, u32[]{:S(2)}) collective-permute-start(bf16[256,1536]{1,0:T(8,128)(2,1)} %shard_map.415.refs_3_), channel_id=1, source_target_pairs={{0,4},{4,0},{1,5},{5,1},{2,6},{6,2},{3,7},{7,3},{8,12},{12,8},{9,1... | collective-permute-start | bytes 2359304 | tf_op jit(solution)/shard_map/ppermute | solution.py:61
  357.3 32.6 %collective-permute-start.27 = (bf16[384,768]{1,0:T(8,128)(2,1)S(1)}, bf16[384,768]{1,0:T(8,128)(2,1)S(1)}, u32[]{:S(2)}, u32[]{:S(2)}) collective-permute-start(bf16[384,768]{1,0:T(8,128)(2,1)S(1)} %copy-done.13), channel_id=1, source_target_pairs={{0,16},{8,24},{16,0},{24,8},{1,17},{9,25},{17,1},{25,9},{2,18},{10... | collective-permute-start | bytes 1769480 | tf_op jit(solution)/shard_map/ppermute | solution.py:57
  365.8 24.1 %collective-permute-start.28 = (bf16[192,1536]{1,0:T(8,128)(2,1)}, bf16[192,1536]{1,0:T(8,128)(2,1)S(1)}, u32[]{:S(2)}, u32[]{:S(2)}) collective-permute-start(bf16[192,1536]{1,0:T(8,128)(2,1)} %bitcast.110), channel_id=1, source_target_pairs={{0,1},{1,0},{2,3},{3,2},{4,5},{5,4},{6,7},{7,6},{8,9},{9,8},{10,11... | collective-permute-start | bytes 1769480 | tf_op jit(solution)/shard_map/ppermute | solution.py:71
  366.6 23.4 %collective-permute-start.29 = (bf16[96,1536]{1,0:T(8,128)(2,1)}, bf16[96,1536]{1,0:T(8,128)(2,1)S(1)}, u32[]{:S(2)}, u32[]{:S(2)}) collective-permute-start(bf16[96,1536]{1,0:T(8,128)(2,1)} %bitcast.127), channel_id=1, source_target_pairs={{0,2},{1,3},{2,0},{3,1},{4,6},{5,7},{6,4},{7,5},{8,10},{9,11},{10,... | collective-permute-start | bytes 884744 | tf_op jit(solution)/shard_map/ppermute | solution.py:71
  384.2 20.8 %collective-permute-start.35 = (bf16[192,2048]{1,0:T(8,128)(2,1)}, bf16[192,2048]{1,0:T(8,128)(2,1)}, u32[]{:S(2)}, u32[]{:S(2)}) collective-permute-start(bf16[192,2048]{1,0:T(8,128)(2,1)} %get-tuple-element.143.refs_3_), channel_id=1, source_target_pairs={{0,1},{1,0},{2,3},{3,2},{4,5},{5,4},{6,7},{7,6},{8,9},{9,8},{10,11... | collective-permute-start | bytes 2359304 | tf_op jit(solution)/shard_map/ppermute | solution.py:71
  398.1 1.7 collective-permute-start.30
  398.2 10.9 %collective-permute-start.36 = (bf16[160,768]{1,0:T(8,128)(2,1)S(1)}, bf16[160,768]{1,0:T(8,128)(2,1)S(1)}, u32[]{:S(2)}, u32[]{:S(2)}) collective-permute-start(bf16[160,768]{1,0:T(8,128)(2,1)S(1)} %bitcast.131), channel_id=1, source_target_pairs={{0,1},{1,0},{2,3},{3,2},{4,5},{5,4},{6,7},{7,6},{8,9},{9,8},{10,11... | collective-permute-start | bytes 737288 | tf_op jit(solution)/shard_map/ppermute | solution.py:71
  399.8 15.0 %collective-permute-start.31 = (f32[4,1328]{1,0:T(4,128)S(1)}, f32[4,1328]{1,0:T(4,128)S(1)}, u32[]{:S(2)}, u32[]{:S(2)}) collective-permute-start(f32[4,1328]{1,0:T(4,128)S(1)} %dynamic-slice_bitcast_fusion.1), channel_id=1, source_target_pairs={{0,16},{8,24},{16,0},{24,8},{1,17},{9,25},{17,1},{25,9},{2,18},{10... | collective-permute-start | bytes 63752 | tf_op jit(solution)/shard_map/ppermute | solution.py:57
  412.4 25.1 %collective-permute-start.39 = (bf16[96,1536]{1,0:T(8,128)(2,1)}, bf16[96,1536]{1,0:T(8,128)(2,1)S(1)}, u32[]{:S(2)}, u32[]{:S(2)}) collective-permute-start(bf16[96,1536]{1,0:T(8,128)(2,1)} %bitcast.122), channel_id=1, source_target_pairs={{0,2},{1,3},{2,0},{3,1},{4,6},{5,7},{6,4},{7,5},{8,10},{9,11},{10,... | collective-permute-start | bytes 884744 | tf_op jit(solution)/shard_map/ppermute | solution.py:71
  415.4 40.3 %collective-permute-start.34 = (f32[1,1328]{1,0:T(1,128)S(1)}, f32[1,1328]{1,0:T(1,128)S(1)}, u32[]{:S(2)}, u32[]{:S(2)}) collective-permute-start(f32[1,1328]{1,0:T(1,128)S(1)} %get-tuple-element.251), channel_id=1, source_target_pairs={{0,3},{1,2},{2,1},{3,0},{4,7},{5,6},{6,5},{7,4},{8,11},{9,10},{10,... | collective-permute-start | bytes 15944 | tf_op jit(solution)/shard_map/ppermute | solution.py:71
  416.8 38.9 %collective-permute-start.33 = (f32[1,1328]{1,0:T(1,128)S(1)}, f32[1,1328]{1,0:T(1,128)S(1)}, u32[]{:S(2)}, u32[]{:S(2)}) collective-permute-start(f32[1,1328]{1,0:T(1,128)S(1)} %get-tuple-element.252), channel_id=1, source_target_pairs={{0,2},{1,3},{2,0},{3,1},{4,6},{5,7},{6,4},{7,5},{8,10},{9,11},{10,... | collective-permute-start | bytes 15944 | tf_op jit(solution)/shard_map/ppermute | solution.py:71
  418.4 37.3 %collective-permute-start.32 = (f32[1,1328]{1,0:T(1,128)S(1)}, f32[1,1328]{1,0:T(1,128)S(1)}, u32[]{:S(2)}, u32[]{:S(2)}) collective-permute-start(f32[1,1328]{1,0:T(1,128)S(1)} %get-tuple-element.253), channel_id=1, source_target_pairs={{0,1},{1,0},{2,3},{3,2},{4,5},{5,4},{6,7},{7,6},{8,9},{9,8},{10,11... | collective-permute-start | bytes 15944 | tf_op jit(solution)/shard_map/ppermute | solution.py:71
  419.8 33.1 %collective-permute-start.38 = (bf16[96,2048]{1,0:T(8,128)(2,1)S(1)}, bf16[96,2048]{1,0:T(8,128)(2,1)S(1)}, u32[]{:S(2)}, u32[]{:S(2)}) collective-permute-start(bf16[96,2048]{1,0:T(8,128)(2,1)S(1)} %bitcast.121), channel_id=1, source_target_pairs={{0,2},{1,3},{2,0},{3,1},{4,6},{5,7},{6,4},{7,5},{8,10},{9,11},{10,... | collective-permute-start | bytes 1179656 | tf_op jit(solution)/shard_map/ppermute | solution.py:71
  437.5 14.0 %collective-permute-start.37 = (bf16[192,768]{1,0:T(8,128)(2,1)}, bf16[192,768]{1,0:T(8,128)(2,1)S(1)}, u32[]{:S(2)}, u32[]{:S(2)}) collective-permute-start(bf16[192,768]{1,0:T(8,128)(2,1)} %get-tuple-element.161.refs_3_.refs_2_), channel_id=1, source_target_pairs={{0,1},{1,0},{2,3},{3,2},{4,5},{5,4},{6,7},{7,6},{8,9},{9,8},{10,11... | collective-permute-start | bytes 884744 | tf_op jit(solution)/shard_map/ppermute | solution.py:71
  451.5 13.8 %collective-permute-start.40 = (bf16[80,768]{1,0:T(8,128)(2,1)S(1)}, bf16[80,768]{1,0:T(8,128)(2,1)S(1)}, u32[]{:S(2)}, u32[]{:S(2)}) collective-permute-start(bf16[80,768]{1,0:T(8,128)(2,1)S(1)} %bitcast.133), channel_id=1, source_target_pairs={{0,2},{1,3},{2,0},{3,1},{4,6},{5,7},{6,4},{7,5},{8,10},{9,11},{10,... | collective-permute-start | bytes 368648 | tf_op jit(solution)/shard_map/ppermute | solution.py:71
  459.7 9.8 %collective-permute-start.41 = (bf16[96,768]{1,0:T(8,128)(2,1)}, bf16[96,768]{1,0:T(8,128)(2,1)S(1)}, u32[]{:S(2)}, u32[]{:S(2)}) collective-permute-start(bf16[96,768]{1,0:T(8,128)(2,1)} %bitcast.101), channel_id=1, source_target_pairs={{0,2},{1,3},{2,0},{3,1},{4,6},{5,7},{6,4},{7,5},{8,10},{9,11},{10,... | collective-permute-start | bytes 442376 | tf_op jit(solution)/shard_map/ppermute | solution.py:71
  (47 other events, 353.2 us)
Sparse Core Ops, SparseCore 0:
  11.6 134.7 all-gather.1
  244.8 49.2 reduce-scatter.2
  296.8 66.6 reduce-scatter.4
